TPU v7x, 256 devices: a whole 4x4x8 slice. The times are simulated.
256 devices in a mesh: ctx: 32 (over y, z), tp: 8 (over x, core).
Axes of the slice: x: 4, y: 4, z: 8, core: 2. Of those that a mesh axis runs over, the one named last changes fastest.
Arguments:
- queries: bfloat16 [8192, 2048], P('ctx', 'tp'), may hold values from -8 to 8
- key_states: bfloat16 [8192, 512], P('ctx'), may hold values from -6 to 6
- value_states: bfloat16 [8192, 512], P('ctx'), may hold values from -6 to 6
- saved_output: bfloat16 [8192, 2048], P('ctx', 'tp'), may hold values from -6 to 6
- output_grad: bfloat16 [8192, 2048], P('ctx', 'tp'), may hold values from -6 to 6
- block_place: int32 [32, 2], replicated, may hold values from 0 to 63, as said below
- prompt_length: int32 [1], replicated, may hold values from 128 to 1023
Outputs:
- query_grad: bfloat16 [8192, 2048], P('ctx', 'tp')
- key_grad: bfloat16 [8192, 512], P('ctx')
- value_grad: bfloat16 [8192, 512], P('ctx')
Inputs may be any that keep to these rules, and one draw needn't show every extreme that they name: Each of the 2 * 32 blocks appears once; the two blocks of one device lie at mirrored places, block_place[d, 1] = 2 * 32 - 1 - block_place[d, 0], with block_place[d, 0] < 32.
All inputs are finite; a program needn't handle non-finite values.
Results may differ from a plain program's by a relative error of at most 0.012.
Values may be sent and summed in bfloat16 or wider, within the bound.
No kernel may reach another device: no remote copies, remote signals or barrier semaphores. Data moves between devices by JAX's collectives and lax.ppermute only.
A program may use at most 64 MiB of HBM per device.

v0:
```python
import jax
import jax.numpy as jnp
from jax import lax
from jax.sharding import PartitionSpec as P

DH = 128
QH = 16
KVH = 4


def positions(block_table, offset, length, block_size):
    row_ids = offset + jnp.arange(length, dtype=jnp.int32)
    block_ids = row_ids // block_size
    table_ids = jnp.arange(block_table.shape[0], dtype=jnp.int32)
    matches = block_ids[:, None] == table_ids[None, :]
    placed = jnp.sum(jnp.where(matches, block_table[None, :], 0), axis=1)
    return placed * block_size + row_ids % block_size


def tile_spans(length, block_size):
    return [(turn * block_size, block_size) for turn in range(length // block_size)]


def shards(
    queries, key_states, value_states, saved_output, output_grad, block_place, prompt_length
):
    local_rows = queries.shape[0]
    block_size = local_rows // 2
    heads_here = queries.shape[1] // DH
    tile_rows = heads_here * block_size
    group_size = QH // KVH
    tp_rank = lax.axis_index("tp")
    ctx_rank = lax.axis_index("ctx")
    ctx_count = lax.axis_size("ctx")
    kv_head = tp_rank * heads_here // group_size
    score_scale = DH ** (-0.5)
    block_table = block_place.reshape(-1)
    prompt_end = prompt_length[0]
    own_pos = positions(block_table, ctx_rank * local_rows, local_rows, block_size)
    tile_pos = jnp.broadcast_to(
        own_pos.reshape(2, 1, block_size), (2, heads_here, block_size)
    ).reshape(2, tile_rows)

    def by_half(array):
        return (
            array.reshape(2, block_size, heads_here, DH)
            .transpose(0, 2, 1, 3)
            .reshape(2, tile_rows, DH)
        )

    query_tiles = by_half(queries)
    grad_tiles = by_half(output_grad)
    delta = jnp.sum(
        grad_tiles.astype(jnp.float32) * by_half(saved_output).astype(jnp.float32), axis=2
    )

    def visible(key_pos, half_index):
        return (key_pos[None, :] <= tile_pos[half_index][:, None]) | (key_pos[None, :] < prompt_end)

    def stats_step(state_pair, piece, offset):
        length = piece.shape[0]
        key_pos = positions(block_table, offset, length, block_size)
        peaks, totals = state_pair
        new_peaks = []
        new_totals = []
        for half_index in range(2):
            tile_state = (peaks[half_index], totals[half_index])
            for first_row, span in tile_spans(length, block_size):
                visible_mask = visible(key_pos[first_row : first_row + span], half_index)
                key_block = piece[first_row : first_row + span]

                def stats_update(
                    current, visible_mask=visible_mask, key_block=key_block, half_index=half_index
                ):
                    peak, total = current
                    scores = (
                        jnp.einsum(
                            "qd,kd->qk",
                            query_tiles[half_index],
                            key_block,
                            preferred_element_type=jnp.float32,
                        )
                        * score_scale
                    )
                    scores = jnp.where(visible_mask, scores, -jnp.inf)
                    new_peak = jnp.maximum(peak, jnp.max(scores, axis=1))
                    total = total * jnp.exp(peak - new_peak) + jnp.sum(
                        jnp.exp(scores - new_peak[:, None]), axis=1
                    )
                    return (new_peak, total)

                tile_state = lax.cond(
                    jnp.any(visible_mask), stats_update, lambda current: current, tile_state
                )
            new_peaks.append(tile_state[0])
            new_totals.append(tile_state[1])
        return (jnp.stack(new_peaks), jnp.stack(new_totals))

    def grad_step(state_pair, piece, offset):
        query_acc, key_acc = state_pair
        key_piece, value_piece = piece
        length = key_piece.shape[0]
        key_pos = positions(block_table, offset, length, block_size)
        for first_row, span in tile_spans(length, block_size):
            key_block = key_piece[first_row : first_row + span]
            value_block = value_piece[first_row : first_row + span]
            rows_acc = lax.dynamic_slice_in_dim(key_acc, offset + first_row, span, 0)
            for half_index in range(2):
                visible_mask = visible(key_pos[first_row : first_row + span], half_index)

                def grad_update(
                    current,
                    visible_mask=visible_mask,
                    key_block=key_block,
                    value_block=value_block,
                    half_index=half_index,
                ):
                    query_part, rows_part = current
                    scores = (
                        jnp.einsum(
                            "qd,kd->qk",
                            query_tiles[half_index],
                            key_block,
                            preferred_element_type=jnp.float32,
                        )
                        * score_scale
                    )
                    scores = jnp.where(visible_mask, scores, -jnp.inf)
                    probs = jnp.exp(scores - log_total[half_index][:, None])
                    dprobs = jnp.einsum(
                        "qd,kd->qk",
                        grad_tiles[half_index],
                        value_block,
                        preferred_element_type=jnp.float32,
                    )
                    dscores = (probs * (dprobs - delta[half_index][:, None]) * score_scale).astype(
                        jnp.bfloat16
                    )
                    probs_low = probs.astype(jnp.bfloat16)
                    query_part = query_part + jnp.dot(
                        dscores, key_block, preferred_element_type=jnp.float32
                    )
                    key_term = jnp.einsum(
                        "qk,qd->kd",
                        dscores,
                        query_tiles[half_index],
                        preferred_element_type=jnp.float32,
                    )
                    value_term = jnp.einsum(
                        "qk,qd->kd",
                        probs_low,
                        grad_tiles[half_index],
                        preferred_element_type=jnp.float32,
                    )
                    rows_part = rows_part + jnp.concatenate([key_term, value_term], axis=1)
                    return (query_part, rows_part)

                query_half, rows_acc = lax.cond(
                    jnp.any(visible_mask),
                    grad_update,
                    lambda current: current,
                    (query_acc[half_index], rows_acc),
                )
                query_acc = query_acc.at[half_index].set(query_half)
            key_acc = lax.dynamic_update_slice_in_dim(key_acc, rows_acc, offset + first_row, 0)
        return (query_acc, key_acc)

    own_keys = lax.dynamic_slice_in_dim(key_states, kv_head * DH, DH, 1)
    own_values = lax.dynamic_slice_in_dim(value_states, kv_head * DH, DH, 1)
    stats_init = (
        jnp.full((2, tile_rows), -1e30, jnp.float32),
        jnp.zeros((2, tile_rows), jnp.float32),
    )
    grad_init = (
        jnp.zeros((2, tile_rows, DH), jnp.float32),
        jnp.zeros((ctx_count * local_rows, 2 * DH), jnp.float32),
    )
    all_keys, all_values = (
        lax.all_gather(own_keys, "ctx", axis=0, tiled=True),
        lax.all_gather(own_values, "ctx", axis=0, tiled=True),
    )
    span_rows = min(all_keys.shape[0], 8 * block_size)
    turn_count = all_keys.shape[0] // span_rows

    def stats_turn(turn_index, state_pair):
        offset = (turn_index * span_rows).astype(jnp.int32)
        return stats_step(
            state_pair, lax.dynamic_slice_in_dim(all_keys, offset, span_rows, 0), offset
        )

    peaks, totals = lax.fori_loop(0, turn_count, stats_turn, stats_init)
    log_total = peaks + jnp.log(totals)

    def grad_turn(turn_index, state_pair):
        offset = (turn_index * span_rows).astype(jnp.int32)
        piece = (
            lax.dynamic_slice_in_dim(all_keys, offset, span_rows, 0),
            lax.dynamic_slice_in_dim(all_values, offset, span_rows, 0),
        )
        return grad_step(state_pair, piece, offset)

    query_acc, key_acc = lax.fori_loop(0, turn_count, grad_turn, grad_init)
    query_grad = (
        query_acc.reshape(2, heads_here, block_size, DH)
        .transpose(0, 2, 1, 3)
        .reshape(local_rows, heads_here * DH)
        .astype(jnp.bfloat16)
    )
    summed = lax.psum_scatter(key_acc, "ctx", scatter_dimension=0, tiled=True)
    head_slots = jnp.zeros((local_rows, KVH, 2 * DH), jnp.float32)
    head_slots = lax.dynamic_update_slice_in_dim(head_slots, summed[:, None, :], kv_head, 1)
    heads_all = lax.psum(head_slots.astype(jnp.bfloat16), "tp").astype(jnp.float32)
    key_grad = heads_all[:, :, :DH].reshape(local_rows, KVH * DH).astype(jnp.bfloat16)
    value_grad = heads_all[:, :, DH:].reshape(local_rows, KVH * DH).astype(jnp.bfloat16)
    return (query_grad, key_grad, value_grad)


def solution(mesh):
    placed = (
        P("ctx", "tp"),
        P("ctx", None),
        P("ctx", None),
        P("ctx", "tp"),
        P("ctx", "tp"),
        P(),
        P(),
    )
    return jax.shard_map(
        shards,
        mesh=mesh,
        in_specs=placed,
        out_specs=(P("ctx", "tp"), P("ctx", None), P("ctx", None)),
        check_vma=False,
    )
```

profile of v0, /device:TPU:1, one launch (start us, length us, event | category | flops | bytes accessed | tf_op | source)
XLA Modules:
  0.0 974.5 jit_solution(16087911129201663085)
XLA Ops:
  14.8 74.3 %all-gather.3.cloned.1.call-done = bf16[8192,128]{1,0:T(8,128)(2,1)} async-done(((bf16[256,128]{1,0:T(8,128)(2,1)}), bf16[8192,128]{1,0:T(8,128)(2,1)}) %all-gather.3.cloned.1.call-update) | async-done | bytes 2097168 | tf_op jit(solution)/shard_map/all_gather | solution.py:179
  89.1 274.0 %while.52 = (s32[]{:T(128)}, f32[2,256]{1,0:T(2,128)S(1)}, f32[2,256]{1,0:T(2,128)S(1)}, s32[32,2]{1,0:T(8,128)}, s32[2,256]{1,0:T(2,128)S(1)}, /*index=5*/s32[]...) while((s32[]{:T(128)}, f32[2,256]{1,0:T(2,128)S(1)}, ...), condition=%wide.wide.region_83.84_spmd, body=%wide.wide.region_1.83_spmd.sunk | while | flops 138648576 | bytes 7616219 | solution.py:191
  98.1 2.2 conditional.96
  100.3 2.2 conditional.97
  102.5 2.2 conditional.98
  104.7 2.2 conditional.99
  106.9 2.2 conditional.100
  109.1 2.2 conditional.101
  111.2 2.2 conditional.102
  121.3 2.2 conditional.104
  123.5 2.2 conditional.110
  136.2 2.2 conditional.96
  138.4 2.2 conditional.98
  140.6 2.2 conditional.99
  142.8 2.2 conditional.100
  144.9 2.2 conditional.101
  147.1 2.2 conditional.102
  157.1 2.2 conditional.104
  169.8 2.2 conditional.96
  174.2 2.2 conditional.99
  176.4 2.2 conditional.100
  178.6 2.2 conditional.102
  188.6 2.2 conditional.104
  190.9 2.2 conditional.108
  203.5 2.2 conditional.96
  207.9 2.2 conditional.99
  210.1 2.2 conditional.100
  212.3 2.2 conditional.101
  214.5 2.2 conditional.102
  224.5 2.2 conditional.104
  237.2 2.2 conditional.96
  239.4 2.2 conditional.97
  241.6 2.2 conditional.98
  243.8 2.2 conditional.99
  246.0 2.2 conditional.100
  248.1 2.2 conditional.101
  250.3 2.2 conditional.102
  270.9 2.2 conditional.96
  273.1 2.2 conditional.97
  275.3 2.2 conditional.98
  277.5 2.2 conditional.99
  279.7 2.2 conditional.100
  281.9 2.2 conditional.101
  284.1 2.2 conditional.102
  304.7 2.2 conditional.96
  306.9 2.2 conditional.97
  309.1 2.2 conditional.98
  311.2 2.2 conditional.99
  313.4 2.2 conditional.100
  315.6 2.2 conditional.101
  317.8 2.2 conditional.102
  338.4 2.2 conditional.96
  340.6 2.2 conditional.97
  342.8 2.2 conditional.98
  345.0 2.2 conditional.99
  347.2 2.2 conditional.100
  349.3 2.2 conditional.101
  351.5 2.2 conditional.102
  359.5 2.2 conditional.110
  363.2 4.2 broadcast_in_dim.331
  367.4 284.7 %while.53 = (s32[]{:T(128)}, f32[2,256,128]{2,1,0:T(8,128)S(1)}, f32[8192,256]{0,1:T(8,128)}, s32[32,2]{1,0:T(8,128)}, s32[2,256]{1,0:T(2,128)S(1)}, /*index=5*/...) while((s32[]{:T(128)}, f32[2,256,128]{2,1,0:T(8,128)S(1)}, ...), condition=%wide.wide.region_135.136_spmd, body=%wide.wide.region_85.135_spmd.sunk | while | flops 678656000 | bytes 42613576 | solution.py:202
  652.2 242.1 %reduce-scatter.2.cloned.1.call-done = f32[256,256]{0,1:T(8,128)} async-done(((f32[8192,256]{0,1:T(8,128)}), f32[256,256]{0,1:T(8,128)}) %reduce-scatter.2.cloned.1.call-update) | async-done | bytes 262160 | tf_op jit(solution)/shard_map/reduce_scatter | solution.py:209
  895.6 3.4 dynamic_update_slice.83
  900.7 65.3 %all-reduce.2.cloned.1.call-done = bf16[256,4,256]{2,1,0:T(4,128)(2,1)} async-done(((bf16[256,4,256]{2,1,0:T(4,128)(2,1)}), bf16[256,4,256]{2,1,0:T(4,128)(2,1)}) %all-reduce.2.cloned.1.call-update) | async-done | bytes 524304 | tf_op jit(solution)/shard_map/psum | solution.py:212
  (1646 shorter events, 490.2 us)
Async XLA Ops:
  7.2 1.0 copy-start
  7.2 81.9 %all-gather.3.cloned.1.call-start = ((), (), s32[]{:S(2)}) async-start(), calls=%async_computation.1 | async-start | bytes 2162688 | tf_op jit(solution)/shard_map/all_gather | solution.py:179
  8.8 354.4 %all-gather.5.cloned.1.call-start = ((), (), s32[]{:S(2)}) async-start(), calls=%async_computation.2 | async-start | bytes 2162688 | tf_op jit(solution)/shard_map/all_gather | solution.py:180
  10.3 883.9 %reduce-scatter.2.cloned.1.call-start = ((), (), s32[]{:S(2)}) async-start(), calls=%async_computation.3 | async-start | bytes 8650752 | tf_op jit(solution)/shard_map/reduce_scatter | solution.py:209
  11.2 77.9 %copy-start.2 = (s32[32,2]{1,0:T(8,128)}, s32[32,2]{1,0:T(8,128)S(1)}, u32[]{:S(2)}) copy-start(s32[32,2]{1,0:T(8,128)S(1)} %copy.31) | copy-start | bytes 772
  652.1 313.8 %all-reduce.2.cloned.1.call-start = ((), (), s32[]{:S(2)}) async-start(), calls=%async_computation.4 | async-start | bytes 1048576 | tf_op jit(solution)/shard_map/psum | solution.py:212
  899.0 0.8 copy-start.1
Sparse Core Ops, SparseCore 0:
  11.2 77.8 all-gather.2
  92.2 75.4 all-gather.4
  652.3 241.9 reduce-scatter.1
  900.0 65.9 all-reduce.1
where the time goes:
time: 984 us; the launch traced here: 975 us
  waiting for transfers between devices  382 us (39%)
  local copies, waits for them, and re-layouts  191 us (19%)
  loops' own time  171 us (17%)
  other arithmetic  143 us (15%)
  matrix products  74.1 us (8%)
  between operations  13.9 us (1%)
    reduce_scatter x1, waiting for transfers between devices, shards(): summed = lax.psum_scatter(key_acc, 'ctx', scatter_dimension=0, tiled=True)  242 us
    another operation x1, loops' own time, shards(): query_acc, key_acc = lax.fori_loop(0, turn_count, grad_turn, grad_init)  83.5 us
    another operation x1, loops' own time, shards(): peaks, totals = lax.fori_loop(0, turn_count, stats_turn, stats_init)  81 us
    all_gather x1, waiting for transfers between devices, shards(): lax.all_gather(own_keys, 'ctx', axis=0, tiled=True)  74.3 us
    psum x1, waiting for transfers between devices, shards(): lax.psum(head_slots.astype(jnp.bfloat16), 'tp').astype(jnp.float32)  65.3 us
    dynamic_slice x64, local copies, waits for them, and re-layouts, grad_step(): rows_acc = lax.dynamic_slice_in_dim(key_acc, offset + first_row, span, 0)  58.5 us
    add x66, other arithmetic, stats_update(): total * jnp.exp(peak - new_peak)  45.6 us
    max x66, other arithmetic, stats_update(): new_peak = jnp.maximum(peak, jnp.max(scores, axis=1))  44.3 us
  transfers between devices with their start and end apart: 4, of which 3 were waited for; matrix products, arithmetic and copies ran while one was open for 20% of the time, Pallas kernels for 0%

commit v1 on v0

v1 whole, which is shorter than its diff:
```python
import jax
import jax.numpy as jnp
from jax import lax
from jax.experimental import pallas as pl
from jax.experimental.pallas import tpu as pltpu
from jax.sharding import Mesh, PartitionSpec as P

DH = 128
QH = 16
KVH = 4
BLOCK = 128
NY, NZ, NX, NCORE = 4, 8, 4, 2
ROWS = 2 * BLOCK
WIDE = 2 * BLOCK
SCALE = DH ** (-0.5)
EXP2_SCALE = SCALE * 1.4426950408889634
LOWEST = -1e30
VMEM_BYTES = 40 * 1024 * 1024
F32 = jnp.float32
BF16 = jnp.bfloat16


def dot_nt(left, right):
    return lax.dot_general(left, right, (((1,), (1,)), ((), ())), preferred_element_type=F32)


def dot_nn(left, right):
    return lax.dot_general(left, right, (((1,), (0,)), ((), ())), preferred_element_type=F32)


def place_of(place_ref, row, slot):
    return place_ref[row, slot]


def load_keys(core, z_rank, mine_ref, theirs_ref, targets):
    for owner in range(2):

        @pl.when(core == owner)
        def _(owner=owner):
            for j in range(NZ):
                src = lax.rem(z_rank + j, NZ)
                for which, target in targets:
                    target[owner, j] = mine_ref[src, which]
                    target[1 - owner, j] = theirs_ref[src, which]


def load_queries(piece_refs, first_col, target):
    for k, ref in enumerate(piece_refs):
        for slot in range(2):
            for head in range(2):
                target[2 * k + slot, head * BLOCK : (head + 1) * BLOCK, :] = ref[
                    slot * BLOCK : (slot + 1) * BLOCK,
                    first_col + head * DH : first_col + (head + 1) * DH,
                ]


def masked_tiles(place_ref, prompt_ref, y_rank, z_rank, low_places, key_places, tile):
    prompt_end = prompt_ref[0]

    def step(index, carry):
        k = index // NZ
        j = lax.rem(index, NZ)
        query_place = place_of(place_ref, lax.rem(y_rank + NY - k, NY) * NZ + z_rank, 0)
        key_place = place_of(place_ref, y_rank * NZ + lax.rem(z_rank + j, NZ), 0)
        ahead = (key_place > query_place) & (key_place * BLOCK < prompt_end)

        @pl.when(ahead | (index == 0))
        def _():
            tile(2 * k, 0, j, visible_tile(query_place, key_place, prompt_end))

        return carry

    lax.fori_loop(0, NY * NZ, step, 0)
    own_high = place_of(place_ref, y_rank * NZ + z_rank, 1)
    tile(1, 1, 0, visible_tile(own_high, own_high, prompt_end))


def visible_tile(query_place, key_place, prompt_end):
    key_pos = key_place * BLOCK + lax.broadcasted_iota(jnp.int32, (BLOCK, WIDE), 0)
    query_pos = query_place * BLOCK + lax.rem(
        lax.broadcasted_iota(jnp.int32, (BLOCK, WIDE), 1), BLOCK
    )
    return (key_pos <= query_pos) | (key_pos < prompt_end)


def tile_stats(scores):
    groups = scores.reshape(scores.shape[0] // 8, 8, WIDE)
    peak = jnp.max(groups, axis=0)
    total = jnp.sum(jnp.exp2(groups - peak[None]), axis=0)
    return peak, total


def merge_stats(parts):
    peak = parts[0][0]
    for other, _ in parts[1:]:
        peak = jnp.maximum(peak, other)
    total = parts[0][1] * jnp.exp2(parts[0][0] - peak)
    for other, part in parts[1:]:
        total = total + part * jnp.exp2(other - peak)
    return peak, total


def stats_kernel(
    place_ref, prompt_ref, rank_ref, qg0, qg1, qg2, qg3, saved_ref, mine_ref, theirs_ref,
    out_ref, qs, ks, peaks, totals,
):
    y_rank, z_rank, core = rank_ref[0], rank_ref[1], rank_ref[2]
    load_keys(core, z_rank, mine_ref, theirs_ref, [(0, ks)])
    load_queries((qg0, qg1, qg2, qg3), 0, qs)
    low_places = [
        place_of(place_ref, lax.rem(y_rank + NY - k, NY) * NZ + z_rank, 0) for k in range(NY)
    ]
    key_places = [
        place_of(place_ref, y_rank * NZ + lax.rem(z_rank + j, NZ), 0) for j in range(NZ)
    ]
    for k in range(NY):
        high = []
        low = []
        query_high = qs[2 * k + 1]
        for chunk in range(NZ // 2):
            keys = ks[0, 2 * chunk : 2 * chunk + 2].reshape(2 * BLOCK, DH)
            high.append(tile_stats(dot_nt(keys, query_high) * EXP2_SCALE))
        for j in range(NZ):
            if k == 0 and j == 0:
                continue
            slot = jnp.where(key_places[j] < low_places[k], 0, 1)
            peak, total = tile_stats(dot_nt(ks[slot, j], qs[2 * k + slot]) * EXP2_SCALE)
            high.append((jnp.where(slot == 1, peak, LOWEST), jnp.where(slot == 1, total, 0.0)))
            low.append((jnp.where(slot == 0, peak, LOWEST), jnp.where(slot == 0, total, 0.0)))
        for slot, parts in ((0, low), (1, high)):
            peak, total = merge_stats(parts)
            peaks[2 * k + slot] = peak
            totals[2 * k + slot] = total

    def tile(query_index, slot, j, visible):
        scores = dot_nt(ks[slot, j], qs[query_index]) * EXP2_SCALE
        peak, total = tile_stats(jnp.where(visible, scores, LOWEST))
        total = jnp.where(peak > 0.5 * LOWEST, total, 0.0)
        peak, total = merge_stats([(peaks[query_index], totals[query_index]), (peak, total)])
        peaks[query_index] = peak
        totals[query_index] = total

    masked_tiles(place_ref, prompt_ref, y_rank, z_rank, low_places, key_places, tile)

    for k in range(NY):
        for slot in range(2):
            peak = peaks[2 * k + slot]
            top = jnp.max(peak, axis=0, keepdims=True)
            total = jnp.sum(totals[2 * k + slot] * jnp.exp2(peak - top), axis=0, keepdims=True)
            row = lax.rem(y_rank + NY - k, NY) * 2 + slot
            out_ref[pl.ds(row, 1), :] = top
            out_ref[pl.ds(row + 8, 1), :] = total
    out_ref[16:24, :] = jnp.zeros((8, WIDE), F32)
    for slot in range(2):
        for head in range(2):
            rows = slice(slot * BLOCK, (slot + 1) * BLOCK)
            grad = qg0[rows, WIDE + head * DH : WIDE + (head + 1) * DH].astype(F32)
            saved = saved_ref[rows, head * DH : (head + 1) * DH].astype(F32)
            out_ref[16 + slot : 17 + slot, head * BLOCK : (head + 1) * BLOCK] = jnp.sum(
                (grad * saved).T, axis=0, keepdims=True
            )


def grad_kernel(
    place_ref, prompt_ref, rank_ref, qg0, qg1, qg2, qg3, mine_ref, theirs_ref, st0, st1, st2, st3,
    own_query, query1, query2, query3, keep_ref, send_ref,
    qs, gs, ks, vs, kt, lse, delta, lse_rows, query_acc, key_acc, value_acc,
):
    y_rank, z_rank, core = rank_ref[0], rank_ref[1], rank_ref[2]
    load_keys(core, z_rank, mine_ref, theirs_ref, [(0, ks), (1, vs)])
    load_queries((qg0, qg1, qg2, qg3), 0, qs)
    load_queries((qg0, qg1, qg2, qg3), WIDE, gs)
    for slot in range(2):
        for j in range(NZ):
            kt[slot, :, j * BLOCK : (j + 1) * BLOCK] = ks[slot, j].T
    stats = (st0, st1, st2, st3)
    top, total = merge_stats([(ref[0:8, :], ref[8:16, :]) for ref in stats])
    lse_rows[...] = top + jnp.log2(total)
    for k in range(NY):
        for slot in range(2):
            row = lax.rem(y_rank + NY - k, NY) * 2 + slot
            lse[2 * k + slot] = jnp.broadcast_to(lse_rows[pl.ds(row, 1), :], (8, WIDE))
            delta[2 * k + slot] = jnp.broadcast_to(stats[k][16 + slot : 17 + slot, :], (8, WIDE))

    def tile_grads(query_index, keys, values, visible=None):
        length = keys.shape[0]
        shape = (length // 8, 8, WIDE)
        scores = (dot_nt(keys, qs[query_index]) * EXP2_SCALE).reshape(shape)
        logits = scores - lse[query_index][None]
        if visible is not None:
            logits = jnp.where(visible.reshape(shape), logits, LOWEST)
        probs = jnp.exp2(logits)
        dprobs = dot_nt(values, gs[query_index]).reshape(shape)
        dscores = (probs * (dprobs - delta[query_index][None])).reshape(length, WIDE)
        return probs.reshape(length, WIDE).astype(BF16), dscores.astype(BF16)

    for chunk in range(NZ // 2):
        blocks = slice(2 * chunk, 2 * chunk + 2)
        columns = slice(2 * chunk * BLOCK, (2 * chunk + 2) * BLOCK)
        keys = ks[0, blocks].reshape(2 * BLOCK, DH)
        values = vs[0, blocks].reshape(2 * BLOCK, DH)
        key_sum = None
        for k in range(NY):
            probs, dscores = tile_grads(2 * k + 1, keys, values)
            value_part = dot_nn(probs, gs[2 * k + 1])
            key_part = dot_nn(dscores, qs[2 * k + 1])
            if key_sum is None:
                key_sum, value_sum = key_part, value_part
            else:
                key_sum, value_sum = key_sum + key_part, value_sum + value_part
            query_part = dot_nn(kt[0, :, columns], dscores)
            if chunk == 0:
                query_acc[2 * k + 1] = query_part
            else:
                query_acc[2 * k + 1] += query_part
        key_acc[0, blocks] = key_sum.reshape(2, BLOCK, DH)
        value_acc[0, blocks] = value_sum.reshape(2, BLOCK, DH)
    for k in range(NY):
        query_acc[2 * k] = jnp.zeros((DH, WIDE), F32)
    key_acc[1] = jnp.zeros((NZ, BLOCK, DH), F32)
    value_acc[1] = jnp.zeros((NZ, BLOCK, DH), F32)

    def add_tile(query_index, slot, j, columns, visible=None):
        probs, dscores = tile_grads(query_index, ks[slot, j], vs[slot, j], visible)
        value_acc[slot, j] += dot_nn(probs, gs[query_index])
        key_acc[slot, j] += dot_nn(dscores, qs[query_index])
        query_acc[query_index] += dot_nn(kt[slot, :, columns], dscores)

    low_places = [
        place_of(place_ref, lax.rem(y_rank + NY - k, NY) * NZ + z_rank, 0) for k in range(NY)
    ]
    key_places = [
        place_of(place_ref, y_rank * NZ + lax.rem(z_rank + j, NZ), 0) for j in range(NZ)
    ]
    for j in range(NZ):
        for k in range(NY):
            if k == 0 and j == 0:
                continue
            slot = jnp.where(key_places[j] < low_places[k], 0, 1)
            add_tile(2 * k + slot, slot, j, slice(j * BLOCK, (j + 1) * BLOCK))

    def masked_tile(query_index, slot, j, visible):
        first = j * BLOCK
        if not isinstance(first, int):
            first = pl.multiple_of(first, BLOCK)
        add_tile(query_index, slot, j, pl.ds(first, BLOCK), visible)

    masked_tiles(place_ref, prompt_ref, y_rank, z_rank, low_places, key_places, masked_tile)

    for k, out in enumerate((own_query, query1, query2, query3)):
        for slot in range(2):
            for head in range(2):
                block = query_acc[2 * k + slot, :, head * BLOCK : (head + 1) * BLOCK].T * SCALE
                out[
                    slot * BLOCK : (slot + 1) * BLOCK, head * DH : (head + 1) * DH
                ] = block.astype(out.dtype)
    for owner in range(2):

        @pl.when(core == owner)
        def _(owner=owner):
            for j in range(NZ):
                to = lax.rem(z_rank + j, NZ)
                for slot in range(2):
                    rows = slice(slot * BLOCK, (slot + 1) * BLOCK)
                    key_block = key_acc[slot, j] * SCALE
                    value_block = value_acc[slot, j]
                    kept, sent = (key_block, value_block) if owner == 0 else (value_block, key_block)
                    keep_ref[to, rows, :] = kept
                    send_ref[to, rows, :] = sent.astype(BF16)


def join_kernel(rank_ref, own_ref, p1, p2, p3, theirs_ref, key_ref, value_ref):
    x_rank, core = rank_ref[3], rank_ref[2]
    for k, ref in enumerate((own_ref, p1, p2, p3)):
        column = pl.multiple_of(lax.rem(x_rank + NX - k, NX) * DH, DH)
        for owner in range(2):

            @pl.when(core == owner)
            def _(owner=owner, ref=ref, k=k, column=column):
                outs = (key_ref, value_ref)
                outs[owner][:, pl.ds(column, DH)] = ref[...]
                outs[1 - owner][:, pl.ds(column, DH)] = theirs_ref[k]


def call(kernel, n_scalars, n_arrays, out_shape, scratch=(), flops=0):
    return pl.pallas_call(
        kernel,
        out_shape=out_shape,
        in_specs=[pl.BlockSpec(memory_space=pltpu.SMEM)] * n_scalars
        + [pl.BlockSpec(memory_space=pltpu.VMEM)] * n_arrays,
        out_specs=jax.tree.map(lambda _: pl.BlockSpec(memory_space=pltpu.VMEM), out_shape),
        scratch_shapes=list(scratch),
        compiler_params=pltpu.CompilerParams(vmem_limit_bytes=VMEM_BYTES),
        cost_estimate=pl.CostEstimate(flops=flops, bytes_accessed=4 << 20, transcendentals=0),
    )


def shifts(array, axis, size):
    return [
        lax.ppermute(array, axis, [(i, (i + k) % size) for i in range(size)])
        for k in range(1, size)
    ]


def shards(
    queries, key_states, value_states, saved_output, output_grad, block_place, prompt_length
):
    y_rank, z_rank = lax.axis_index("y"), lax.axis_index("z")
    x_rank, core = lax.axis_index("x"), lax.axis_index("core")
    ranks = jnp.stack([y_rank, z_rank, core, x_rank]).astype(jnp.int32)
    swap = [(0, 1), (1, 0)]

    with jax.named_scope("gather_queries"):
        own_qg = jnp.concatenate([queries, output_grad], axis=1)
        pieces = [own_qg] + shifts(own_qg, "y", NY)
    with jax.named_scope("gather_keys"):
        start = (core * BLOCK, x_rank * DH)
        own_kv = jnp.stack(
            [
                lax.dynamic_slice(key_states, start, (BLOCK, DH)),
                lax.dynamic_slice(value_states, start, (BLOCK, DH)),
            ]
        )
        spread = jnp.broadcast_to(own_kv[None], (NZ, 2, BLOCK, DH))
        mine = lax.all_to_all(spread, "z", 0, 0, tiled=True)
        theirs = lax.ppermute(mine, "core", swap)
    with jax.named_scope("stats"):
        stats = call(
            stats_kernel, 3, 7, jax.ShapeDtypeStruct((24, WIDE), F32),
            [
                pltpu.VMEM((8, WIDE, DH), BF16),
                pltpu.VMEM((2, NZ, BLOCK, DH), BF16),
                pltpu.VMEM((8, 8, WIDE), F32),
                pltpu.VMEM((8, 8, WIDE), F32),
            ],
            flops=600_000_000,
        )(block_place, prompt_length, ranks, *pieces, saved_output, mine, theirs)
        all_stats = [stats] + shifts(stats, "y", NY)
    with jax.named_scope("grads"):
        piece = jax.ShapeDtypeStruct((ROWS, WIDE), BF16)
        own_query, query1, query2, query3, keep, send = call(
            grad_kernel, 3, 10,
            (
                jax.ShapeDtypeStruct((ROWS, WIDE), F32), piece, piece, piece,
                jax.ShapeDtypeStruct((NZ, ROWS, DH), F32),
                jax.ShapeDtypeStruct((NZ, ROWS, DH), BF16),
            ),
            [
                pltpu.VMEM((8, WIDE, DH), BF16),
                pltpu.VMEM((8, WIDE, DH), BF16),
                pltpu.VMEM((2, NZ, BLOCK, DH), BF16),
                pltpu.VMEM((2, NZ, BLOCK, DH), BF16),
                pltpu.VMEM((2, DH, NZ * BLOCK), BF16),
                pltpu.VMEM((8, 8, WIDE), F32),
                pltpu.VMEM((8, 8, WIDE), F32),
                pltpu.VMEM((8, WIDE), F32),
                pltpu.VMEM((8, DH, WIDE), F32),
                pltpu.VMEM((2, NZ, BLOCK, DH), F32),
                pltpu.VMEM((2, NZ, BLOCK, DH), F32),
            ],
            flops=3_000_000_000,
        )(block_place, prompt_length, ranks, *pieces, mine, theirs, *all_stats)
    with jax.named_scope("query_sum"):
        back = [
            lax.ppermute(part, "y", [(i, (i - k) % NY) for i in range(NY)])
            for k, part in ((1, query1), (2, query2), (3, query3))
        ]
        query_grad = own_query
        for part in back:
            query_grad = query_grad + part.astype(F32)
        query_grad = query_grad.astype(BF16)
    with jax.named_scope("key_sum"):
        pair = (keep + lax.ppermute(send, "core", swap).astype(F32)).astype(BF16)
        terms = lax.all_to_all(pair, "z", 0, 0, tiled=True)
        own_sum = jnp.sum(terms.astype(F32), axis=0).astype(BF16)
    with jax.named_scope("heads"):
        heads = shifts(own_sum, "x", NX)
        theirs_sum = lax.ppermute(jnp.stack([own_sum, *heads]), "core", swap)
        full = jax.ShapeDtypeStruct((ROWS, KVH * DH), BF16)
        key_grad, value_grad = call(join_kernel, 1, 5, (full, full))(
            ranks, own_sum, *heads, theirs_sum
        )
    return (query_grad, key_grad, value_grad)


def solution(mesh):
    grid = Mesh(mesh.devices.reshape(NY, NZ, NX, NCORE), ("y", "z", "x", "core"))
    rows, heads = ("y", "z"), ("x", "core")
    placed = (
        P(rows, heads),
        P(rows, None),
        P(rows, None),
        P(rows, heads),
        P(rows, heads),
        P(),
        P(),
    )
    return jax.shard_map(
        shards,
        mesh=grid,
        in_specs=placed,
        out_specs=(P(rows, heads), P(rows, None), P(rows, None)),
        check_vma=False,
    )
```

time: 984 us -> 111 us (0.11)
  waiting for transfers between devices: 382 us -> 25 us
  local copies, waits for them, and re-layouts: 191 us -> 1.02 us
  loops' own time: 171 us -> 0 us
  other arithmetic: 143 us -> 1.04 us
  matrix products: 74.1 us -> 0 us
  blocking collectives: 0 us -> 45.3 us
  Pallas kernels: 0 us -> 19.2 us
  starting transfers between devices: 0.16 us -> 17.6 us
  between operations: 13.9 us -> 1.4 us
    reduce_scatter x1 -> x0, waiting for transfers between devices: 242 us -> none  [shards(): summed = lax.psum_scatter(key_acc, 'ctx', scatter_dimension=0, tiled=True)]
    another operation x258 -> x0, loops' own time: 171 us -> none  [the longest x1 83.5 us: shards(): query_acc, key_acc = lax.fori_loop(0, turn_count, grad_turn, grad_init)]
    all_gather x2 -> x0, waiting for transfers between devices: 74.3 us -> none  [the longest x1 74.3 us: shards(): lax.all_gather(own_keys, 'ctx', axis=0, tiled=True)]
    dot_general x396 -> x0, matrix products: 74.1 us -> none  [the longest x66 14.2 us: grad_update(): jnp.einsum('qk,qd->kd', probs_low, grad_tiles[half_index], preferred_elem...]
    psum x1 -> x0, waiting for transfers between devices: 65.3 us -> none  [shards(): lax.psum(head_slots.astype(jnp.bfloat16), 'tp').astype(jnp.float32)]
    dynamic_slice x66 -> x0, local copies, waits for them, and re-layouts: 60.6 us -> none  [the longest x64 58.5 us: grad_step(): rows_acc = lax.dynamic_slice_in_dim(key_acc, offset + first_row, span, 0)]
    add x150 -> x0, other arithmetic: 47.7 us -> none  [the longest x66 45.6 us: stats_update(): total * jnp.exp(peak - new_peak)]
    dynamic_update_slice x65 -> x0, local copies, waits for them, and re-layouts: 47.3 us -> none  [the longest x64 43.9 us: grad_step(): lax.dynamic_update_slice_in_dim(key_acc, rows_acc, offset + first_row, 0)]
  transfers between devices with their start and end apart: 4 -> 15, of which waited for: 3 -> 11; matrix products, arithmetic and copies ran while one was open for 20% -> 1% of each run, Pallas kernels for 0% -> 0%
where the time goes in v1:
time: 111 us
  blocking collectives  45.3 us (41%)
  waiting for transfers between devices  25 us (23%)
  Pallas kernels  19.2 us (17%)
  starting transfers between devices  17.6 us (16%)
  between operations  1.4 us (1%)
    all_to_all x1, blocking collectives, shards(): mine = lax.all_to_all(spread, 'z', 0, 0, tiled=True)  24.9 us
    all_to_all x1, blocking collectives, shards(): terms = lax.all_to_all(pair, 'z', 0, 0, tiled=True)  20.4 us
    ppermute x9, waiting for transfers between devices, shifts(): lax.ppermute(array, axis, [(i, (i + k) % size) for i in range(size)])  19.4 us
    pallas_call x1, Pallas kernels, shards(): call(grad_kernel, 3, 10, (jax.ShapeDtypeStruct((ROWS, WIDE), F32), piece,...  13.1 us
    ppermute x9, starting transfers between devices, shifts(): lax.ppermute(array, axis, [(i, (i + k) % size) for i in range(size)])  9.07 us
    pallas_call x1, Pallas kernels, shards(): call(stats_kernel, 3, 7, jax.ShapeDtypeStruct((24, WIDE), F32), [pltpu.VM...  4.63 us
    ppermute x3, waiting for transfers between devices, shards(): lax.ppermute(part, 'y', [(i, (i - k) % NY) for i in range(NY)])  4.07 us
    ppermute x1, starting transfers between devices, shards(): theirs = lax.ppermute(mine, 'core', swap)  2.46 us
  transfers between devices with their start and end apart: 15, of which 11 were waited for; matrix products, arithmetic and copies ran while one was open for 1% of the time, Pallas kernels for 0%

profile of v1, /device:TPU:1, one launch (start us, length us, event | category | flops | bytes accessed | tf_op | source)
XLA Modules:
  0.0 110.5 jit_solution(4769124046335167464)
XLA Ops:
  0.6 0.8 dynamic-slice_bitcast_fusion
  1.4 0.1 broadcast_in_dim.2
  1.5 0.0 copy-start.1
  1.5 24.9 %all_to_all.10.mine_ref = bf16[8,2,128,128]{3,2,1,0:T(8,128)(2,1)S(1)} all-to-all(bf16[8,2,128,128]{3,2,1,0:T(8,128)(2,1)S(1)} %broadcast_in_dim.2), channel_id=1, replica_groups=mesh['y'=4,'z'=8,'x'=4,'core'=2] {'z'}, dimensions={0} | all-to-all | bytes 1048576 | tf_op jit(solution)/shard_map/gather_keys/all_to_all | solution.py:325
  26.5 0.0 copy-start.2
  26.5 2.5 %collective-permute-start.3 = (bf16[8,2,128,128]{3,2,1,0:T(8,128)(2,1)S(1)}, bf16[8,2,128,128]{3,2,1,0:T(8,128)(2,1)S(1)}, u32[]{:S(2)}, u32[]{:S(2)}) collective-permute-start(bf16[8,2,128,128]{3,2,1,0:T(8,128)(2,1)S(1)} %all_to_all.10.mine_ref), channel_id=1, source_target_pairs={{0,1},{1,0},{2,3},{3,2},{4,5},{5,4},{6,7},{7,6},{8,9},{9,8},{10,11... | collective-permute-start | bytes 1572872 | tf_op jit(solution)/shard_map/gather_keys/ppermute | solution.py:326
  28.9 0.0 copy-done.1
  29.0 0.0 copy-done.2
  29.0 0.0 copy-start
  29.0 2.8 %collective-permute-start.2 = (bf16[256,512]{1,0:T(8,128)(2,1)S(1)}, bf16[256,512]{1,0:T(8,128)(2,1)S(1)}, u32[]{:S(2)}, u32[]{:S(2)}) collective-permute-start(bf16[256,512]{1,0:T(8,128)(2,1)S(1)} %constant_dynamic-update-slice_fusion.qg0), channel_id=1, source_target_pairs={{0,192},{64,0},{128,64},{192,128},{1,193},{65,1},{129,65},{193,129... | collective-permute-start | bytes 786440 | tf_op jit(solution)/shard_map/gather_queries/ppermute | solution.py:300
  31.8 0.3 collective-permute-start.1
  32.2 0.7 collective-permute-start
  32.9 0.0 copy-start.3
  33.5 0.0 copy-done.3
  33.5 0.1 copy.11.place_ref
  33.6 0.1 pad_add_fusion.rank_ref
  33.7 3.9 %collective-permute-done.2.qg3 = bf16[256,512]{1,0:T(8,128)(2,1)S(1)} collective-permute-done((bf16[256,512]{1,0:T(8,128)(2,1)S(1)}, bf16[256,512]{1,0:T(8,128)(2,1)S(1)}, u32[]{:S(2)}, u32[]{:S(2)}) %collective-permute-start.2) | collective-permute-done | bytes 262176 | tf_op jit(solution)/shard_map/gather_queries/ppermute | solution.py:300
  37.6 2.4 %collective-permute-done.1.qg2 = bf16[256,512]{1,0:T(8,128)(2,1)S(1)} collective-permute-done((bf16[256,512]{1,0:T(8,128)(2,1)S(1)}, bf16[256,512]{1,0:T(8,128)(2,1)S(1)}, u32[]{:S(2)}, u32[]{:S(2)}) %collective-permute-start.1) | collective-permute-done | bytes 262176 | tf_op jit(solution)/shard_map/gather_queries/ppermute | solution.py:300
  40.0 7.1 %collective-permute-done.qg1 = bf16[256,512]{1,0:T(8,128)(2,1)S(1)} collective-permute-done((bf16[256,512]{1,0:T(8,128)(2,1)S(1)}, bf16[256,512]{1,0:T(8,128)(2,1)S(1)}, u32[]{:S(2)}, u32[]{:S(2)}) %collective-permute-start) | collective-permute-done | bytes 262176 | tf_op jit(solution)/shard_map/gather_queries/ppermute | solution.py:300
  47.2 0.0 collective-permute-done.3.theirs_ref
  47.2 0.0 copy-done
  47.2 4.6 %stats.1.st0 = f32[24,256]{1,0:T(8,128)S(1)} custom-call(s32[32,2]{1,0:T(8,128)S(1)} %copy.11.place_ref, s32[1]{0:T(128)S(6)} %copy.13.prompt_ref, s32[4]{0:T(128)S(1)} %pad_add_fusion.rank_ref, bf16[256,512]{1,0:T(8,128)(2,1)S(1)} %constant_dynamic-update-slice_fusion.qg0, bf16[256,512]{1,0:T(8,128)(2,1)S(1)} %collective-permute-done.qg1, ...), custom_call_target="tpu_custom_call" | custom-call | flops 600000000 | bytes 4194304 | tf_op jit(solution)/shard_map/stats/pallas_call | solution.py:328
  51.8 0.1 collective-permute-start.6
  51.9 0.5 collective-permute-start.5
  52.4 1.0 collective-permute-start.4
  53.3 1.2 %collective-permute-done.6.st3 = f32[24,256]{1,0:T(8,128)S(1)} collective-permute-done((f32[24,256]{1,0:T(8,128)S(1)}, f32[24,256]{1,0:T(8,128)S(1)}, u32[]{:S(2)}, u32[]{:S(2)}) %collective-permute-start.6) | collective-permute-done | bytes 24608 | tf_op jit(solution)/shard_map/stats/ppermute | solution.py:300
  54.6 1.6 %collective-permute-done.5.st2 = f32[24,256]{1,0:T(8,128)S(1)} collective-permute-done((f32[24,256]{1,0:T(8,128)S(1)}, f32[24,256]{1,0:T(8,128)S(1)}, u32[]{:S(2)}, u32[]{:S(2)}) %collective-permute-start.5) | collective-permute-done | bytes 24608 | tf_op jit(solution)/shard_map/stats/ppermute | solution.py:300
  56.2 0.8 collective-permute-done.4.st1
  57.0 13.1 %grads.1 = (f32[256,256]{1,0:T(8,128)S(1)}, bf16[256,256]{1,0:T(8,128)(2,1)S(1)}, bf16[256,256]{1,0:T(8,128)(2,1)S(1)}, bf16[256,256]{1,0:T(8,128)(2,1)S(1)}, f3...) custom-call(s32[32,2]{1,0:T(8,128)S(1)} %copy.11.place_ref, s32[1]{0:T(128)S(6)} %copy.13.prompt_ref, ...), custom_call_target="tpu_custom_call" | custom-call | flops 3000000000 | bytes 4194304 | tf_op jit(solution)/shard_map/grads/pallas_call | solution.py:341
  70.1 2.0 %collective-permute-start.10 = (bf16[8,256,128]{2,1,0:T(8,128)(2,1)S(1)}, bf16[8,256,128]{2,1,0:T(8,128)(2,1)S(1)}, u32[]{:S(2)}, u32[]{:S(2)}) collective-permute-start(bf16[8,256,128]{2,1,0:T(8,128)(2,1)S(1)} %get-tuple-element.16), channel_id=1, source_target_pairs={{0,1},{1,0},{2,3},{3,2},{4,5},{5,4},{6,7},{7,6},{8,9},{9,8},{10,11... | collective-permute-start | bytes 1572872 | tf_op jit(solution)/shard_map/key_sum/ppermute | solution.py:373
  72.0 1.5 %collective-permute-done.10 = bf16[8,256,128]{2,1,0:T(8,128)(2,1)S(1)} collective-permute-done((bf16[8,256,128]{2,1,0:T(8,128)(2,1)S(1)}, bf16[8,256,128]{2,1,0:T(8,128)(2,1)S(1)}, u32[]{:S(2)}, u32[]{:S(2)}) %collective-permute-start.10) | collective-permute-done | bytes 524320 | tf_op jit(solution)/shard_map/key_sum/ppermute | solution.py:373
  73.6 0.1 add_convert_fusion
  73.7 20.4 %all_to_all.11 = bf16[8,256,128]{2,1,0:T(8,128)(2,1)S(1)} all-to-all(bf16[8,256,128]{2,1,0:T(8,128)(2,1)S(1)} %add_convert_fusion), channel_id=1, replica_groups=mesh['y'=4,'z'=8,'x'=4,'core'=2] {'z'}, dimensions={0} | all-to-all | bytes 1048576 | tf_op jit(solution)/shard_map/key_sum/all_to_all | solution.py:374
  94.1 0.1 reduce_sum.12.own_ref
  94.2 2.6 %collective-permute-start.13 = (bf16[256,128]{1,0:T(8,128)(2,1)S(1)}, bf16[256,128]{1,0:T(8,128)(2,1)S(1)}, u32[]{:S(2)}, u32[]{:S(2)}) collective-permute-start(bf16[256,128]{1,0:T(8,128)(2,1)S(1)} %reduce_sum.12.own_ref), channel_id=1, source_target_pairs={{0,6},{2,0},{4,2},{6,4},{1,7},{3,1},{5,3},{7,5},{8,14},{10,8},{12,... | collective-permute-start | bytes 196616 | tf_op jit(solution)/shard_map/heads/ppermute | solution.py:300
  96.7 0.5 collective-permute-start.12
  97.3 0.6 collective-permute-start.11
  97.9 1.7 %collective-permute-start.7 = (bf16[256,256]{1,0:T(8,128)(2,1)S(1)}, bf16[256,256]{1,0:T(8,128)(2,1)S(1)}, u32[]{:S(2)}, u32[]{:S(2)}) collective-permute-start(bf16[256,256]{1,0:T(8,128)(2,1)S(1)} %get-tuple-element.12), channel_id=1, source_target_pairs={{0,192},{64,0},{128,64},{192,128},{1,193},{65,1},{129,65},{193,129... | collective-permute-start | bytes 393224 | tf_op jit(solution)/shard_map/query_sum/ppermute | solution.py:365
  99.6 0.6 collective-permute-start.8
  100.2 0.0 collective-permute-done.13.p3
  100.2 0.0 collective-permute-start.9
  100.2 1.2 %collective-permute-done.12.p2 = bf16[256,128]{1,0:T(8,128)(2,1)S(1)} collective-permute-done((bf16[256,128]{1,0:T(8,128)(2,1)S(1)}, bf16[256,128]{1,0:T(8,128)(2,1)S(1)}, u32[]{:S(2)}, u32[]{:S(2)}) %collective-permute-start.12) | collective-permute-done | bytes 65568 | tf_op jit(solution)/shard_map/heads/ppermute | solution.py:300
  101.4 1.1 %collective-permute-done.11.p1 = bf16[256,128]{1,0:T(8,128)(2,1)S(1)} collective-permute-done((bf16[256,128]{1,0:T(8,128)(2,1)S(1)}, bf16[256,128]{1,0:T(8,128)(2,1)S(1)}, u32[]{:S(2)}, u32[]{:S(2)}) %collective-permute-start.11) | collective-permute-done | bytes 65568 | tf_op jit(solution)/shard_map/heads/ppermute | solution.py:300
  102.6 1.7 %collective-permute-start.14 = (bf16[4,256,128]{2,1,0:T(8,128)(2,1)S(1)}, bf16[4,256,128]{2,1,0:T(8,128)(2,1)S(1)}, u32[]{:S(2)}, u32[]{:S(2)}) collective-permute-start(bf16[4,256,128]{2,1,0:T(8,128)(2,1)S(1)} %pad_maximum_fusion), channel_id=1, source_target_pairs={{0,1},{1,0},{2,3},{3,2},{4,5},{5,4},{6,7},{7,6},{8,9},{9,8},{10,11... | collective-permute-start | bytes 786440 | tf_op jit(solution)/shard_map/heads/ppermute | solution.py:378
  104.3 0.0 collective-permute-done.7
  104.3 0.7 collective-permute-done.8
  105.0 3.3 %collective-permute-done.9 = bf16[256,256]{1,0:T(8,128)(2,1)S(1)} collective-permute-done((bf16[256,256]{1,0:T(8,128)(2,1)S(1)}, bf16[256,256]{1,0:T(8,128)(2,1)S(1)}, u32[]{:S(2)}, u32[]{:S(2)}) %collective-permute-start.9) | collective-permute-done | bytes 131104 | tf_op jit(solution)/shard_map/query_sum/ppermute | solution.py:365
  108.4 0.7 add_convert_fusion.1
  109.1 0.0 collective-permute-done.14.theirs_ref
  109.1 1.4 %heads.1 = (bf16[256,512]{1,0:T(8,128)(2,1)}, bf16[256,512]{1,0:T(8,128)(2,1)}) custom-call(s32[4]{0:T(128)S(1)} %pad_add_fusion.rank_ref, bf16[256,128]{1,0:T(8,128)(2,1)S(1)} %reduce_sum.12.own_ref, bf16[256,128]{1,0:T(8,128)(2,1)S(1)} %collective-permute-done.11.p1, bf16[256,128]{1,0:T(8,128)(2,1)S(1)} %collective-permute-done.12.p2, ...), custom_call_target="tpu_custom_call" | custom-call | bytes 4194304 | tf_op jit(solution)/shard_map/heads/pallas_call | solution.py:380
  (4 shorter events, 0.1 us)
Async XLA Ops:
  1.5 27.4 %copy-start.1 = (bf16[256,256]{1,0:T(8,128)(2,1)S(1)}, bf16[256,256]{1,0:T(8,128)(2,1)}, u32[]{:S(2)}) copy-start(bf16[256,256]{1,0:T(8,128)(2,1)} %param.7) | copy-start | bytes 393220
  26.5 2.5 %copy-start.2 = (bf16[256,256]{1,0:T(8,128)(2,1)S(1)}, bf16[256,256]{1,0:T(8,128)(2,1)}, u32[]{:S(2)}) copy-start(bf16[256,256]{1,0:T(8,128)(2,1)} %param.11) | copy-start | bytes 393220
  26.5 20.7 %collective-permute-start.3 = (bf16[8,2,128,128]{3,2,1,0:T(8,128)(2,1)S(1)}, bf16[8,2,128,128]{3,2,1,0:T(8,128)(2,1)S(1)}, u32[]{:S(2)}, u32[]{:S(2)}) collective-permute-start(bf16[8,2,128,128]{3,2,1,0:T(8,128)(2,1)S(1)} %all_to_all.10.mine_ref), channel_id=1, source_target_pairs={{0,1},{1,0},{2,3},{3,2},{4,5},{5,4},{6,7},{7,6},{8,9},{9,8},{10,11... | collective-permute-start | bytes 1572872 | tf_op jit(solution)/shard_map/gather_keys/ppermute | solution.py:326
  29.0 18.2 %copy-start = (bf16[256,256]{1,0:T(8,128)(2,1)S(1)}, bf16[256,256]{1,0:T(8,128)(2,1)}, u32[]{:S(2)}) copy-start(bf16[256,256]{1,0:T(8,128)(2,1)} %saved_ref.1) | copy-start | bytes 393220
  29.0 8.6 %collective-permute-start.2 = (bf16[256,512]{1,0:T(8,128)(2,1)S(1)}, bf16[256,512]{1,0:T(8,128)(2,1)S(1)}, u32[]{:S(2)}, u32[]{:S(2)}) collective-permute-start(bf16[256,512]{1,0:T(8,128)(2,1)S(1)} %constant_dynamic-update-slice_fusion.qg0), channel_id=1, source_target_pairs={{0,192},{64,0},{128,64},{192,128},{1,193},{65,1},{129,65},{193,129... | collective-permute-start | bytes 786440 | tf_op jit(solution)/shard_map/gather_queries/ppermute | solution.py:300
  31.8 8.2 %collective-permute-start.1 = (bf16[256,512]{1,0:T(8,128)(2,1)S(1)}, bf16[256,512]{1,0:T(8,128)(2,1)S(1)}, u32[]{:S(2)}, u32[]{:S(2)}) collective-permute-start(bf16[256,512]{1,0:T(8,128)(2,1)S(1)} %constant_dynamic-update-slice_fusion.qg0), channel_id=1, source_target_pairs={{0,128},{64,192},{128,0},{192,64},{1,129},{65,193},{129,1},{193,65... | collective-permute-start | bytes 786440 | tf_op jit(solution)/shard_map/gather_queries/ppermute | solution.py:300
  32.2 15.0 %collective-permute-start = (bf16[256,512]{1,0:T(8,128)(2,1)S(1)}, bf16[256,512]{1,0:T(8,128)(2,1)S(1)}, u32[]{:S(2)}, u32[]{:S(2)}) collective-permute-start(bf16[256,512]{1,0:T(8,128)(2,1)S(1)} %constant_dynamic-update-slice_fusion.qg0), channel_id=1, source_target_pairs={{0,64},{64,128},{128,192},{192,0},{1,65},{65,129},{129,193},{193,1... | collective-permute-start | bytes 786440 | tf_op jit(solution)/shard_map/gather_queries/ppermute | solution.py:300
  32.9 0.7 copy-start.3
  51.8 2.8 %collective-permute-start.6 = (f32[24,256]{1,0:T(8,128)S(1)}, f32[24,256]{1,0:T(8,128)S(1)}, u32[]{:S(2)}, u32[]{:S(2)}) collective-permute-start(f32[24,256]{1,0:T(8,128)S(1)} %stats.1.st0), channel_id=1, source_target_pairs={{0,192},{64,0},{128,64},{192,128},{1,193},{65,1},{129,65},{193,129... | collective-permute-start | bytes 73736 | tf_op jit(solution)/shard_map/stats/ppermute | solution.py:300
  51.9 4.3 %collective-permute-start.5 = (f32[24,256]{1,0:T(8,128)S(1)}, f32[24,256]{1,0:T(8,128)S(1)}, u32[]{:S(2)}, u32[]{:S(2)}) collective-permute-start(f32[24,256]{1,0:T(8,128)S(1)} %stats.1.st0), channel_id=1, source_target_pairs={{0,128},{64,192},{128,0},{192,64},{1,129},{65,193},{129,1},{193,65... | collective-permute-start | bytes 73736 | tf_op jit(solution)/shard_map/stats/ppermute | solution.py:300
  52.4 4.6 %collective-permute-start.4 = (f32[24,256]{1,0:T(8,128)S(1)}, f32[24,256]{1,0:T(8,128)S(1)}, u32[]{:S(2)}, u32[]{:S(2)}) collective-permute-start(f32[24,256]{1,0:T(8,128)S(1)} %stats.1.st0), channel_id=1, source_target_pairs={{0,64},{64,128},{128,192},{192,0},{1,65},{65,129},{129,193},{193,1... | collective-permute-start | bytes 73736 | tf_op jit(solution)/shard_map/stats/ppermute | solution.py:300
  70.1 3.5 %collective-permute-start.10 = (bf16[8,256,128]{2,1,0:T(8,128)(2,1)S(1)}, bf16[8,256,128]{2,1,0:T(8,128)(2,1)S(1)}, u32[]{:S(2)}, u32[]{:S(2)}) collective-permute-start(bf16[8,256,128]{2,1,0:T(8,128)(2,1)S(1)} %get-tuple-element.16), channel_id=1, source_target_pairs={{0,1},{1,0},{2,3},{3,2},{4,5},{5,4},{6,7},{7,6},{8,9},{9,8},{10,11... | collective-permute-start | bytes 1572872 | tf_op jit(solution)/shard_map/key_sum/ppermute | solution.py:373
  94.2 6.1 %collective-permute-start.13 = (bf16[256,128]{1,0:T(8,128)(2,1)S(1)}, bf16[256,128]{1,0:T(8,128)(2,1)S(1)}, u32[]{:S(2)}, u32[]{:S(2)}) collective-permute-start(bf16[256,128]{1,0:T(8,128)(2,1)S(1)} %reduce_sum.12.own_ref), channel_id=1, source_target_pairs={{0,6},{2,0},{4,2},{6,4},{1,7},{3,1},{5,3},{7,5},{8,14},{10,8},{12,... | collective-permute-start | bytes 196616 | tf_op jit(solution)/shard_map/heads/ppermute | solution.py:300
  96.7 4.7 %collective-permute-start.12 = (bf16[256,128]{1,0:T(8,128)(2,1)S(1)}, bf16[256,128]{1,0:T(8,128)(2,1)S(1)}, u32[]{:S(2)}, u32[]{:S(2)}) collective-permute-start(bf16[256,128]{1,0:T(8,128)(2,1)S(1)} %reduce_sum.12.own_ref), channel_id=1, source_target_pairs={{0,4},{2,6},{4,0},{6,2},{1,5},{3,7},{5,1},{7,3},{8,12},{10,14},{12... | collective-permute-start | bytes 196616 | tf_op jit(solution)/shard_map/heads/ppermute | solution.py:300
  97.3 5.3 %collective-permute-start.11 = (bf16[256,128]{1,0:T(8,128)(2,1)S(1)}, bf16[256,128]{1,0:T(8,128)(2,1)S(1)}, u32[]{:S(2)}, u32[]{:S(2)}) collective-permute-start(bf16[256,128]{1,0:T(8,128)(2,1)S(1)} %reduce_sum.12.own_ref), channel_id=1, source_target_pairs={{0,2},{2,4},{4,6},{6,0},{1,3},{3,5},{5,7},{7,1},{8,10},{10,12},{12... | collective-permute-start | bytes 196616 | tf_op jit(solution)/shard_map/heads/ppermute | solution.py:300
  97.9 6.4 %collective-permute-start.7 = (bf16[256,256]{1,0:T(8,128)(2,1)S(1)}, bf16[256,256]{1,0:T(8,128)(2,1)S(1)}, u32[]{:S(2)}, u32[]{:S(2)}) collective-permute-start(bf16[256,256]{1,0:T(8,128)(2,1)S(1)} %get-tuple-element.12), channel_id=1, source_target_pairs={{0,192},{64,0},{128,64},{192,128},{1,193},{65,1},{129,65},{193,129... | collective-permute-start | bytes 393224 | tf_op jit(solution)/shard_map/query_sum/ppermute | solution.py:365
  99.6 5.4 %collective-permute-start.8 = (bf16[256,256]{1,0:T(8,128)(2,1)S(1)}, bf16[256,256]{1,0:T(8,128)(2,1)S(1)}, u32[]{:S(2)}, u32[]{:S(2)}) collective-permute-start(bf16[256,256]{1,0:T(8,128)(2,1)S(1)} %get-tuple-element.13), channel_id=1, source_target_pairs={{0,128},{64,192},{128,0},{192,64},{1,129},{65,193},{129,1},{193,65... | collective-permute-start | bytes 393224 | tf_op jit(solution)/shard_map/query_sum/ppermute | solution.py:365
  100.2 8.1 %collective-permute-start.9 = (bf16[256,256]{1,0:T(8,128)(2,1)S(1)}, bf16[256,256]{1,0:T(8,128)(2,1)S(1)}, u32[]{:S(2)}, u32[]{:S(2)}) collective-permute-start(bf16[256,256]{1,0:T(8,128)(2,1)S(1)} %get-tuple-element.14), channel_id=1, source_target_pairs={{0,64},{64,128},{128,192},{192,0},{1,65},{65,129},{129,193},{193,1... | collective-permute-start | bytes 393224 | tf_op jit(solution)/shard_map/query_sum/ppermute | solution.py:365
  102.6 6.5 %collective-permute-start.14 = (bf16[4,256,128]{2,1,0:T(8,128)(2,1)S(1)}, bf16[4,256,128]{2,1,0:T(8,128)(2,1)S(1)}, u32[]{:S(2)}, u32[]{:S(2)}) collective-permute-start(bf16[4,256,128]{2,1,0:T(8,128)(2,1)S(1)} %pad_maximum_fusion), channel_id=1, source_target_pairs={{0,1},{1,0},{2,3},{3,2},{4,5},{5,4},{6,7},{7,6},{8,9},{9,8},{10,11... | collective-permute-start | bytes 786440 | tf_op jit(solution)/shard_map/heads/ppermute | solution.py:378

commit v2 on v1

v2 whole, which is shorter than its diff:
```python
import functools

import jax
import jax.numpy as jnp
from jax import lax
from jax.experimental import pallas as pl
from jax.experimental.pallas import tpu as pltpu
from jax.sharding import Mesh, PartitionSpec as P

DH = 128
QH = 16
KVH = 4
BLOCK = 128
NY, NZ, NX, NCORE = 4, 8, 4, 2
ROWS = 2 * BLOCK
WIDE = 2 * BLOCK
PACKED = ROWS + 16
SCALE = DH ** (-0.5)
EXP2_SCALE = SCALE * 1.4426950408889634
LOWEST = -1e30
VMEM_BYTES = 24 * 1024 * 1024
WHOLE_VMEM = 60 * 1024 * 1024
F32 = jnp.float32
BF16 = jnp.bfloat16


def dot_nt(left, right):
    return lax.dot_general(left, right, (((1,), (1,)), ((), ())), preferred_element_type=F32)


def dot_nn(left, right):
    return lax.dot_general(left, right, (((1,), (0,)), ((), ())), preferred_element_type=F32)


def load_keys(core, z_rank, mine_ref, theirs_ref, which, target):
    for owner in range(2):

        @pl.when(core == owner)
        def _(owner=owner):
            for j in range(NZ):
                src = lax.rem(z_rank + j, NZ)
                target[owner, j] = mine_ref[src, which]
                target[1 - owner, j] = theirs_ref[src, which]


def load_queries(core, piece_refs, first_col, target, delta=None):
    def load(k, ref, first_col):
        for slot in range(2):
            for head in range(2):
                target[2 * k + slot, head * BLOCK : (head + 1) * BLOCK, :] = ref[
                    slot * BLOCK : (slot + 1) * BLOCK,
                    first_col + head * DH : first_col + (head + 1) * DH,
                ]
        if delta is not None and k:
            lines = ref[ROWS:PACKED, :WIDE].astype(F32)
            for slot in range(2):
                line = sum(lines[3 * slot + i : 3 * slot + i + 1, :] for i in range(3))
                delta[2 * k + slot] = jnp.broadcast_to(line, (8, WIDE))

    load(0, piece_refs[0], 0)
    load(1, piece_refs[1], first_col)
    load(3, piece_refs[3], first_col)
    for owner, ref in ((0, piece_refs[2]), (1, piece_refs[4])):

        @pl.when(core == owner)
        def _(ref=ref):
            load(2, ref, first_col)


def visible_tile(query_place, key_place, prompt_end):
    key_pos = key_place * BLOCK + lax.broadcasted_iota(jnp.int32, (BLOCK, WIDE), 0)
    query_pos = query_place * BLOCK + lax.rem(
        lax.broadcasted_iota(jnp.int32, (BLOCK, WIDE), 1), BLOCK
    )
    return (key_pos <= query_pos) | (key_pos < prompt_end)


def tile_max(scores):
    return jnp.max(scores.reshape(scores.shape[0] // 8, 8, WIDE), axis=0)


def tile_sum(probs):
    return jnp.sum(probs.reshape(probs.shape[0] // 8, 8, WIDE), axis=0)


def all_places(place_ref, y_rank, z_rank):
    low_places = [
        place_ref[0, lax.rem(y_rank + NY - k, NY) * NZ + z_rank] for k in range(NY)
    ]
    key_places = [place_ref[0, y_rank * NZ + lax.rem(z_rank + j, NZ)] for j in range(NZ)]
    return low_places, key_places


def extra_tile(low_places, key_places, prompt_end, k, j):
    ahead = (key_places[j] > low_places[k]) & (key_places[j] * BLOCK < prompt_end)
    return (ahead | (key_places[j] == low_places[k])) if (k, j) == (0, 0) else ahead


def probs_kernel(
    place_ref, prompt_ref, q0, q1, q2, q3, q4, mine_ref, theirs_ref,
    qs, ks, dense_ref, pair_ref, extra_ref, stats_ref, dense, pair, extra, low_peak,
):
    y_rank, z_rank, core = (lax.axis_index(axis) for axis in ("y", "z", "core"))
    prompt_end = prompt_ref[0]
    load_keys(core, z_rank, mine_ref, theirs_ref, 0, ks)
    load_queries(core, (q0, q1, q2, q3, q4), 0, qs)
    low_places, key_places = all_places(place_ref, y_rank, z_rank)
    own_high = place_ref[1, y_rank * NZ + z_rank]
    stats_ref[...] = jnp.zeros((24, WIDE), F32)
    for k in range(NY):
        query_high = qs[2 * k + 1]
        high = []
        low = []
        for chunk in range(NZ // 2):
            keys = ks[0, 2 * chunk : 2 * chunk + 2].reshape(2 * BLOCK, DH)
            scores = dot_nt(keys, query_high) * EXP2_SCALE
            dense[2 * chunk * BLOCK : 2 * (chunk + 1) * BLOCK, :] = scores
            high.append(tile_max(scores))
        for j in range(NZ):
            is_low = key_places[j] < low_places[k]
            slot = jnp.where(is_low, 0, 1)
            scores = dot_nt(ks[slot, j], qs[2 * k + slot]) * EXP2_SCALE
            if (k, j) == (0, 0):
                scores = jnp.where(visible_tile(own_high, own_high, prompt_end), scores, LOWEST)
            pair[j * BLOCK : (j + 1) * BLOCK, :] = scores
            peak = tile_max(scores)
            high.append(jnp.where(is_low, LOWEST, peak))
            low.append(jnp.where(is_low, peak, LOWEST))
        low_peak[...] = functools.reduce(jnp.maximum, low)
        for j in range(NZ):

            @pl.when(extra_tile(low_places, key_places, prompt_end, k, j))
            def _(k=k, j=j):
                scores = dot_nt(ks[0, j], qs[2 * k]) * EXP2_SCALE
                visible = visible_tile(low_places[k], key_places[j], prompt_end)
                scores = jnp.where(visible, scores, LOWEST)
                extra[j] = scores
                low_peak[...] = jnp.maximum(low_peak[...], tile_max(scores))

        high_top = jnp.max(functools.reduce(jnp.maximum, high), axis=0, keepdims=True)
        low_top = jnp.max(low_peak[...], axis=0, keepdims=True)
        high_sum = jnp.zeros((8, WIDE), F32)
        low_sum = jnp.zeros((8, WIDE), F32)
        for chunk in range(NZ // 2):
            rows = slice(2 * chunk * BLOCK, 2 * (chunk + 1) * BLOCK)
            probs = jnp.exp2(dense[rows, :] - high_top)
            dense_ref[k, rows, :] = probs.astype(BF16)
            high_sum = high_sum + tile_sum(probs)
        for j in range(NZ):
            rows = slice(j * BLOCK, (j + 1) * BLOCK)
            is_low = key_places[j] < low_places[k]
            probs = jnp.exp2(pair[rows, :] - jnp.where(is_low, low_top, high_top))
            pair_ref[k, rows, :] = probs.astype(BF16)
            part = tile_sum(probs)
            high_sum = high_sum + jnp.where(is_low, 0.0, part)
            low_sum = low_sum + jnp.where(is_low, part, 0.0)
        low_peak[...] = low_sum
        for j in range(NZ):

            @pl.when(extra_tile(low_places, key_places, prompt_end, k, j))
            def _(k=k, j=j):
                probs = jnp.exp2(extra[j] - low_top)
                extra_ref[k, j] = probs.astype(BF16)
                low_peak[...] += tile_sum(probs)

        row = lax.rem(y_rank + NY - k, NY) * 2
        low_total = jnp.sum(low_peak[...], axis=0, keepdims=True)
        high_total = jnp.sum(high_sum, axis=0, keepdims=True)
        stats_ref[pl.ds(row, 1), :] = low_top
        stats_ref[pl.ds(row + 1, 1), :] = high_top
        stats_ref[pl.ds(row + 8, 1), :] = low_total
        stats_ref[pl.ds(row + 9, 1), :] = high_total


def scores_kernel(
    place_ref, prompt_ref, ks, g0, g1, g2, g3, g4, own_delta, mine_ref, theirs_ref,
    dense_ref, pair_ref, extra_ref,
    gs, dense_out, pair_out, extra_out, query_acc, vs, kt, delta,
):
    y_rank, z_rank, core = (lax.axis_index(axis) for axis in ("y", "z", "core"))
    prompt_end = prompt_ref[0]
    load_keys(core, z_rank, mine_ref, theirs_ref, 1, vs)
    load_queries(core, (g0, g1, g2, g3, g4), WIDE, gs, delta)
    for slot in range(2):
        delta[slot] = jnp.broadcast_to(own_delta[slot : slot + 1, :], (8, WIDE))
    low_places, key_places = all_places(place_ref, y_rank, z_rank)
    for slot in range(2):
        for j in range(NZ):
            kt[slot, :, j * BLOCK : (j + 1) * BLOCK] = ks[slot, j].T

    def scores(probs, values, query_index):
        length = values.shape[0]
        shape = (length // 8, 8, WIDE)
        dprobs = dot_nt(values, gs[query_index]).reshape(shape) - delta[query_index][None]
        return (probs.astype(F32) * dprobs.reshape(length, WIDE)).astype(BF16)

    for k in range(NY):
        for chunk in range(NZ // 2):
            rows = slice(2 * chunk * BLOCK, 2 * (chunk + 1) * BLOCK)
            values = vs[0, 2 * chunk : 2 * chunk + 2].reshape(2 * BLOCK, DH)
            dense_out[k, rows, :] = scores(dense_ref[k, rows, :], values, 2 * k + 1)
        query_acc[2 * k + 1] = dot_nn(kt[0], dense_out[k])
        query_acc[2 * k] = jnp.zeros((DH, WIDE), F32)
        for j in range(NZ):
            rows = slice(j * BLOCK, (j + 1) * BLOCK)
            slot = jnp.where(key_places[j] < low_places[k], 0, 1)
            dscores = scores(pair_ref[k, rows, :], vs[slot, j], 2 * k + slot)
            pair_out[k, rows, :] = dscores
            query_acc[2 * k + slot] += dot_nn(kt[slot, :, rows], dscores)
        for j in range(NZ):

            @pl.when(extra_tile(low_places, key_places, prompt_end, k, j))
            def _(k=k, j=j):
                dscores = scores(extra_ref[k, j], vs[0, j], 2 * k)
                extra_out[k, j] = dscores
                query_acc[2 * k] += dot_nn(kt[0, :, j * BLOCK : (j + 1) * BLOCK], dscores)


def grad_kernel(
    place_ref, prompt_ref, qs, gs, dense_p, pair_p, extra_p, dense_s, pair_s, extra_s,
    query_acc, st0, st1, st2, st3,
    own_query, query1, query2, query3, keep_ref, send_ref,
    qr, gr, factor_rows, key_acc, value_acc,
):
    y_rank, z_rank, core = (lax.axis_index(axis) for axis in ("y", "z", "core"))
    prompt_end = prompt_ref[0]
    low_places, key_places = all_places(place_ref, y_rank, z_rank)
    parts = [(ref[0:8, :], ref[8:16, :]) for ref in (st0, st1, st2, st3)]
    top = functools.reduce(jnp.maximum, [peak for peak, _ in parts])
    total = sum(part * jnp.exp2(peak - top) for peak, part in parts)
    factor_rows[...] = jnp.exp2(parts[0][0] - top) / total
    for k in range(NY):
        for slot in range(2):
            row = lax.rem(y_rank + NY - k, NY) * 2 + slot
            line = factor_rows[pl.ds(row, 1), :]
            column = jnp.broadcast_to(line, (BLOCK, WIDE)).T
            index = 2 * k + slot
            qr[index] = (qs[index].astype(F32) * column).astype(BF16)
            gr[index] = (gs[index].astype(F32) * column).astype(BF16)
            out = (own_query, query1, query2, query3)[k]
            for head in range(2):
                lanes = slice(head * BLOCK, (head + 1) * BLOCK)
                block = (query_acc[index, :, lanes] * (line[:, lanes] * SCALE)).T
                out[
                    slot * BLOCK : (slot + 1) * BLOCK, head * DH : (head + 1) * DH
                ] = block.astype(out.dtype)
    for chunk in range(NZ // 2):
        blocks = slice(2 * chunk, 2 * chunk + 2)
        rows = slice(2 * chunk * BLOCK, 2 * (chunk + 1) * BLOCK)
        key_sum = value_sum = None
        for k in range(NY):
            value_part = dot_nn(dense_p[k, rows, :], gr[2 * k + 1])
            key_part = dot_nn(dense_s[k, rows, :], qr[2 * k + 1])
            value_sum = value_part if k == 0 else value_sum + value_part
            key_sum = key_part if k == 0 else key_sum + key_part
        key_acc[0, blocks] = key_sum.reshape(2, BLOCK, DH)
        value_acc[0, blocks] = value_sum.reshape(2, BLOCK, DH)
    key_acc[1] = jnp.zeros((NZ, BLOCK, DH), F32)
    value_acc[1] = jnp.zeros((NZ, BLOCK, DH), F32)
    for j in range(NZ):
        rows = slice(j * BLOCK, (j + 1) * BLOCK)
        for k in range(NY):
            slot = jnp.where(key_places[j] < low_places[k], 0, 1)
            value_acc[slot, j] += dot_nn(pair_p[k, rows, :], gr[2 * k + slot])
            key_acc[slot, j] += dot_nn(pair_s[k, rows, :], qr[2 * k + slot])
    for j in range(NZ):
        for k in range(NY):

            @pl.when(extra_tile(low_places, key_places, prompt_end, k, j))
            def _(k=k, j=j):
                value_acc[0, j] += dot_nn(extra_p[k, j], gr[2 * k])
                key_acc[0, j] += dot_nn(extra_s[k, j], qr[2 * k])

    for owner in range(2):

        @pl.when(core == owner)
        def _(owner=owner):
            for j in range(NZ):
                to = lax.rem(z_rank + j, NZ)
                for slot in range(2):
                    rows = slice(slot * BLOCK, (slot + 1) * BLOCK)
                    key_block = key_acc[slot, j] * SCALE
                    value_block = value_acc[slot, j]
                    kept, sent = (key_block, value_block) if owner == 0 else (value_block, key_block)
                    keep_ref[to, rows, :] = kept
                    send_ref[to, rows, :] = sent.astype(BF16)


def prepare_kernel(
    queries_ref, saved_ref, grad_ref, key_ref, value_ref, out_ref, spread_ref, delta_ref,
    saved, sems,
):
    first_row = pl.multiple_of(lax.axis_index("core") * BLOCK, BLOCK)
    first_col = pl.multiple_of(lax.axis_index("x") * DH, DH)
    own = (pl.ds(first_row, BLOCK), pl.ds(first_col, DH))
    copies = [
        pltpu.make_async_copy(source, target, sems.at[i])
        for i, (source, target) in enumerate(
            (
                (key_ref.at[own], spread_ref.at[0, 0]),
                (value_ref.at[own], spread_ref.at[0, 1]),
                (grad_ref, out_ref.at[pl.ds(0, ROWS), pl.ds(WIDE, WIDE)]),
                (saved_ref, saved),
                (queries_ref, out_ref.at[pl.ds(0, ROWS), pl.ds(0, WIDE)]),
            )
        )
    ]
    for copy in copies:
        copy.start()
    copies[0].wait()
    copies[1].wait()
    for z in range(1, NZ):
        spread_ref[z] = spread_ref[0]
    copies[2].wait()
    copies[3].wait()
    lines = []
    for slot in range(2):
        rows = slice(slot * BLOCK, (slot + 1) * BLOCK)
        heads = []
        for head in range(2):
            columns = slice(head * DH, (head + 1) * DH)
            beside = slice(WIDE + head * DH, WIDE + (head + 1) * DH)
            product = out_ref[rows, beside].astype(F32) * saved[rows, columns].astype(F32)
            heads.append(jnp.sum(product.T, axis=0, keepdims=True))
        rest = jnp.concatenate(heads, axis=1)
        for _ in range(3):
            term = rest.astype(BF16).astype(F32)
            lines.append(term)
            rest = rest - term
        delta_ref[slot : slot + 1, :] = jnp.concatenate(heads, axis=1)
    lines.append(jnp.zeros((PACKED - ROWS - len(lines), WIDE), F32))
    out_ref[ROWS:, :WIDE] = jnp.concatenate(lines, axis=0).astype(BF16)
    out_ref[ROWS:, WIDE:] = jnp.zeros((PACKED - ROWS, WIDE), BF16)
    copies[4].wait()


def join_kernel(own_ref, p1, p2, p3, theirs_ref, key_ref, value_ref):
    x_rank, core = lax.axis_index("x"), lax.axis_index("core")
    for k, ref in enumerate((own_ref, p1, p2, p3)):
        column = pl.multiple_of(lax.rem(x_rank + NX - k, NX) * DH, DH)
        for owner in range(2):

            @pl.when(core == owner)
            def _(owner=owner, ref=ref, k=k, column=column):
                outs = (key_ref, value_ref)
                outs[owner][:, pl.ds(column, DH)] = ref[...]
                outs[1 - owner][:, pl.ds(column, DH)] = theirs_ref[k]


def call(kernel, n_scalars, n_arrays, out_shape, scratch=(), flops=0, far_in=0):
    return pl.pallas_call(
        kernel,
        out_shape=out_shape,
        in_specs=[pl.BlockSpec(memory_space=pltpu.SMEM)] * n_scalars
        + [pl.BlockSpec(memory_space=pl.ANY)] * far_in
        + [pl.BlockSpec(memory_space=pltpu.VMEM)] * n_arrays,
        out_specs=jax.tree.map(lambda _: pl.BlockSpec(memory_space=pltpu.VMEM), out_shape),
        scratch_shapes=list(scratch),
        compiler_params=pltpu.CompilerParams(vmem_limit_bytes=WHOLE_VMEM if far_in else VMEM_BYTES),
        cost_estimate=pl.CostEstimate(flops=flops, bytes_accessed=0, transcendentals=0),
    )


def shifts(array, axis, size):
    return [
        lax.ppermute(array, axis, [(i, (i + k) % size) for i in range(size)])
        for k in range(1, size)
    ]


def step_of_one_core(mover, step):
    return [
        (y * NCORE + core, (y + step) % NY * NCORE + core if core == mover else y * NCORE + core)
        for y in range(NY)
        for core in range(NCORE)
    ]


def shards(
    queries, key_states, value_states, saved_output, output_grad, block_place, prompt_length
):
    scalars = (block_place.T, prompt_length)
    shape = jax.ShapeDtypeStruct

    def swap(array):
        return lax.ppermute(array, "core", [(0, 1), (1, 0)])

    blocks = shape((8, WIDE, DH), BF16)
    sides = shape((2, NZ, BLOCK, DH), BF16)
    tall = shape((NY, NZ * BLOCK, WIDE), BF16)
    tiles = shape((NY, NZ, BLOCK, WIDE), BF16)
    with jax.named_scope("gather"):
        packed, spread, own_delta = call(
            prepare_kernel, 0, 0,
            (
                shape((PACKED, 2 * WIDE), BF16), shape((NZ, 2, BLOCK, DH), BF16),
                shape((8, WIDE), F32),
            ),
            [pltpu.VMEM((ROWS, WIDE), BF16), pltpu.SemaphoreType.DMA((5,))],
            far_in=5,
        )(queries, saved_output, output_grad, key_states, value_states)
        down = lax.ppermute(packed, "y", [(i, (i - 1) % NY) for i in range(NY)])
        up = lax.ppermute(packed, "y", [(i, (i + 1) % NY) for i in range(NY)])
        far = lax.ppermute(packed, ("y", "core"), step_of_one_core(0, 2))
        relayed = lax.ppermute(down, ("y", "core"), step_of_one_core(1, -1))
        pieces = [up, far, down, relayed]
        mine = lax.all_to_all(spread, "z", 0, 0, tiled=True)
        mine, *pieces = lax.optimization_barrier((mine, *pieces))
        theirs = swap(mine)
    with jax.named_scope("probs"):
        qs, ks, dense_p, pair_p, extra_p, stats = call(
            probs_kernel, 2, 7, (blocks, sides, tall, tall, tiles, shape((24, WIDE), F32)),
            [
                pltpu.VMEM((NZ * BLOCK, WIDE), F32),
                pltpu.VMEM((NZ * BLOCK, WIDE), F32),
                pltpu.VMEM((NZ, BLOCK, WIDE), F32),
                pltpu.VMEM((8, WIDE), F32),
            ],
        )(*scalars, queries, *pieces, mine, theirs)
        all_stats = [stats, *shifts(stats, "y", NY)]
    with jax.named_scope("scores"):
        gs, dense_s, pair_s, extra_s, query_acc = call(
            scores_kernel, 2, 12, (blocks, tall, tall, tiles, shape((8, DH, WIDE), F32)),
            [
                pltpu.VMEM((2, NZ, BLOCK, DH), BF16),
                pltpu.VMEM((2, DH, NZ * BLOCK), BF16),
                pltpu.VMEM((8, 8, WIDE), F32),
            ],
            flops=4_000_000_000,
        )(
            *scalars, ks, output_grad, *pieces, own_delta, mine, theirs, dense_p, pair_p,
            extra_p,
        )
    with jax.named_scope("grads"):
        piece = shape((ROWS, WIDE), BF16)
        own_query, query1, query2, query3, keep, send = call(
            grad_kernel, 2, 13,
            (
                shape((ROWS, WIDE), F32), piece, piece, piece,
                shape((NZ, ROWS, DH), F32), shape((NZ, ROWS, DH), BF16),
            ),
            [
                pltpu.VMEM((8, WIDE, DH), BF16),
                pltpu.VMEM((8, WIDE, DH), BF16),
                pltpu.VMEM((8, WIDE), F32),
                pltpu.VMEM((2, NZ, BLOCK, DH), F32),
                pltpu.VMEM((2, NZ, BLOCK, DH), F32),
            ],
        )(
            *scalars, qs, gs, dense_p, pair_p, extra_p, dense_s, pair_s, extra_s, query_acc,
            *all_stats,
        )
    with jax.named_scope("query_sum"):
        back = [
            lax.ppermute(part, "y", [(i, (i - k) % NY) for i in range(NY)])
            for k, part in ((1, query1), (2, query2), (3, query3))
        ]
        query_grad = own_query
        for part in back:
            query_grad = query_grad + part.astype(F32)
        query_grad = query_grad.astype(BF16)
    with jax.named_scope("key_sum"):
        pair = (keep + swap(send).astype(F32)).astype(BF16)
        terms = lax.all_to_all(pair, "z", 0, 0, tiled=True)
        own_sum = jnp.sum(terms.astype(F32), axis=0).astype(BF16)
        own_sum, query_grad = lax.optimization_barrier((own_sum, query_grad))
    with jax.named_scope("heads"):
        heads = shifts(own_sum, "x", NX)
        theirs_sum = swap(jnp.stack([own_sum, *heads]))
        full = shape((ROWS, KVH * DH), BF16)
        key_grad, value_grad = call(join_kernel, 0, 5, (full, full))(
            own_sum, *heads, theirs_sum
        )
    return (query_grad, key_grad, value_grad)


def solution(mesh):
    grid = Mesh(mesh.devices.reshape(NY, NZ, NX, NCORE), ("y", "z", "x", "core"))
    rows, heads = ("y", "z"), ("x", "core")
    placed = (
        P(rows, heads),
        P(rows, None),
        P(rows, None),
        P(rows, heads),
        P(rows, heads),
        P(),
        P(),
    )
    return jax.shard_map(
        shards,
        mesh=grid,
        in_specs=placed,
        out_specs=(P(rows, heads), P(rows, None), P(rows, None)),
        check_vma=False,
    )
```

time: 111 us -> 90.3 us (0.81)
  blocking collectives: 45.3 us -> 0 us
  starting transfers between devices: 17.6 us -> 41.7 us
  Pallas kernels: 19.2 us -> 16.3 us
  waiting for transfers between devices: 25 us -> 27.1 us
    all_to_all x2 -> x0, blocking collectives: 45.3 us -> none  [the longest x1 24.9 us: shards(): mine = lax.all_to_all(spread, 'z', 0, 0, tiled=True)]
    ppermute x9 -> x6, waiting for transfers between devices: 19.4 us -> 2.32 us  [shifts(): lax.ppermute(array, axis, [(i, (i + k) % size) for i in range(size)])]
    all_to_all x0 -> x2, starting transfers between devices: none -> 14.1 us  [the longest x1 9.03 us: shards(): mine = lax.all_to_all(spread, 'z', 0, 0, tiled=True)]
    ppermute x3 -> x7, waiting for transfers between devices: 1.54 us -> 11.3 us  [the longest x1 4 us: shards(): relayed = lax.ppermute(down, ('y', 'core'), step_of_one_core(1, -1))]
    all_to_all x0 -> x2, waiting for transfers between devices: none -> 8.32 us  [the longest x1 7.65 us: shards(): terms = lax.all_to_all(pair, 'z', 0, 0, tiled=True)]
    ppermute x3 -> x7, starting transfers between devices: 6.18 us -> 13.3 us  [the longest x1 5.2 us: shards(): relayed = lax.ppermute(down, ('y', 'core'), step_of_one_core(1, -1))]
    pallas_call x3 -> x5, Pallas kernels: 19.2 us -> 16.3 us  [the longest x1 5.18 us: shards(): call(scores_kernel, 2, 12, (blocks, tall, tall, tiles, shape((8, DH, WIDE...]
    ppermute x3, starting transfers between devices: 2.37 us -> 4.42 us  [shards(): lax.ppermute(part, 'y', [(i, (i - k) % NY) for i in range(NY)])]
  transfers between devices with their start and end apart: 15 -> 18, of which waited for: 11 -> 11; matrix products, arithmetic and copies ran while one was open for 1% -> 1% of each run, Pallas kernels for 0% -> 6%
where the time goes in v2:
time: 90.3 us; the launch traced here: 89.9 us
  starting transfers between devices  41.7 us (46%)
  waiting for transfers between devices  27.1 us (30%)
  Pallas kernels  16.3 us (18%)
  other arithmetic  1.74 us (2%)
  local copies, waits for them, and re-layouts  1.6 us (2%)
  between operations  1.41 us (2%)
    ppermute x6, starting transfers between devices, shifts(): lax.ppermute(array, axis, [(i, (i + k) % size) for i in range(size)])  9.96 us
    all_to_all x1, starting transfers between devices, shards(): mine = lax.all_to_all(spread, 'z', 0, 0, tiled=True)  9.03 us
    all_to_all x1, waiting for transfers between devices, shards(): terms = lax.all_to_all(pair, 'z', 0, 0, tiled=True)  7.65 us
    ppermute x1, starting transfers between devices, shards(): relayed = lax.ppermute(down, ('y', 'core'), step_of_one_core(1, -1))  5.2 us
    pallas_call x1, Pallas kernels, shards(): call(scores_kernel, 2, 12, (blocks, tall, tall, tiles, shape((8, DH, WIDE...  5.18 us
    ppermute x3, waiting for transfers between devices, shards(): lax.ppermute(part, 'y', [(i, (i - k) % NY) for i in range(NY)])  5.16 us
    all_to_all x1, starting transfers between devices, shards(): terms = lax.all_to_all(pair, 'z', 0, 0, tiled=True)  5.04 us
    ppermute x3, starting transfers between devices, shards(): lax.ppermute(part, 'y', [(i, (i - k) % NY) for i in range(NY)])  4.42 us
  transfers between devices with their start and end apart: 18, of which 11 were waited for; matrix products, arithmetic and copies ran while one was open for 1% of the time, Pallas kernels for 6%

profile of v2, /device:TPU:1, one launch (start us, length us, event | category | flops | bytes accessed | tf_op | source)
XLA Modules:
  0.0 89.9 jit_solution(11347627207331557336)
XLA Ops:
  0.6 0.0 copy-start.1
  0.6 0.0 copy-start.3
  0.7 2.2 %gather.1 = (bf16[272,512]{1,0:T(8,128)(2,1)}, bf16[8,2,128,128]{3,2,1,0:T(8,128)(2,1)}, f32[8,256]{1,0:T(8,128)}) custom-call(bf16[256,256]{1,0:T(8,128)(2,1)} %q0.1, bf16[256,256]{1,0:T(8,128)(2,1)} %saved_ref.1, bf16[256,256]{1,0:T(8,128)(2,1)} %g0.1, bf16[256,512]{1,0:T(8,128)(2,1)} %key_ref.1, bf16[256,512]{1,0:T(8,128)(2,1)} %value_ref.1), custom_call_target="tpu_custom_call" | custom-call | tf_op jit(solution)/shard_map/gather/pallas_call | solution.py:393
  2.8 0.0 copy-start.4
  2.8 9.0 %all-to-all-start = ((bf16[8,2,128,128]{3,2,1,0:T(8,128)(2,1)}), bf16[8,2,128,128]{3,2,1,0:T(8,128)(2,1)S(1)}, u32[]{:S(2)}, u32[]{:S(2)}) async-start(bf16[8,2,128,128]{3,2,1,0:T(8,128)(2,1)} %get-tuple-element.32), calls=%async_computation | async-start | bytes 1048576 | tf_op jit(solution)/shard_map/gather/all_to_all | solution.py:407
  11.9 2.7 %collective-permute-start.2 = (bf16[272,512]{1,0:T(8,128)(2,1)}, bf16[272,512]{1,0:T(8,128)(2,1)S(1)}, u32[]{:S(2)}, u32[]{:S(2)}) collective-permute-start(bf16[272,512]{1,0:T(8,128)(2,1)} %get-tuple-element.33), channel_id=1, source_target_pairs={{0,192},{64,0},{128,64},{192,128},{1,193},{65,1},{129,65},{193,129... | collective-permute-start | bytes 835592 | tf_op jit(solution)/shard_map/gather/ppermute | solution.py:402
  14.6 0.0 collective-permute-start
  14.6 1.6 %collective-permute-start.1 = (bf16[272,512]{1,0:T(8,128)(2,1)}, bf16[272,512]{1,0:T(8,128)(2,1)S(1)}, u32[]{:S(2)}, u32[]{:S(2)}) collective-permute-start(bf16[272,512]{1,0:T(8,128)(2,1)} %get-tuple-element.33), channel_id=1, source_target_pairs={{0,128},{1,1},{64,192},{65,65},{128,0},{129,129},{192,64},{193,193... | collective-permute-start | bytes 835592 | tf_op jit(solution)/shard_map/gather/ppermute | solution.py:404
  16.2 3.7 %collective-permute-done.2.q3.g3 = bf16[272,512]{1,0:T(8,128)(2,1)S(1)} collective-permute-done((bf16[272,512]{1,0:T(8,128)(2,1)}, bf16[272,512]{1,0:T(8,128)(2,1)S(1)}, u32[]{:S(2)}, u32[]{:S(2)}) %collective-permute-start.2) | collective-permute-done | bytes 278560 | tf_op jit(solution)/shard_map/gather/ppermute | solution.py:402
  19.9 5.2 %collective-permute-start.3 = (bf16[272,512]{1,0:T(8,128)(2,1)S(1)}, bf16[272,512]{1,0:T(8,128)(2,1)S(1)}, u32[]{:S(2)}, u32[]{:S(2)}) collective-permute-start(bf16[272,512]{1,0:T(8,128)(2,1)S(1)} %collective-permute-done.2.q3.g3), channel_id=1, source_target_pairs={{0,0},{1,193},{64,64},{65,1},{128,128},{129,65},{192,192},{193,129... | collective-permute-start | bytes 835592 | tf_op jit(solution)/shard_map/gather/ppermute | solution.py:405
  25.1 0.0 collective-permute-done.q1.g1
  25.1 0.0 collective-permute-done.1.q2.g2
  25.2 4.0 %collective-permute-done.3.q4.g4 = bf16[272,512]{1,0:T(8,128)(2,1)S(1)} collective-permute-done((bf16[272,512]{1,0:T(8,128)(2,1)S(1)}, bf16[272,512]{1,0:T(8,128)(2,1)S(1)}, u32[]{:S(2)}, u32[]{:S(2)}) %collective-permute-start.3) | collective-permute-done | bytes 278560 | tf_op jit(solution)/shard_map/gather/ppermute | solution.py:405
  29.2 0.7 all-to-all-done.mine_ref
  29.8 0.5 collective-permute-start.4
  31.0 0.9 collective-permute-done.4.theirs_ref
  31.9 0.0 copy-start
  31.9 0.9 %copy-done = bf16[256,256]{1,0:T(8,128)(2,1)S(1)} copy-done((bf16[256,256]{1,0:T(8,128)(2,1)S(1)}, bf16[256,256]{1,0:T(8,128)(2,1)}, u32[]{:S(2)}) %copy-start) | copy-done | bytes 131096
  32.8 0.0 copy-start.2
  32.8 0.7 copy-done.2
  33.4 4.2 %probs.1 = (bf16[8,256,128]{2,1,0:T(8,128)(2,1)S(1)}, bf16[2,8,128,128]{3,2,1,0:T(8,128)(2,1)S(1)}, bf16[4,1024,256]{2,1,0:T(8,128)(2,1)S(1)}, bf16[4,1024,256]{...) custom-call(s32[2,32]{1,0:T(2,128)S(1)} %bitcast.9, s32[1]{0:T(128)S(6)} %copy.10.prompt_ref, ...), custom_call_target="tpu_custom_call" | custom-call | tf_op jit(solution)/shard_map/probs/pallas_call | solution.py:411
  37.6 1.4 %collective-permute-start.5 = (f32[24,256]{1,0:T(8,128)S(1)}, f32[24,256]{1,0:T(8,128)S(1)}, u32[]{:S(2)}, u32[]{:S(2)}) collective-permute-start(f32[24,256]{1,0:T(8,128)S(1)} %get-tuple-element.50.st0), channel_id=1, source_target_pairs={{0,64},{64,128},{128,192},{192,0},{1,65},{65,129},{129,193},{193,1... | collective-permute-start | bytes 73736 | tf_op jit(solution)/shard_map/probs/ppermute | solution.py:366
  39.0 2.6 %collective-permute-start.6 = (f32[24,256]{1,0:T(8,128)S(1)}, f32[24,256]{1,0:T(8,128)S(1)}, u32[]{:S(2)}, u32[]{:S(2)}) collective-permute-start(f32[24,256]{1,0:T(8,128)S(1)} %get-tuple-element.50.st0), channel_id=1, source_target_pairs={{0,128},{64,192},{128,0},{192,64},{1,129},{65,193},{129,1},{193,65... | collective-permute-start | bytes 73736 | tf_op jit(solution)/shard_map/probs/ppermute | solution.py:366
  41.6 1.1 %collective-permute-start.7 = (f32[24,256]{1,0:T(8,128)S(1)}, f32[24,256]{1,0:T(8,128)S(1)}, u32[]{:S(2)}, u32[]{:S(2)}) collective-permute-start(f32[24,256]{1,0:T(8,128)S(1)} %get-tuple-element.50.st0), channel_id=1, source_target_pairs={{0,192},{64,0},{128,64},{192,128},{1,193},{65,1},{129,65},{193,129... | collective-permute-start | bytes 73736 | tf_op jit(solution)/shard_map/probs/ppermute | solution.py:366
  42.7 0.0 copy-done.1
  42.7 0.0 copy-done.3
  42.7 0.0 copy-done.4
  42.7 5.2 %scores.1 = (bf16[8,256,128]{2,1,0:T(8,128)(2,1)S(1)}, bf16[4,1024,256]{2,1,0:T(8,128)(2,1)S(1)}, bf16[4,1024,256]{2,1,0:T(8,128)(2,1)S(1)}, bf16[4,8,128,256]{3,2,1,0:T(8,128)(2,1)S(1)}, f32[8,128,256]{2,1,0:T(8,128)S(1)}) custom-call(s32[2,32]{1,0:T(2,128)S(1)} %bitcast.10, s32[1]{0:T(128)S(6)} %copy.10.prompt_ref, ...), custom_call_target="tpu_custom_call" | custom-call | flops 4000000000 | tf_op jit(solution)/shard_map/scores/pallas_call | solution.py:422
  47.9 0.0 collective-permute-done.5.st1
  47.9 0.0 collective-permute-done.6.st2
  47.9 0.0 collective-permute-done.7.st3
  47.9 3.9 %grads.1 = (f32[256,256]{1,0:T(8,128)S(1)}, bf16[256,256]{1,0:T(8,128)(2,1)S(1)}, bf16[256,256]{1,0:T(8,128)(2,1)S(1)}, bf16[256,256]{1,0:T(8,128)(2,1)S(1)}, f3...) custom-call(s32[2,32]{1,0:T(2,128)S(1)} %bitcast.11, s32[1]{0:T(128)S(6)} %copy.10.prompt_ref, ...), custom_call_target="tpu_custom_call" | custom-call | tf_op jit(solution)/shard_map/grads/pallas_call | solution.py:436
  51.8 1.3 %collective-permute-start.8 = (bf16[8,256,128]{2,1,0:T(8,128)(2,1)S(1)}, bf16[8,256,128]{2,1,0:T(8,128)(2,1)S(1)}, u32[]{:S(2)}, u32[]{:S(2)}) collective-permute-start(bf16[8,256,128]{2,1,0:T(8,128)(2,1)S(1)} %get-tuple-element.52), channel_id=1, source_target_pairs={{0,1},{1,0},{2,3},{3,2},{4,5},{5,4},{6,7},{7,6},{8,9},{9,8},{10,11... | collective-permute-start | bytes 1572872 | tf_op jit(solution)/shard_map/key_sum/ppermute | solution.py:386
  53.1 1.5 %collective-permute-done.8 = bf16[8,256,128]{2,1,0:T(8,128)(2,1)S(1)} collective-permute-done((bf16[8,256,128]{2,1,0:T(8,128)(2,1)S(1)}, bf16[8,256,128]{2,1,0:T(8,128)(2,1)S(1)}, u32[]{:S(2)}, u32[]{:S(2)}) %collective-permute-start.8) | collective-permute-done | bytes 524320 | tf_op jit(solution)/shard_map/key_sum/ppermute | solution.py:386
  54.6 0.9 %add_convert_fusion = bf16[8,256,128]{2,1,0:T(8,128)(2,1)} fusion(f32[8,256,128]{2,1,0:T(8,128)S(1)} %get-tuple-element.51, bf16[8,256,128]{2,1,0:T(8,128)(2,1)S(1)} %collective-permute-done.8), kind=kLoop, calls=%fused_computation | loop fusion | flops 786432 | bytes 2097152 | tf_op jit(solution)/shard_map/key_sum/convert_element_type | solution.py:463
  55.6 5.0 %all-to-all-start.1 = ((bf16[8,256,128]{2,1,0:T(8,128)(2,1)}), bf16[8,256,128]{2,1,0:T(8,128)(2,1)S(1)}, u32[]{:S(2)}, u32[]{:S(2)}) async-start(bf16[8,256,128]{2,1,0:T(8,128)(2,1)} %add_convert_fusion), calls=%async_computation.1 | async-start | bytes 1048576 | tf_op jit(solution)/shard_map/key_sum/all_to_all | solution.py:464
  60.6 1.7 %collective-permute-start.10 = (bf16[256,256]{1,0:T(8,128)(2,1)S(1)}, bf16[256,256]{1,0:T(8,128)(2,1)S(1)}, u32[]{:S(2)}, u32[]{:S(2)}) collective-permute-start(bf16[256,256]{1,0:T(8,128)(2,1)S(1)} %get-tuple-element.55), channel_id=1, source_target_pairs={{0,128},{64,192},{128,0},{192,64},{1,129},{65,193},{129,1},{193,65... | collective-permute-start | bytes 393224 | tf_op jit(solution)/shard_map/query_sum/ppermute | solution.py:455
  62.3 0.1 collective-permute-start.11
  62.4 2.6 %collective-permute-start.9 = (bf16[256,256]{1,0:T(8,128)(2,1)S(1)}, bf16[256,256]{1,0:T(8,128)(2,1)S(1)}, u32[]{:S(2)}, u32[]{:S(2)}) collective-permute-start(bf16[256,256]{1,0:T(8,128)(2,1)S(1)} %get-tuple-element.54), channel_id=1, source_target_pairs={{0,192},{64,0},{128,64},{192,128},{1,193},{65,1},{129,65},{193,129... | collective-permute-start | bytes 393224 | tf_op jit(solution)/shard_map/query_sum/ppermute | solution.py:455
  65.0 1.5 %collective-permute-done.10 = bf16[256,256]{1,0:T(8,128)(2,1)S(1)} collective-permute-done((bf16[256,256]{1,0:T(8,128)(2,1)S(1)}, bf16[256,256]{1,0:T(8,128)(2,1)S(1)}, u32[]{:S(2)}, u32[]{:S(2)}) %collective-permute-start.10) | collective-permute-done | bytes 131104 | tf_op jit(solution)/shard_map/query_sum/ppermute | solution.py:455
  66.5 3.7 %collective-permute-done.11 = bf16[256,256]{1,0:T(8,128)(2,1)S(1)} collective-permute-done((bf16[256,256]{1,0:T(8,128)(2,1)S(1)}, bf16[256,256]{1,0:T(8,128)(2,1)S(1)}, u32[]{:S(2)}, u32[]{:S(2)}) %collective-permute-start.11) | collective-permute-done | bytes 131104 | tf_op jit(solution)/shard_map/query_sum/ppermute | solution.py:455
  70.2 0.0 collective-permute-done.9
  70.2 0.7 add_convert_fusion.1
  70.9 7.7 %all-to-all-done.1 = bf16[8,256,128]{2,1,0:T(8,128)(2,1)S(1)} async-done(((bf16[8,256,128]{2,1,0:T(8,128)(2,1)}), bf16[8,256,128]{2,1,0:T(8,128)(2,1)S(1)}, u32[]{:S(2)}, u32[]{:S(2)}) %all-to-all-start.1) | async-done | bytes 524320 | tf_op jit(solution)/shard_map/key_sum/all_to_all | solution.py:464
  78.5 0.1 reduce_sum.12.own_ref
  78.6 1.3 %collective-permute-start.12 = (bf16[256,128]{1,0:T(8,128)(2,1)S(1)}, bf16[256,128]{1,0:T(8,128)(2,1)S(1)}, u32[]{:S(2)}, u32[]{:S(2)}) collective-permute-start(bf16[256,128]{1,0:T(8,128)(2,1)S(1)} %reduce_sum.12.own_ref), channel_id=1, source_target_pairs={{0,2},{2,4},{4,6},{6,0},{1,3},{3,5},{5,7},{7,1},{8,10},{10,12},{12... | collective-permute-start | bytes 196616 | tf_op jit(solution)/shard_map/heads/ppermute | solution.py:366
  79.9 2.5 %collective-permute-start.13 = (bf16[256,128]{1,0:T(8,128)(2,1)S(1)}, bf16[256,128]{1,0:T(8,128)(2,1)S(1)}, u32[]{:S(2)}, u32[]{:S(2)}) collective-permute-start(bf16[256,128]{1,0:T(8,128)(2,1)S(1)} %reduce_sum.12.own_ref), channel_id=1, source_target_pairs={{0,4},{2,6},{4,0},{6,2},{1,5},{3,7},{5,1},{7,3},{8,12},{10,14},{12... | collective-permute-start | bytes 196616 | tf_op jit(solution)/shard_map/heads/ppermute | solution.py:366
  82.4 1.2 %collective-permute-start.14 = (bf16[256,128]{1,0:T(8,128)(2,1)S(1)}, bf16[256,128]{1,0:T(8,128)(2,1)S(1)}, u32[]{:S(2)}, u32[]{:S(2)}) collective-permute-start(bf16[256,128]{1,0:T(8,128)(2,1)S(1)} %reduce_sum.12.own_ref), channel_id=1, source_target_pairs={{0,6},{2,0},{4,2},{6,4},{1,7},{3,1},{5,3},{7,5},{8,14},{10,8},{12,... | collective-permute-start | bytes 196616 | tf_op jit(solution)/shard_map/heads/ppermute | solution.py:366
  83.5 0.0 collective-permute-done.12.p1
  83.5 1.7 %collective-permute-done.13.p2 = bf16[256,128]{1,0:T(8,128)(2,1)S(1)} collective-permute-done((bf16[256,128]{1,0:T(8,128)(2,1)S(1)}, bf16[256,128]{1,0:T(8,128)(2,1)S(1)}, u32[]{:S(2)}, u32[]{:S(2)}) %collective-permute-start.13) | collective-permute-done | bytes 65568 | tf_op jit(solution)/shard_map/heads/ppermute | solution.py:366
  85.2 0.7 collective-permute-done.14.p3
  85.9 1.9 %collective-permute-start.15 = (bf16[4,256,128]{2,1,0:T(8,128)(2,1)S(1)}, bf16[4,256,128]{2,1,0:T(8,128)(2,1)S(1)}, u32[]{:S(2)}, u32[]{:S(2)}) collective-permute-start(bf16[4,256,128]{2,1,0:T(8,128)(2,1)S(1)} %pad_maximum_fusion), channel_id=1, source_target_pairs={{0,1},{1,0},{2,3},{3,2},{4,5},{5,4},{6,7},{7,6},{8,9},{9,8},{10,11... | collective-permute-start | bytes 786440 | tf_op jit(solution)/shard_map/heads/ppermute | solution.py:386
  87.8 1.2 %collective-permute-done.15.theirs_ref = bf16[4,256,128]{2,1,0:T(8,128)(2,1)S(1)} collective-permute-done((bf16[4,256,128]{2,1,0:T(8,128)(2,1)S(1)}, bf16[4,256,128]{2,1,0:T(8,128)(2,1)S(1)}, u32[]{:S(2)}, u32[]{:S(2)}) %collective-permute-start.15) | collective-permute-done | bytes 262176 | tf_op jit(solution)/shard_map/heads/ppermute | solution.py:386
  89.0 0.9 heads.1
  (1 shorter events, 0.0 us)
Async XLA Ops:
  0.6 42.1 %copy-start.1 = (bf16[256,256]{1,0:T(8,128)(2,1)S(1)}, bf16[256,256]{1,0:T(8,128)(2,1)}, u32[]{:S(2)}) copy-start(bf16[256,256]{1,0:T(8,128)(2,1)} %g0.1) | copy-start | bytes 393220
  0.6 42.1 %copy-start.3 = (s32[32,2]{0,1:T(2,128)S(1)}, s32[32,2]{0,1:T(2,128)}, u32[]{:S(2)}) copy-start(s32[32,2]{0,1:T(2,128)} %param.12) | copy-start | bytes 772
  2.8 39.9 %copy-start.4 = (f32[8,256]{1,0:T(8,128)S(1)}, f32[8,256]{1,0:T(8,128)}, u32[]{:S(2)}) copy-start(f32[8,256]{1,0:T(8,128)} %get-tuple-element.41.own_delta) | copy-start | bytes 24580
  2.8 27.0 %all-to-all-start = ((bf16[8,2,128,128]{3,2,1,0:T(8,128)(2,1)}), bf16[8,2,128,128]{3,2,1,0:T(8,128)(2,1)S(1)}, u32[]{:S(2)}, u32[]{:S(2)}) async-start(bf16[8,2,128,128]{3,2,1,0:T(8,128)(2,1)} %get-tuple-element.32), calls=%async_computation | async-start | bytes 1048576 | tf_op jit(solution)/shard_map/gather/all_to_all | solution.py:407
  11.9 8.1 %collective-permute-start.2 = (bf16[272,512]{1,0:T(8,128)(2,1)}, bf16[272,512]{1,0:T(8,128)(2,1)S(1)}, u32[]{:S(2)}, u32[]{:S(2)}) collective-permute-start(bf16[272,512]{1,0:T(8,128)(2,1)} %get-tuple-element.33), channel_id=1, source_target_pairs={{0,192},{64,0},{128,64},{192,128},{1,193},{65,1},{129,65},{193,129... | collective-permute-start | bytes 835592 | tf_op jit(solution)/shard_map/gather/ppermute | solution.py:402
  14.6 10.5 %collective-permute-start = (bf16[272,512]{1,0:T(8,128)(2,1)}, bf16[272,512]{1,0:T(8,128)(2,1)S(1)}, u32[]{:S(2)}, u32[]{:S(2)}) collective-permute-start(bf16[272,512]{1,0:T(8,128)(2,1)} %get-tuple-element.33), channel_id=1, source_target_pairs={{0,64},{64,128},{128,192},{192,0},{1,65},{65,129},{129,193},{193,1... | collective-permute-start | bytes 835592 | tf_op jit(solution)/shard_map/gather/ppermute | solution.py:403
  14.6 10.5 %collective-permute-start.1 = (bf16[272,512]{1,0:T(8,128)(2,1)}, bf16[272,512]{1,0:T(8,128)(2,1)S(1)}, u32[]{:S(2)}, u32[]{:S(2)}) collective-permute-start(bf16[272,512]{1,0:T(8,128)(2,1)} %get-tuple-element.33), channel_id=1, source_target_pairs={{0,128},{1,1},{64,192},{65,65},{128,0},{129,129},{192,64},{193,193... | collective-permute-start | bytes 835592 | tf_op jit(solution)/shard_map/gather/ppermute | solution.py:404
  19.9 9.2 %collective-permute-start.3 = (bf16[272,512]{1,0:T(8,128)(2,1)S(1)}, bf16[272,512]{1,0:T(8,128)(2,1)S(1)}, u32[]{:S(2)}, u32[]{:S(2)}) collective-permute-start(bf16[272,512]{1,0:T(8,128)(2,1)S(1)} %collective-permute-done.2.q3.g3), channel_id=1, source_target_pairs={{0,0},{1,193},{64,64},{65,1},{128,128},{129,65},{192,192},{193,129... | collective-permute-start | bytes 835592 | tf_op jit(solution)/shard_map/gather/ppermute | solution.py:405
  29.8 2.0 %collective-permute-start.4 = (bf16[8,2,128,128]{3,2,1,0:T(8,128)(2,1)S(1)}, bf16[8,2,128,128]{3,2,1,0:T(8,128)(2,1)S(1)}, u32[]{:S(2)}, u32[]{:S(2)}) collective-permute-start(bf16[8,2,128,128]{3,2,1,0:T(8,128)(2,1)S(1)} %all-to-all-done.mine_ref), channel_id=1, source_target_pairs={{0,1},{1,0},{2,3},{3,2},{4,5},{5,4},{6,7},{7,6},{8,9},{9,8},{10,11... | collective-permute-start | bytes 1572872 | tf_op jit(solution)/shard_map/gather/ppermute | solution.py:386
  31.9 0.9 %copy-start = (bf16[256,256]{1,0:T(8,128)(2,1)S(1)}, bf16[256,256]{1,0:T(8,128)(2,1)}, u32[]{:S(2)}) copy-start(bf16[256,256]{1,0:T(8,128)(2,1)} %q0.1) | copy-start | bytes 393220
  32.8 0.7 copy-start.2
  37.6 10.3 %collective-permute-start.5 = (f32[24,256]{1,0:T(8,128)S(1)}, f32[24,256]{1,0:T(8,128)S(1)}, u32[]{:S(2)}, u32[]{:S(2)}) collective-permute-start(f32[24,256]{1,0:T(8,128)S(1)} %get-tuple-element.50.st0), channel_id=1, source_target_pairs={{0,64},{64,128},{128,192},{192,0},{1,65},{65,129},{129,193},{193,1... | collective-permute-start | bytes 73736 | tf_op jit(solution)/shard_map/probs/ppermute | solution.py:366
  39.0 8.9 %collective-permute-start.6 = (f32[24,256]{1,0:T(8,128)S(1)}, f32[24,256]{1,0:T(8,128)S(1)}, u32[]{:S(2)}, u32[]{:S(2)}) collective-permute-start(f32[24,256]{1,0:T(8,128)S(1)} %get-tuple-element.50.st0), channel_id=1, source_target_pairs={{0,128},{64,192},{128,0},{192,64},{1,129},{65,193},{129,1},{193,65... | collective-permute-start | bytes 73736 | tf_op jit(solution)/shard_map/probs/ppermute | solution.py:366
  41.6 6.3 %collective-permute-start.7 = (f32[24,256]{1,0:T(8,128)S(1)}, f32[24,256]{1,0:T(8,128)S(1)}, u32[]{:S(2)}, u32[]{:S(2)}) collective-permute-start(f32[24,256]{1,0:T(8,128)S(1)} %get-tuple-element.50.st0), channel_id=1, source_target_pairs={{0,192},{64,0},{128,64},{192,128},{1,193},{65,1},{129,65},{193,129... | collective-permute-start | bytes 73736 | tf_op jit(solution)/shard_map/probs/ppermute | solution.py:366
  51.8 2.8 %collective-permute-start.8 = (bf16[8,256,128]{2,1,0:T(8,128)(2,1)S(1)}, bf16[8,256,128]{2,1,0:T(8,128)(2,1)S(1)}, u32[]{:S(2)}, u32[]{:S(2)}) collective-permute-start(bf16[8,256,128]{2,1,0:T(8,128)(2,1)S(1)} %get-tuple-element.52), channel_id=1, source_target_pairs={{0,1},{1,0},{2,3},{3,2},{4,5},{5,4},{6,7},{7,6},{8,9},{9,8},{10,11... | collective-permute-start | bytes 1572872 | tf_op jit(solution)/shard_map/key_sum/ppermute | solution.py:386
  55.6 23.0 %all-to-all-start.1 = ((bf16[8,256,128]{2,1,0:T(8,128)(2,1)}), bf16[8,256,128]{2,1,0:T(8,128)(2,1)S(1)}, u32[]{:S(2)}, u32[]{:S(2)}) async-start(bf16[8,256,128]{2,1,0:T(8,128)(2,1)} %add_convert_fusion), calls=%async_computation.1 | async-start | bytes 1048576 | tf_op jit(solution)/shard_map/key_sum/all_to_all | solution.py:464
  60.6 5.9 %collective-permute-start.10 = (bf16[256,256]{1,0:T(8,128)(2,1)S(1)}, bf16[256,256]{1,0:T(8,128)(2,1)S(1)}, u32[]{:S(2)}, u32[]{:S(2)}) collective-permute-start(bf16[256,256]{1,0:T(8,128)(2,1)S(1)} %get-tuple-element.55), channel_id=1, source_target_pairs={{0,128},{64,192},{128,0},{192,64},{1,129},{65,193},{129,1},{193,65... | collective-permute-start | bytes 393224 | tf_op jit(solution)/shard_map/query_sum/ppermute | solution.py:455
  62.3 7.8 %collective-permute-start.11 = (bf16[256,256]{1,0:T(8,128)(2,1)S(1)}, bf16[256,256]{1,0:T(8,128)(2,1)S(1)}, u32[]{:S(2)}, u32[]{:S(2)}) collective-permute-start(bf16[256,256]{1,0:T(8,128)(2,1)S(1)} %get-tuple-element.56), channel_id=1, source_target_pairs={{0,64},{64,128},{128,192},{192,0},{1,65},{65,129},{129,193},{193,1... | collective-permute-start | bytes 393224 | tf_op jit(solution)/shard_map/query_sum/ppermute | solution.py:455
  62.4 7.8 %collective-permute-start.9 = (bf16[256,256]{1,0:T(8,128)(2,1)S(1)}, bf16[256,256]{1,0:T(8,128)(2,1)S(1)}, u32[]{:S(2)}, u32[]{:S(2)}) collective-permute-start(bf16[256,256]{1,0:T(8,128)(2,1)S(1)} %get-tuple-element.54), channel_id=1, source_target_pairs={{0,192},{64,0},{128,64},{192,128},{1,193},{65,1},{129,65},{193,129... | collective-permute-start | bytes 393224 | tf_op jit(solution)/shard_map/query_sum/ppermute | solution.py:455
  78.6 4.9 %collective-permute-start.12 = (bf16[256,128]{1,0:T(8,128)(2,1)S(1)}, bf16[256,128]{1,0:T(8,128)(2,1)S(1)}, u32[]{:S(2)}, u32[]{:S(2)}) collective-permute-start(bf16[256,128]{1,0:T(8,128)(2,1)S(1)} %reduce_sum.12.own_ref), channel_id=1, source_target_pairs={{0,2},{2,4},{4,6},{6,0},{1,3},{3,5},{5,7},{7,1},{8,10},{10,12},{12... | collective-permute-start | bytes 196616 | tf_op jit(solution)/shard_map/heads/ppermute | solution.py:366
  79.9 5.3 %collective-permute-start.13 = (bf16[256,128]{1,0:T(8,128)(2,1)S(1)}, bf16[256,128]{1,0:T(8,128)(2,1)S(1)}, u32[]{:S(2)}, u32[]{:S(2)}) collective-permute-start(bf16[256,128]{1,0:T(8,128)(2,1)S(1)} %reduce_sum.12.own_ref), channel_id=1, source_target_pairs={{0,4},{2,6},{4,0},{6,2},{1,5},{3,7},{5,1},{7,3},{8,12},{10,14},{12... | collective-permute-start | bytes 196616 | tf_op jit(solution)/shard_map/heads/ppermute | solution.py:366
  82.4 3.5 %collective-permute-start.14 = (bf16[256,128]{1,0:T(8,128)(2,1)S(1)}, bf16[256,128]{1,0:T(8,128)(2,1)S(1)}, u32[]{:S(2)}, u32[]{:S(2)}) collective-permute-start(bf16[256,128]{1,0:T(8,128)(2,1)S(1)} %reduce_sum.12.own_ref), channel_id=1, source_target_pairs={{0,6},{2,0},{4,2},{6,4},{1,7},{3,1},{5,3},{7,5},{8,14},{10,8},{12,... | collective-permute-start | bytes 196616 | tf_op jit(solution)/shard_map/heads/ppermute | solution.py:366
  85.9 3.1 %collective-permute-start.15 = (bf16[4,256,128]{2,1,0:T(8,128)(2,1)S(1)}, bf16[4,256,128]{2,1,0:T(8,128)(2,1)S(1)}, u32[]{:S(2)}, u32[]{:S(2)}) collective-permute-start(bf16[4,256,128]{2,1,0:T(8,128)(2,1)S(1)} %pad_maximum_fusion), channel_id=1, source_target_pairs={{0,1},{1,0},{2,3},{3,2},{4,5},{5,4},{6,7},{7,6},{8,9},{9,8},{10,11... | collective-permute-start | bytes 786440 | tf_op jit(solution)/shard_map/heads/ppermute | solution.py:386

commit v3 on v2

--- a/solution.py
+++ b/solution.py
@@ -18,8 +18,9 @@
 SCALE = DH ** (-0.5)
 EXP2_SCALE = SCALE * 1.4426950408889634
 LOWEST = -1e30
-VMEM_BYTES = 24 * 1024 * 1024
+VMEM_BYTES = 32 * 1024 * 1024
 WHOLE_VMEM = 60 * 1024 * 1024
+STEPS = ((0, 7), (1, 3), (2, 4), (6, 5))
 F32 = jnp.float32
 BF16 = jnp.bfloat16
 
@@ -91,14 +92,32 @@
     return low_places, key_places
 
 
-def extra_tile(low_places, key_places, prompt_end, k, j):
-    ahead = (key_places[j] > low_places[k]) & (key_places[j] * BLOCK < prompt_end)
-    return (ahead | (key_places[j] == low_places[k])) if (k, j) == (0, 0) else ahead
+def ahead_of(low_places, key_places, prompt_end, k, j):
+    return (key_places[j] > low_places[k]) & (key_places[j] * BLOCK < prompt_end)
+
+
+def tiles_ahead(low_places, key_places, prompt_end, visit):
+    flags = [
+        [ahead_of(low_places, key_places, prompt_end, k, j) for j in range(NZ)] for k in range(NY)
+    ]
+    some = [functools.reduce(jnp.logical_or, flags[k]) for k in range(NY)]
+
+    @pl.when(functools.reduce(jnp.logical_or, some))
+    def _():
+        for k in range(NY):
+
+            @pl.when(some[k])
+            def _(k=k):
+                for j in range(NZ):
+
+                    @pl.when(flags[k][j])
+                    def _(j=j):
+                        visit(k, j)
 
 
 def probs_kernel(
     place_ref, prompt_ref, q0, q1, q2, q3, q4, mine_ref, theirs_ref,
-    qs, ks, dense_ref, pair_ref, extra_ref, stats_ref, dense, pair, extra, low_peak,
+    qs, ks, dense_ref, pair_ref, extra_ref, stats_ref, dense, pair, extra, low_peak, low_tops,
 ):
     y_rank, z_rank, core = (lax.axis_index(axis) for axis in ("y", "z", "core"))
     prompt_end = prompt_ref[0]
@@ -108,13 +127,25 @@
     own_high = place_ref[1, y_rank * NZ + z_rank]
     stats_ref[...] = jnp.zeros((24, WIDE), F32)
     for k in range(NY):
+        low_peak[k] = jnp.full((8, WIDE), LOWEST, F32)
+
+    def score_ahead(k, j):
+        scores = dot_nt(ks[0, j], qs[2 * k]) * EXP2_SCALE
+        visible = visible_tile(low_places[k], key_places[j], prompt_end)
+        scores = jnp.where(visible, scores, LOWEST)
+        extra[k, j] = scores
+        low_peak[k] = jnp.maximum(low_peak[k], tile_max(scores))
+
+    tiles_ahead(low_places, key_places, prompt_end, score_ahead)
+    tops = []
+    for k in range(NY):
         query_high = qs[2 * k + 1]
         high = []
-        low = []
+        low = [low_peak[k]]
         for chunk in range(NZ // 2):
             keys = ks[0, 2 * chunk : 2 * chunk + 2].reshape(2 * BLOCK, DH)
             scores = dot_nt(keys, query_high) * EXP2_SCALE
-            dense[2 * chunk * BLOCK : 2 * (chunk + 1) * BLOCK, :] = scores
+            dense[k, 2 * chunk * BLOCK : 2 * (chunk + 1) * BLOCK, :] = scores
             high.append(tile_max(scores))
         for j in range(NZ):
             is_low = key_places[j] < low_places[k]
@@ -122,60 +153,61 @@
             scores = dot_nt(ks[slot, j], qs[2 * k + slot]) * EXP2_SCALE
             if (k, j) == (0, 0):
                 scores = jnp.where(visible_tile(own_high, own_high, prompt_end), scores, LOWEST)
-            pair[j * BLOCK : (j + 1) * BLOCK, :] = scores
+            pair[k, j * BLOCK : (j + 1) * BLOCK, :] = scores
             peak = tile_max(scores)
             high.append(jnp.where(is_low, LOWEST, peak))
             low.append(jnp.where(is_low, peak, LOWEST))
-        low_peak[...] = functools.reduce(jnp.maximum, low)
-        for j in range(NZ):
-
-            @pl.when(extra_tile(low_places, key_places, prompt_end, k, j))
-            def _(k=k, j=j):
-                scores = dot_nt(ks[0, j], qs[2 * k]) * EXP2_SCALE
-                visible = visible_tile(low_places[k], key_places[j], prompt_end)
-                scores = jnp.where(visible, scores, LOWEST)
-                extra[j] = scores
-                low_peak[...] = jnp.maximum(low_peak[...], tile_max(scores))
-
+        if k == 0:
+            scores = dot_nt(ks[0, 0], qs[0]) * EXP2_SCALE
+            visible = visible_tile(low_places[0], key_places[0], prompt_end)
+            scores = jnp.where(visible, scores, LOWEST)
+            extra[0, 0] = scores
+            low.append(tile_max(scores))
         high_top = jnp.max(functools.reduce(jnp.maximum, high), axis=0, keepdims=True)
-        low_top = jnp.max(low_peak[...], axis=0, keepdims=True)
+        low_top = jnp.max(functools.reduce(jnp.maximum, low), axis=0, keepdims=True)
+        tops.append((low_top, high_top))
         high_sum = jnp.zeros((8, WIDE), F32)
         low_sum = jnp.zeros((8, WIDE), F32)
         for chunk in range(NZ // 2):
             rows = slice(2 * chunk * BLOCK, 2 * (chunk + 1) * BLOCK)
-            probs = jnp.exp2(dense[rows, :] - high_top)
+            probs = jnp.exp2(dense[k, rows, :] - high_top)
             dense_ref[k, rows, :] = probs.astype(BF16)
             high_sum = high_sum + tile_sum(probs)
         for j in range(NZ):
             rows = slice(j * BLOCK, (j + 1) * BLOCK)
             is_low = key_places[j] < low_places[k]
-            probs = jnp.exp2(pair[rows, :] - jnp.where(is_low, low_top, high_top))
+            probs = jnp.exp2(pair[k, rows, :] - jnp.where(is_low, low_top, high_top))
             pair_ref[k, rows, :] = probs.astype(BF16)
             part = tile_sum(probs)
             high_sum = high_sum + jnp.where(is_low, 0.0, part)
             low_sum = low_sum + jnp.where(is_low, part, 0.0)
-        low_peak[...] = low_sum
-        for j in range(NZ):
-
-            @pl.when(extra_tile(low_places, key_places, prompt_end, k, j))
-            def _(k=k, j=j):
-                probs = jnp.exp2(extra[j] - low_top)
-                extra_ref[k, j] = probs.astype(BF16)
-                low_peak[...] += tile_sum(probs)
-
+        if k == 0:
+            probs = jnp.exp2(extra[0, 0] - low_top)
+            extra_ref[0, 0] = probs.astype(BF16)
+            low_sum = low_sum + tile_sum(probs)
+        low_peak[k] = low_sum
+        low_tops[k] = jnp.broadcast_to(low_top, (8, WIDE))
         row = lax.rem(y_rank + NY - k, NY) * 2
-        low_total = jnp.sum(low_peak[...], axis=0, keepdims=True)
-        high_total = jnp.sum(high_sum, axis=0, keepdims=True)
         stats_ref[pl.ds(row, 1), :] = low_top
         stats_ref[pl.ds(row + 1, 1), :] = high_top
-        stats_ref[pl.ds(row + 8, 1), :] = low_total
-        stats_ref[pl.ds(row + 9, 1), :] = high_total
+        stats_ref[pl.ds(row + 9, 1), :] = jnp.sum(high_sum, axis=0, keepdims=True)
+
+    def probs_ahead(k, j):
+        probs = jnp.exp2((extra[k, j].reshape(BLOCK // 8, 8, WIDE) - low_tops[k][None]))
+        probs = probs.reshape(BLOCK, WIDE)
+        extra_ref[k, j] = probs.astype(BF16)
+        low_peak[k] += tile_sum(probs)
+
+    tiles_ahead(low_places, key_places, prompt_end, probs_ahead)
+    for k in range(NY):
+        row = lax.rem(y_rank + NY - k, NY) * 2
+        stats_ref[pl.ds(row + 8, 1), :] = jnp.sum(low_peak[k], axis=0, keepdims=True)
 
 
 def scores_kernel(
     place_ref, prompt_ref, ks, g0, g1, g2, g3, g4, own_delta, mine_ref, theirs_ref,
     dense_ref, pair_ref, extra_ref,
-    gs, dense_out, pair_out, extra_out, query_acc, vs, kt, delta,
+    gs, dense_out, pair_out, extra_out, query_acc, vs, kt, delta, low_part, chosen,
 ):
     y_rank, z_rank, core = (lax.axis_index(axis) for axis in ("y", "z", "core"))
     prompt_end = prompt_ref[0]
@@ -199,21 +231,27 @@
             rows = slice(2 * chunk * BLOCK, 2 * (chunk + 1) * BLOCK)
             values = vs[0, 2 * chunk : 2 * chunk + 2].reshape(2 * BLOCK, DH)
             dense_out[k, rows, :] = scores(dense_ref[k, rows, :], values, 2 * k + 1)
-        query_acc[2 * k + 1] = dot_nn(kt[0], dense_out[k])
-        query_acc[2 * k] = jnp.zeros((DH, WIDE), F32)
         for j in range(NZ):
             rows = slice(j * BLOCK, (j + 1) * BLOCK)
-            slot = jnp.where(key_places[j] < low_places[k], 0, 1)
+            is_low = key_places[j] < low_places[k]
+            slot = jnp.where(is_low, 0, 1)
             dscores = scores(pair_ref[k, rows, :], vs[slot, j], 2 * k + slot)
             pair_out[k, rows, :] = dscores
-            query_acc[2 * k + slot] += dot_nn(kt[slot, :, rows], dscores)
-        for j in range(NZ):
-
-            @pl.when(extra_tile(low_places, key_places, prompt_end, k, j))
-            def _(k=k, j=j):
-                dscores = scores(extra_ref[k, j], vs[0, j], 2 * k)
-                extra_out[k, j] = dscores
-                query_acc[2 * k] += dot_nn(kt[0, :, j * BLOCK : (j + 1) * BLOCK], dscores)
+            low_part[rows, :] = jnp.where(is_low, dscores, jnp.zeros_like(dscores))
+            chosen[:, rows] = kt[slot, :, rows]
+        low_query = dot_nn(chosen[...], low_part[...])
+        query_acc[2 * k] = low_query
+        query_acc[2 * k + 1] = (
+            dot_nn(kt[0], dense_out[k]) + dot_nn(chosen[...], pair_out[k]) - low_query
+        )
+
+    def scores_ahead(k, j):
+        dscores = scores(extra_ref[k, j], vs[0, j], 2 * k)
+        extra_out[k, j] = dscores
+        query_acc[2 * k] += dot_nn(kt[0, :, j * BLOCK : (j + 1) * BLOCK], dscores)
+
+    scores_ahead(0, 0)
+    tiles_ahead(low_places, key_places, prompt_end, scores_ahead)
 
 
 def grad_kernel(
@@ -263,27 +301,24 @@
             slot = jnp.where(key_places[j] < low_places[k], 0, 1)
             value_acc[slot, j] += dot_nn(pair_p[k, rows, :], gr[2 * k + slot])
             key_acc[slot, j] += dot_nn(pair_s[k, rows, :], qr[2 * k + slot])
-    for j in range(NZ):
-        for k in range(NY):
-
-            @pl.when(extra_tile(low_places, key_places, prompt_end, k, j))
-            def _(k=k, j=j):
-                value_acc[0, j] += dot_nn(extra_p[k, j], gr[2 * k])
-                key_acc[0, j] += dot_nn(extra_s[k, j], qr[2 * k])
+
+    def grads_ahead(k, j):
+        value_acc[0, j] += dot_nn(extra_p[k, j], gr[2 * k])
+        key_acc[0, j] += dot_nn(extra_s[k, j], qr[2 * k])
+
+    grads_ahead(0, 0)
+    tiles_ahead(low_places, key_places, prompt_end, grads_ahead)
 
     for owner in range(2):
 
         @pl.when(core == owner)
         def _(owner=owner):
-            for j in range(NZ):
-                to = lax.rem(z_rank + j, NZ)
-                for slot in range(2):
-                    rows = slice(slot * BLOCK, (slot + 1) * BLOCK)
-                    key_block = key_acc[slot, j] * SCALE
-                    value_block = value_acc[slot, j]
-                    kept, sent = (key_block, value_block) if owner == 0 else (value_block, key_block)
-                    keep_ref[to, rows, :] = kept
-                    send_ref[to, rows, :] = sent.astype(BF16)
+            for t, steps in enumerate(STEPS):
+                for j, ref in ((steps[owner], keep_ref), (steps[1 - owner], send_ref)):
+                    for slot in range(2):
+                        rows = slice(slot * BLOCK, (slot + 1) * BLOCK)
+                        ref[t, rows, :DH] = (key_acc[slot, j] * SCALE).astype(ref.dtype)
+                        ref[t, rows, DH:] = value_acc[slot, j].astype(ref.dtype)
 
 
 def prepare_kernel(
@@ -376,6 +411,14 @@
     ]
 
 
+def key_pairs(steps):
+    return [
+        (z * NCORE + core, (z + steps[core]) % NZ * NCORE + core)
+        for z in range(NZ)
+        for core in range(NCORE)
+    ]
+
+
 def shards(
     queries, key_states, value_states, saved_output, output_grad, block_place, prompt_length
 ):
@@ -405,18 +448,20 @@
         relayed = lax.ppermute(down, ("y", "core"), step_of_one_core(1, -1))
         pieces = [up, far, down, relayed]
         mine = lax.all_to_all(spread, "z", 0, 0, tiled=True)
-        mine, *pieces = lax.optimization_barrier((mine, *pieces))
+        own_query = packed[:ROWS, :WIDE]
+        mine, own_query, *pieces = lax.optimization_barrier((mine, own_query, *pieces))
         theirs = swap(mine)
     with jax.named_scope("probs"):
         qs, ks, dense_p, pair_p, extra_p, stats = call(
             probs_kernel, 2, 7, (blocks, sides, tall, tall, tiles, shape((24, WIDE), F32)),
             [
-                pltpu.VMEM((NZ * BLOCK, WIDE), F32),
-                pltpu.VMEM((NZ * BLOCK, WIDE), F32),
-                pltpu.VMEM((NZ, BLOCK, WIDE), F32),
-                pltpu.VMEM((8, WIDE), F32),
+                pltpu.VMEM((NY, NZ * BLOCK, WIDE), F32),
+                pltpu.VMEM((NY, NZ * BLOCK, WIDE), F32),
+                pltpu.VMEM((NY, NZ, BLOCK, WIDE), F32),
+                pltpu.VMEM((NY, 8, WIDE), F32),
+                pltpu.VMEM((NY, 8, WIDE), F32),
             ],
-        )(*scalars, queries, *pieces, mine, theirs)
+        )(*scalars, own_query, *pieces, mine, theirs)
         all_stats = [stats, *shifts(stats, "y", NY)]
     with jax.named_scope("scores"):
         gs, dense_s, pair_s, extra_s, query_acc = call(
@@ -425,6 +470,8 @@
                 pltpu.VMEM((2, NZ, BLOCK, DH), BF16),
                 pltpu.VMEM((2, DH, NZ * BLOCK), BF16),
                 pltpu.VMEM((8, 8, WIDE), F32),
+                pltpu.VMEM((NZ * BLOCK, WIDE), BF16),
+                pltpu.VMEM((DH, NZ * BLOCK), BF16),
             ],
             flops=4_000_000_000,
         )(
@@ -437,7 +484,8 @@
             grad_kernel, 2, 13,
             (
                 shape((ROWS, WIDE), F32), piece, piece, piece,
-                shape((NZ, ROWS, DH), F32), shape((NZ, ROWS, DH), BF16),
+                shape((len(STEPS), ROWS, 2 * DH), F32),
+                shape((len(STEPS), ROWS, 2 * DH), BF16),
             ),
             [
                 pltpu.VMEM((8, WIDE, DH), BF16),
@@ -450,20 +498,22 @@
             *scalars, qs, gs, dense_p, pair_p, extra_p, dense_s, pair_s, extra_s, query_acc,
             *all_stats,
         )
-    with jax.named_scope("query_sum"):
+    with jax.named_scope("key_sum"):
+        received = swap(send)
+        parts = {}
+        for t in (2, 3, 1, 0):
+            pair = (keep[t] + received[t].astype(F32)).astype(BF16)
+            parts[t] = lax.ppermute(pair, ("z", "core"), key_pairs(STEPS[t]))
         back = [
             lax.ppermute(part, "y", [(i, (i - k) % NY) for i in range(NY)])
             for k, part in ((1, query1), (2, query2), (3, query3))
         ]
-        query_grad = own_query
-        for part in back:
-            query_grad = query_grad + part.astype(F32)
-        query_grad = query_grad.astype(BF16)
-    with jax.named_scope("key_sum"):
-        pair = (keep + swap(send).astype(F32)).astype(BF16)
-        terms = lax.all_to_all(pair, "z", 0, 0, tiled=True)
-        own_sum = jnp.sum(terms.astype(F32), axis=0).astype(BF16)
-        own_sum, query_grad = lax.optimization_barrier((own_sum, query_grad))
+        parts, back = lax.optimization_barrier((parts, back))
+        total = sum(parts[t].astype(F32) for t in range(len(STEPS)))
+        core = lax.axis_index("core")
+        kept = jnp.where(core == 0, total[:, :DH], total[:, DH:])
+        sent = jnp.where(core == 0, total[:, DH:], total[:, :DH]).astype(BF16)
+        own_sum = (kept + swap(sent).astype(F32)).astype(BF16)
     with jax.named_scope("heads"):
         heads = shifts(own_sum, "x", NX)
         theirs_sum = swap(jnp.stack([own_sum, *heads]))
@@ -471,6 +521,11 @@
         key_grad, value_grad = call(join_kernel, 0, 5, (full, full))(
             own_sum, *heads, theirs_sum
         )
+    with jax.named_scope("query_sum"):
+        query_grad = own_query
+        for part in back:
+            query_grad = query_grad + part.astype(F32)
+        query_grad = query_grad.astype(BF16)
     return (query_grad, key_grad, value_grad)
 
 

time: 90.3 us -> 83.3 us (0.922)
  waiting for transfers between devices: 27.1 us -> 19 us
  starting transfers between devices: 41.7 us -> 46.4 us
  Pallas kernels: 16.3 us -> 14 us
    ppermute x0 -> x4, starting transfers between devices: none -> 11.5 us  [shards(): parts[t] = lax.ppermute(pair, ('z', 'core'), key_pairs(STEPS[t]))]
    all_to_all x1 -> x0, waiting for transfers between devices: 7.65 us -> none  [shards(): terms = lax.all_to_all(pair, 'z', 0, 0, tiled=True)]
    ppermute x0 -> x4, waiting for transfers between devices: none -> 7.02 us  [shards(): parts[t] = lax.ppermute(pair, ('z', 'core'), key_pairs(STEPS[t]))]
    ppermute x3, waiting for transfers between devices: 5.16 us -> 0.01 us  [shards(): lax.ppermute(part, 'y', [(i, (i - k) % NY) for i in range(NY)])]
    all_to_all x1 -> x0, starting transfers between devices: 5.04 us -> none  [shards(): terms = lax.all_to_all(pair, 'z', 0, 0, tiled=True)]
    ppermute x3, starting transfers between devices: 4.42 us -> 2.19 us  [shards(): lax.ppermute(part, 'y', [(i, (i - k) % NY) for i in range(NY)])]
    unnamed x10 -> x6, local copies, waits for them, and re-layouts: 1.6 us -> 0.01 us
    pallas_call x1, Pallas kernels: 5.18 us -> 3.77 us  [shards(): call(scores_kernel, 2, 12, (blocks, tall, tall, tiles, shape((8, DH, WIDE...]
  transfers between devices with their start and end apart: 18 -> 22, of which waited for: 11 -> 11; matrix products, arithmetic and copies ran while one was open for 1% -> 2% of each run, Pallas kernels for 6% -> 5%
where the time goes in v3:
time: 83.3 us; the launch traced here: 82.7 us
  starting transfers between devices  46.4 us (56%)
  waiting for transfers between devices  19 us (23%)
  Pallas kernels  14 us (17%)
  between operations  1.46 us (2%)
  other arithmetic  0.98 us (1%)
  local copies, waits for them, and re-layouts  0.93 us (1%)
    ppermute x4, starting transfers between devices, shards(): parts[t] = lax.ppermute(pair, ('z', 'core'), key_pairs(STEPS[t]))  11.5 us
    ppermute x6, starting transfers between devices, shifts(): lax.ppermute(array, axis, [(i, (i + k) % size) for i in range(size)])  9.99 us
    all_to_all x1, starting transfers between devices, shards(): mine = lax.all_to_all(spread, 'z', 0, 0, tiled=True)  9.03 us
    ppermute x4, waiting for transfers between devices, shards(): parts[t] = lax.ppermute(pair, ('z', 'core'), key_pairs(STEPS[t]))  7.02 us
    ppermute x1, starting transfers between devices, shards(): relayed = lax.ppermute(down, ('y', 'core'), step_of_one_core(1, -1))  5.2 us
    ppermute x4, starting transfers between devices, swap(): return lax.ppermute(array, 'core', [(0, 1), (1, 0)])  4.1 us
    pallas_call x1, Pallas kernels, shards(): call(scores_kernel, 2, 12, (blocks, tall, tall, tiles, shape((8, DH, WIDE...  3.77 us
    ppermute x1, waiting for transfers between devices, shards(): down = lax.ppermute(packed, 'y', [(i, (i - 1) % NY) for i in range(NY)])  3.72 us
  transfers between devices with their start and end apart: 22, of which 11 were waited for; matrix products, arithmetic and copies ran while one was open for 2% of the time, Pallas kernels for 5%

profile of v3, /device:TPU:1, one launch (start us, length us, event | category | flops | bytes accessed | tf_op | source)
XLA Modules:
  0.0 82.7 jit_solution(10265376858318785220)
XLA Ops:
  0.6 0.0 copy-start
  0.6 0.0 copy-start.1
  0.7 2.2 %gather.1 = (bf16[272,512]{1,0:T(8,128)(2,1)}, bf16[8,2,128,128]{3,2,1,0:T(8,128)(2,1)}, f32[8,256]{1,0:T(8,128)}) custom-call(bf16[256,256]{1,0:T(8,128)(2,1)} %queries_ref.1, bf16[256,256]{1,0:T(8,128)(2,1)} %saved_ref.1, bf16[256,256]{1,0:T(8,128)(2,1)} %g0.1, bf16[256,512]{1,0:T(8,128)(2,1)} %key_ref.1, bf16[256,512]{1,0:T(8,128)(2,1)} %value_ref.1), custom_call_target="tpu_custom_call" | custom-call | tf_op jit(solution)/shard_map/gather/pallas_call | solution.py:436
  2.8 0.0 copy-start.2
  2.8 9.0 %all-to-all-start = ((bf16[8,2,128,128]{3,2,1,0:T(8,128)(2,1)}), bf16[8,2,128,128]{3,2,1,0:T(8,128)(2,1)S(1)}, u32[]{:S(2)}, u32[]{:S(2)}) async-start(bf16[8,2,128,128]{3,2,1,0:T(8,128)(2,1)} %get-tuple-element.38), calls=%async_computation | async-start | bytes 1048576 | tf_op jit(solution)/shard_map/gather/all_to_all | solution.py:450
  11.8 2.7 %collective-permute-start.2 = (bf16[272,512]{1,0:T(8,128)(2,1)}, bf16[272,512]{1,0:T(8,128)(2,1)S(1)}, u32[]{:S(2)}, u32[]{:S(2)}) collective-permute-start(bf16[272,512]{1,0:T(8,128)(2,1)} %get-tuple-element.39), channel_id=1, source_target_pairs={{0,192},{64,0},{128,64},{192,128},{1,193},{65,1},{129,65},{193,129... | collective-permute-start | bytes 835592 | tf_op jit(solution)/shard_map/gather/ppermute | solution.py:445
  14.6 0.0 collective-permute-start
  14.6 1.6 %collective-permute-start.1 = (bf16[272,512]{1,0:T(8,128)(2,1)}, bf16[272,512]{1,0:T(8,128)(2,1)S(1)}, u32[]{:S(2)}, u32[]{:S(2)}) collective-permute-start(bf16[272,512]{1,0:T(8,128)(2,1)} %get-tuple-element.39), channel_id=1, source_target_pairs={{0,128},{1,1},{64,192},{65,65},{128,0},{129,129},{192,64},{193,193... | collective-permute-start | bytes 835592 | tf_op jit(solution)/shard_map/gather/ppermute | solution.py:447
  16.2 3.7 %collective-permute-done.2.q3.g3 = bf16[272,512]{1,0:T(8,128)(2,1)S(1)} collective-permute-done((bf16[272,512]{1,0:T(8,128)(2,1)}, bf16[272,512]{1,0:T(8,128)(2,1)S(1)}, u32[]{:S(2)}, u32[]{:S(2)}) %collective-permute-start.2) | collective-permute-done | bytes 278560 | tf_op jit(solution)/shard_map/gather/ppermute | solution.py:445
  19.9 5.2 %collective-permute-start.3 = (bf16[272,512]{1,0:T(8,128)(2,1)S(1)}, bf16[272,512]{1,0:T(8,128)(2,1)S(1)}, u32[]{:S(2)}, u32[]{:S(2)}) collective-permute-start(bf16[272,512]{1,0:T(8,128)(2,1)S(1)} %collective-permute-done.2.q3.g3), channel_id=1, source_target_pairs={{0,0},{1,193},{64,64},{65,1},{128,128},{129,65},{192,192},{193,129... | collective-permute-start | bytes 835592 | tf_op jit(solution)/shard_map/gather/ppermute | solution.py:448
  25.1 0.9 %slice.35.q0 = bf16[256,256]{1,0:T(8,128)(2,1)S(1)} slice(bf16[272,512]{1,0:T(8,128)(2,1)} %get-tuple-element.39), slice={[0:256], [0:256]} | slice | bytes 262144 | tf_op jit(solution)/shard_map/gather/slice | solution.py:451
  26.0 0.0 collective-permute-done.q1.g1
  26.0 0.0 collective-permute-done.1.q2.g2
  26.1 3.1 %collective-permute-done.3.q4.g4 = bf16[272,512]{1,0:T(8,128)(2,1)S(1)} collective-permute-done((bf16[272,512]{1,0:T(8,128)(2,1)S(1)}, bf16[272,512]{1,0:T(8,128)(2,1)S(1)}, u32[]{:S(2)}, u32[]{:S(2)}) %collective-permute-start.3) | collective-permute-done | bytes 278560 | tf_op jit(solution)/shard_map/gather/ppermute | solution.py:448
  29.1 0.7 all-to-all-done.mine_ref
  29.8 0.5 collective-permute-start.4
  31.0 0.9 %collective-permute-done.4.theirs_ref = bf16[8,2,128,128]{3,2,1,0:T(8,128)(2,1)S(1)} collective-permute-done((bf16[8,2,128,128]{3,2,1,0:T(8,128)(2,1)S(1)}, bf16[8,2,128,128]{3,2,1,0:T(8,128)(2,1)S(1)}, u32[]{:S(2)}, u32[]{:S(2)}) %collective-permute-start.4) | collective-permute-done | bytes 524320 | tf_op jit(solution)/shard_map/gather/ppermute | solution.py:429
  31.8 0.0 copy-done.1
  31.8 3.6 %probs.1 = (bf16[8,256,128]{2,1,0:T(8,128)(2,1)S(1)}, bf16[2,8,128,128]{3,2,1,0:T(8,128)(2,1)S(1)}, bf16[4,1024,256]{2,1,0:T(8,128)(2,1)S(1)}, bf16[4,1024,256]{...) custom-call(s32[2,32]{1,0:T(2,128)S(1)} %bitcast.17, s32[1]{0:T(128)S(6)} %copy.10.prompt_ref, ...), custom_call_target="tpu_custom_call" | custom-call | tf_op jit(solution)/shard_map/probs/pallas_call | solution.py:455
  35.5 1.4 %collective-permute-start.5 = (f32[24,256]{1,0:T(8,128)S(1)}, f32[24,256]{1,0:T(8,128)S(1)}, u32[]{:S(2)}, u32[]{:S(2)}) collective-permute-start(f32[24,256]{1,0:T(8,128)S(1)} %get-tuple-element.57.st0), channel_id=1, source_target_pairs={{0,64},{64,128},{128,192},{192,0},{1,65},{65,129},{129,193},{193,1... | collective-permute-start | bytes 73736 | tf_op jit(solution)/shard_map/probs/ppermute | solution.py:401
  36.8 2.6 %collective-permute-start.6 = (f32[24,256]{1,0:T(8,128)S(1)}, f32[24,256]{1,0:T(8,128)S(1)}, u32[]{:S(2)}, u32[]{:S(2)}) collective-permute-start(f32[24,256]{1,0:T(8,128)S(1)} %get-tuple-element.57.st0), channel_id=1, source_target_pairs={{0,128},{64,192},{128,0},{192,64},{1,129},{65,193},{129,1},{193,65... | collective-permute-start | bytes 73736 | tf_op jit(solution)/shard_map/probs/ppermute | solution.py:401
  39.5 1.1 %collective-permute-start.7 = (f32[24,256]{1,0:T(8,128)S(1)}, f32[24,256]{1,0:T(8,128)S(1)}, u32[]{:S(2)}, u32[]{:S(2)}) collective-permute-start(f32[24,256]{1,0:T(8,128)S(1)} %get-tuple-element.57.st0), channel_id=1, source_target_pairs={{0,192},{64,0},{128,64},{192,128},{1,193},{65,1},{129,65},{193,129... | collective-permute-start | bytes 73736 | tf_op jit(solution)/shard_map/probs/ppermute | solution.py:401
  40.5 0.0 copy-done
  40.5 0.0 copy-done.2
  40.5 3.8 %scores.1 = (bf16[8,256,128]{2,1,0:T(8,128)(2,1)S(1)}, bf16[4,1024,256]{2,1,0:T(8,128)(2,1)S(1)}, bf16[4,1024,256]{2,1,0:T(8,128)(2,1)S(1)}, bf16[4,8,128,256]{3,2,1,0:T(8,128)(2,1)S(1)}, f32[8,128,256]{2,1,0:T(8,128)S(1)}) custom-call(s32[2,32]{1,0:T(2,128)S(1)} %bitcast.18, s32[1]{0:T(128)S(6)} %copy.10.prompt_ref, ...), custom_call_target="tpu_custom_call" | custom-call | flops 4000000000 | tf_op jit(solution)/shard_map/scores/pallas_call | solution.py:467
  44.3 0.0 collective-permute-done.5.st1
  44.3 0.0 collective-permute-done.6.st2
  44.3 0.0 collective-permute-done.7.st3
  44.3 3.6 %grads.1 = (f32[256,256]{1,0:T(8,128)S(1)}, bf16[256,256]{1,0:T(8,128)(2,1)S(1)}, bf16[256,256]{1,0:T(8,128)(2,1)S(1)}, bf16[256,256]{1,0:T(8,128)(2,1)S(1)}, f3...) custom-call(s32[2,32]{1,0:T(2,128)S(1)} %bitcast.19, s32[1]{0:T(128)S(6)} %copy.10.prompt_ref, ...), custom_call_target="tpu_custom_call" | custom-call | tf_op jit(solution)/shard_map/grads/pallas_call | solution.py:483
  47.9 1.3 %collective-permute-start.8 = (bf16[4,256,256]{2,1,0:T(8,128)(2,1)S(1)}, bf16[4,256,256]{2,1,0:T(8,128)(2,1)S(1)}, u32[]{:S(2)}, u32[]{:S(2)}) collective-permute-start(bf16[4,256,256]{2,1,0:T(8,128)(2,1)S(1)} %get-tuple-element.60), channel_id=1, source_target_pairs={{0,1},{1,0},{2,3},{3,2},{4,5},{5,4},{6,7},{7,6},{8,9},{9,8},{10,11... | collective-permute-start | bytes 1572872 | tf_op jit(solution)/shard_map/key_sum/ppermute | solution.py:429
  49.2 0.9 %collective-permute-start.13 = (bf16[256,256]{1,0:T(8,128)(2,1)S(1)}, bf16[256,256]{1,0:T(8,128)(2,1)S(1)}, u32[]{:S(2)}, u32[]{:S(2)}) collective-permute-start(bf16[256,256]{1,0:T(8,128)(2,1)S(1)} %get-tuple-element.61), channel_id=1, source_target_pairs={{0,192},{64,0},{128,64},{192,128},{1,193},{65,1},{129,65},{193,129... | collective-permute-start | bytes 393224 | tf_op jit(solution)/shard_map/key_sum/ppermute | solution.py:508
  50.1 1.3 %collective-permute-start.14 = (bf16[256,256]{1,0:T(8,128)(2,1)S(1)}, bf16[256,256]{1,0:T(8,128)(2,1)S(1)}, u32[]{:S(2)}, u32[]{:S(2)}) collective-permute-start(bf16[256,256]{1,0:T(8,128)(2,1)S(1)} %get-tuple-element.62), channel_id=1, source_target_pairs={{0,128},{64,192},{128,0},{192,64},{1,129},{65,193},{129,1},{193,65... | collective-permute-start | bytes 393224 | tf_op jit(solution)/shard_map/key_sum/ppermute | solution.py:508
  51.4 0.0 collective-permute-start.15
  51.4 0.0 collective-permute-done.8
  51.4 0.1 fusion.3
  51.5 3.0 %collective-permute-start.10 = (bf16[256,256]{1,0:T(8,128)(2,1)S(1)}, bf16[256,256]{1,0:T(8,128)(2,1)S(1)}, u32[]{:S(2)}, u32[]{:S(2)}) collective-permute-start(bf16[256,256]{1,0:T(8,128)(2,1)S(1)} %get-tuple-element.75), channel_id=1, source_target_pairs={{0,8},{1,25},{8,16},{9,33},{16,24},{17,41},{24,32},{25,49},{32,40}... | collective-permute-start | bytes 393224 | tf_op jit(solution)/shard_map/key_sum/ppermute | solution.py:506
  54.6 2.4 %collective-permute-start.11 = (bf16[256,256]{1,0:T(8,128)(2,1)S(1)}, bf16[256,256]{1,0:T(8,128)(2,1)S(1)}, u32[]{:S(2)}, u32[]{:S(2)}) collective-permute-start(bf16[256,256]{1,0:T(8,128)(2,1)S(1)} %get-tuple-element.74), channel_id=1, source_target_pairs={{0,16},{1,33},{8,24},{9,41},{16,32},{17,49},{24,40},{25,57},{32,48... | collective-permute-start | bytes 393224 | tf_op jit(solution)/shard_map/key_sum/ppermute | solution.py:506
  57.0 0.0 collective-permute-done.13
  57.0 4.2 %collective-permute-start.12 = (bf16[256,256]{1,0:T(8,128)(2,1)S(1)}, bf16[256,256]{1,0:T(8,128)(2,1)S(1)}, u32[]{:S(2)}, u32[]{:S(2)}) collective-permute-start(bf16[256,256]{1,0:T(8,128)(2,1)S(1)} %get-tuple-element.73), channel_id=1, source_target_pairs={{0,48},{1,41},{8,56},{9,49},{16,0},{17,57},{24,8},{25,1},{32,16},{... | collective-permute-start | bytes 393224 | tf_op jit(solution)/shard_map/key_sum/ppermute | solution.py:506
  61.1 0.0 collective-permute-done.14
  61.2 1.9 %collective-permute-start.9 = (bf16[256,256]{1,0:T(8,128)(2,1)S(1)}, bf16[256,256]{1,0:T(8,128)(2,1)S(1)}, u32[]{:S(2)}, u32[]{:S(2)}) collective-permute-start(bf16[256,256]{1,0:T(8,128)(2,1)S(1)} %get-tuple-element.76), channel_id=1, source_target_pairs={{0,0},{1,57},{8,8},{9,1},{16,16},{17,9},{24,24},{25,17},{32,32},{3... | collective-permute-start | bytes 393224 | tf_op jit(solution)/shard_map/key_sum/ppermute | solution.py:506
  63.1 0.0 collective-permute-done.15
  63.1 0.0 collective-permute-done.10
  63.1 2.6 %collective-permute-done.11 = bf16[256,256]{1,0:T(8,128)(2,1)S(1)} collective-permute-done((bf16[256,256]{1,0:T(8,128)(2,1)S(1)}, bf16[256,256]{1,0:T(8,128)(2,1)S(1)}, u32[]{:S(2)}, u32[]{:S(2)}) %collective-permute-start.11) | collective-permute-done | bytes 131104 | tf_op jit(solution)/shard_map/key_sum/ppermute | solution.py:506
  65.7 0.5 collective-permute-done.12
  66.3 3.9 %collective-permute-done.9 = bf16[256,256]{1,0:T(8,128)(2,1)S(1)} collective-permute-done((bf16[256,256]{1,0:T(8,128)(2,1)S(1)}, bf16[256,256]{1,0:T(8,128)(2,1)S(1)}, u32[]{:S(2)}, u32[]{:S(2)}) %collective-permute-start.9) | collective-permute-done | bytes 131104 | tf_op jit(solution)/shard_map/key_sum/ppermute | solution.py:506
  70.1 0.1 convert_add_fusion
  70.2 0.5 collective-permute-start.16
  70.7 0.9 %collective-permute-done.16 = bf16[256,128]{1,0:T(8,128)(2,1)S(1)} collective-permute-done((bf16[256,128]{1,0:T(8,128)(2,1)S(1)}, bf16[256,128]{1,0:T(8,128)(2,1)S(1)}, u32[]{:S(2)}, u32[]{:S(2)}) %collective-permute-start.16) | collective-permute-done | bytes 65568 | tf_op jit(solution)/shard_map/key_sum/ppermute | solution.py:429
  71.6 1.3 %collective-permute-start.17 = (bf16[256,128]{1,0:T(8,128)(2,1)S(1)}, bf16[256,128]{1,0:T(8,128)(2,1)S(1)}, u32[]{:S(2)}, u32[]{:S(2)}) collective-permute-start(bf16[256,128]{1,0:T(8,128)(2,1)S(1)} %add_convert_fusion.5.own_ref), channel_id=1, source_target_pairs={{0,2},{2,4},{4,6},{6,0},{1,3},{3,5},{5,7},{7,1},{8,10},{10,12},{12... | collective-permute-start | bytes 196616 | tf_op jit(solution)/shard_map/heads/ppermute | solution.py:401
  72.9 2.4 %collective-permute-start.18 = (bf16[256,128]{1,0:T(8,128)(2,1)S(1)}, bf16[256,128]{1,0:T(8,128)(2,1)S(1)}, u32[]{:S(2)}, u32[]{:S(2)}) collective-permute-start(bf16[256,128]{1,0:T(8,128)(2,1)S(1)} %add_convert_fusion.5.own_ref), channel_id=1, source_target_pairs={{0,4},{2,6},{4,0},{6,2},{1,5},{3,7},{5,1},{7,3},{8,12},{10,14},{12... | collective-permute-start | bytes 196616 | tf_op jit(solution)/shard_map/heads/ppermute | solution.py:401
  75.3 1.2 %collective-permute-start.19 = (bf16[256,128]{1,0:T(8,128)(2,1)S(1)}, bf16[256,128]{1,0:T(8,128)(2,1)S(1)}, u32[]{:S(2)}, u32[]{:S(2)}) collective-permute-start(bf16[256,128]{1,0:T(8,128)(2,1)S(1)} %add_convert_fusion.5.own_ref), channel_id=1, source_target_pairs={{0,6},{2,0},{4,2},{6,4},{1,7},{3,1},{5,3},{7,5},{8,14},{10,8},{12,... | collective-permute-start | bytes 196616 | tf_op jit(solution)/shard_map/heads/ppermute | solution.py:401
  76.5 0.0 collective-permute-done.17.p1
  76.5 1.8 %collective-permute-done.18.p2 = bf16[256,128]{1,0:T(8,128)(2,1)S(1)} collective-permute-done((bf16[256,128]{1,0:T(8,128)(2,1)S(1)}, bf16[256,128]{1,0:T(8,128)(2,1)S(1)}, u32[]{:S(2)}, u32[]{:S(2)}) %collective-permute-start.18) | collective-permute-done | bytes 65568 | tf_op jit(solution)/shard_map/heads/ppermute | solution.py:401
  78.3 0.4 collective-permute-done.19.p3
  78.8 1.9 %collective-permute-start.20 = (bf16[4,256,128]{2,1,0:T(8,128)(2,1)S(1)}, bf16[4,256,128]{2,1,0:T(8,128)(2,1)S(1)}, u32[]{:S(2)}, u32[]{:S(2)}) collective-permute-start(bf16[4,256,128]{2,1,0:T(8,128)(2,1)S(1)} %pad_maximum_fusion), channel_id=1, source_target_pairs={{0,1},{1,0},{2,3},{3,2},{4,5},{5,4},{6,7},{7,6},{8,9},{9,8},{10,11... | collective-permute-start | bytes 786440 | tf_op jit(solution)/shard_map/heads/ppermute | solution.py:429
  80.7 0.7 add_convert_fusion
  81.4 0.4 collective-permute-done.20.theirs_ref
  81.8 0.9 %heads.1 = (bf16[256,512]{1,0:T(8,128)(2,1)}, bf16[256,512]{1,0:T(8,128)(2,1)}) custom-call(bf16[256,128]{1,0:T(8,128)(2,1)S(1)} %add_convert_fusion.5.own_ref, bf16[256,128]{1,0:T(8,128)(2,1)S(1)} %collective-permute-done.17.p1, bf16[256,128]{1,0:T(8,128)(2,1)S(1)} %collective-permute-done.18.p2, bf16[256,128]{1,0:T(8,128)(2,1)S(1)} %collective-permute-done.19.p3, ...), custom_call_target="tpu_custom_call" | custom-call | tf_op jit(solution)/shard_map/heads/pallas_call | solution.py:521
  (3 shorter events, 0.1 us)
Async XLA Ops:
  0.6 39.9 %copy-start = (bf16[256,256]{1,0:T(8,128)(2,1)S(1)}, bf16[256,256]{1,0:T(8,128)(2,1)}, u32[]{:S(2)}) copy-start(bf16[256,256]{1,0:T(8,128)(2,1)} %g0.1) | copy-start | bytes 393220
  0.6 31.2 %copy-start.1 = (s32[32,2]{0,1:T(2,128)S(1)}, s32[32,2]{0,1:T(2,128)}, u32[]{:S(2)}) copy-start(s32[32,2]{0,1:T(2,128)} %param.12) | copy-start | bytes 772
  2.8 37.7 %copy-start.2 = (f32[8,256]{1,0:T(8,128)S(1)}, f32[8,256]{1,0:T(8,128)}, u32[]{:S(2)}) copy-start(f32[8,256]{1,0:T(8,128)} %get-tuple-element.48.own_delta) | copy-start | bytes 24580
  2.8 27.0 %all-to-all-start = ((bf16[8,2,128,128]{3,2,1,0:T(8,128)(2,1)}), bf16[8,2,128,128]{3,2,1,0:T(8,128)(2,1)S(1)}, u32[]{:S(2)}, u32[]{:S(2)}) async-start(bf16[8,2,128,128]{3,2,1,0:T(8,128)(2,1)} %get-tuple-element.38), calls=%async_computation | async-start | bytes 1048576 | tf_op jit(solution)/shard_map/gather/all_to_all | solution.py:450
  11.8 8.1 %collective-permute-start.2 = (bf16[272,512]{1,0:T(8,128)(2,1)}, bf16[272,512]{1,0:T(8,128)(2,1)S(1)}, u32[]{:S(2)}, u32[]{:S(2)}) collective-permute-start(bf16[272,512]{1,0:T(8,128)(2,1)} %get-tuple-element.39), channel_id=1, source_target_pairs={{0,192},{64,0},{128,64},{192,128},{1,193},{65,1},{129,65},{193,129... | collective-permute-start | bytes 835592 | tf_op jit(solution)/shard_map/gather/ppermute | solution.py:445
  14.6 11.5 %collective-permute-start = (bf16[272,512]{1,0:T(8,128)(2,1)}, bf16[272,512]{1,0:T(8,128)(2,1)S(1)}, u32[]{:S(2)}, u32[]{:S(2)}) collective-permute-start(bf16[272,512]{1,0:T(8,128)(2,1)} %get-tuple-element.39), channel_id=1, source_target_pairs={{0,64},{64,128},{128,192},{192,0},{1,65},{65,129},{129,193},{193,1... | collective-permute-start | bytes 835592 | tf_op jit(solution)/shard_map/gather/ppermute | solution.py:446
  14.6 11.5 %collective-permute-start.1 = (bf16[272,512]{1,0:T(8,128)(2,1)}, bf16[272,512]{1,0:T(8,128)(2,1)S(1)}, u32[]{:S(2)}, u32[]{:S(2)}) collective-permute-start(bf16[272,512]{1,0:T(8,128)(2,1)} %get-tuple-element.39), channel_id=1, source_target_pairs={{0,128},{1,1},{64,192},{65,65},{128,0},{129,129},{192,64},{193,193... | collective-permute-start | bytes 835592 | tf_op jit(solution)/shard_map/gather/ppermute | solution.py:447
  19.9 9.2 %collective-permute-start.3 = (bf16[272,512]{1,0:T(8,128)(2,1)S(1)}, bf16[272,512]{1,0:T(8,128)(2,1)S(1)}, u32[]{:S(2)}, u32[]{:S(2)}) collective-permute-start(bf16[272,512]{1,0:T(8,128)(2,1)S(1)} %collective-permute-done.2.q3.g3), channel_id=1, source_target_pairs={{0,0},{1,193},{64,64},{65,1},{128,128},{129,65},{192,192},{193,129... | collective-permute-start | bytes 835592 | tf_op jit(solution)/shard_map/gather/ppermute | solution.py:448
  29.8 2.0 %collective-permute-start.4 = (bf16[8,2,128,128]{3,2,1,0:T(8,128)(2,1)S(1)}, bf16[8,2,128,128]{3,2,1,0:T(8,128)(2,1)S(1)}, u32[]{:S(2)}, u32[]{:S(2)}) collective-permute-start(bf16[8,2,128,128]{3,2,1,0:T(8,128)(2,1)S(1)} %all-to-all-done.mine_ref), channel_id=1, source_target_pairs={{0,1},{1,0},{2,3},{3,2},{4,5},{5,4},{6,7},{7,6},{8,9},{9,8},{10,11... | collective-permute-start | bytes 1572872 | tf_op jit(solution)/shard_map/gather/ppermute | solution.py:429
  35.5 8.8 %collective-permute-start.5 = (f32[24,256]{1,0:T(8,128)S(1)}, f32[24,256]{1,0:T(8,128)S(1)}, u32[]{:S(2)}, u32[]{:S(2)}) collective-permute-start(f32[24,256]{1,0:T(8,128)S(1)} %get-tuple-element.57.st0), channel_id=1, source_target_pairs={{0,64},{64,128},{128,192},{192,0},{1,65},{65,129},{129,193},{193,1... | collective-permute-start | bytes 73736 | tf_op jit(solution)/shard_map/probs/ppermute | solution.py:401
  36.8 7.5 %collective-permute-start.6 = (f32[24,256]{1,0:T(8,128)S(1)}, f32[24,256]{1,0:T(8,128)S(1)}, u32[]{:S(2)}, u32[]{:S(2)}) collective-permute-start(f32[24,256]{1,0:T(8,128)S(1)} %get-tuple-element.57.st0), channel_id=1, source_target_pairs={{0,128},{64,192},{128,0},{192,64},{1,129},{65,193},{129,1},{193,65... | collective-permute-start | bytes 73736 | tf_op jit(solution)/shard_map/probs/ppermute | solution.py:401
  39.5 4.9 %collective-permute-start.7 = (f32[24,256]{1,0:T(8,128)S(1)}, f32[24,256]{1,0:T(8,128)S(1)}, u32[]{:S(2)}, u32[]{:S(2)}) collective-permute-start(f32[24,256]{1,0:T(8,128)S(1)} %get-tuple-element.57.st0), channel_id=1, source_target_pairs={{0,192},{64,0},{128,64},{192,128},{1,193},{65,1},{129,65},{193,129... | collective-permute-start | bytes 73736 | tf_op jit(solution)/shard_map/probs/ppermute | solution.py:401
  47.9 3.5 %collective-permute-start.8 = (bf16[4,256,256]{2,1,0:T(8,128)(2,1)S(1)}, bf16[4,256,256]{2,1,0:T(8,128)(2,1)S(1)}, u32[]{:S(2)}, u32[]{:S(2)}) collective-permute-start(bf16[4,256,256]{2,1,0:T(8,128)(2,1)S(1)} %get-tuple-element.60), channel_id=1, source_target_pairs={{0,1},{1,0},{2,3},{3,2},{4,5},{5,4},{6,7},{7,6},{8,9},{9,8},{10,11... | collective-permute-start | bytes 1572872 | tf_op jit(solution)/shard_map/key_sum/ppermute | solution.py:429
  49.2 7.7 %collective-permute-start.13 = (bf16[256,256]{1,0:T(8,128)(2,1)S(1)}, bf16[256,256]{1,0:T(8,128)(2,1)S(1)}, u32[]{:S(2)}, u32[]{:S(2)}) collective-permute-start(bf16[256,256]{1,0:T(8,128)(2,1)S(1)} %get-tuple-element.61), channel_id=1, source_target_pairs={{0,192},{64,0},{128,64},{192,128},{1,193},{65,1},{129,65},{193,129... | collective-permute-start | bytes 393224 | tf_op jit(solution)/shard_map/key_sum/ppermute | solution.py:508
  50.1 11.0 %collective-permute-start.14 = (bf16[256,256]{1,0:T(8,128)(2,1)S(1)}, bf16[256,256]{1,0:T(8,128)(2,1)S(1)}, u32[]{:S(2)}, u32[]{:S(2)}) collective-permute-start(bf16[256,256]{1,0:T(8,128)(2,1)S(1)} %get-tuple-element.62), channel_id=1, source_target_pairs={{0,128},{64,192},{128,0},{192,64},{1,129},{65,193},{129,1},{193,65... | collective-permute-start | bytes 393224 | tf_op jit(solution)/shard_map/key_sum/ppermute | solution.py:508
  51.4 11.7 %collective-permute-start.15 = (bf16[256,256]{1,0:T(8,128)(2,1)S(1)}, bf16[256,256]{1,0:T(8,128)(2,1)S(1)}, u32[]{:S(2)}, u32[]{:S(2)}) collective-permute-start(bf16[256,256]{1,0:T(8,128)(2,1)S(1)} %get-tuple-element.63), channel_id=1, source_target_pairs={{0,64},{64,128},{128,192},{192,0},{1,65},{65,129},{129,193},{193,1... | collective-permute-start | bytes 393224 | tf_op jit(solution)/shard_map/key_sum/ppermute | solution.py:508
  51.5 11.6 %collective-permute-start.10 = (bf16[256,256]{1,0:T(8,128)(2,1)S(1)}, bf16[256,256]{1,0:T(8,128)(2,1)S(1)}, u32[]{:S(2)}, u32[]{:S(2)}) collective-permute-start(bf16[256,256]{1,0:T(8,128)(2,1)S(1)} %get-tuple-element.75), channel_id=1, source_target_pairs={{0,8},{1,25},{8,16},{9,33},{16,24},{17,41},{24,32},{25,49},{32,40}... | collective-permute-start | bytes 393224 | tf_op jit(solution)/shard_map/key_sum/ppermute | solution.py:506
  54.6 11.2 %collective-permute-start.11 = (bf16[256,256]{1,0:T(8,128)(2,1)S(1)}, bf16[256,256]{1,0:T(8,128)(2,1)S(1)}, u32[]{:S(2)}, u32[]{:S(2)}) collective-permute-start(bf16[256,256]{1,0:T(8,128)(2,1)S(1)} %get-tuple-element.74), channel_id=1, source_target_pairs={{0,16},{1,33},{8,24},{9,41},{16,32},{17,49},{24,40},{25,57},{32,48... | collective-permute-start | bytes 393224 | tf_op jit(solution)/shard_map/key_sum/ppermute | solution.py:506
  57.0 9.3 %collective-permute-start.12 = (bf16[256,256]{1,0:T(8,128)(2,1)S(1)}, bf16[256,256]{1,0:T(8,128)(2,1)S(1)}, u32[]{:S(2)}, u32[]{:S(2)}) collective-permute-start(bf16[256,256]{1,0:T(8,128)(2,1)S(1)} %get-tuple-element.73), channel_id=1, source_target_pairs={{0,48},{1,41},{8,56},{9,49},{16,0},{17,57},{24,8},{25,1},{32,16},{... | collective-permute-start | bytes 393224 | tf_op jit(solution)/shard_map/key_sum/ppermute | solution.py:506
  61.2 9.0 %collective-permute-start.9 = (bf16[256,256]{1,0:T(8,128)(2,1)S(1)}, bf16[256,256]{1,0:T(8,128)(2,1)S(1)}, u32[]{:S(2)}, u32[]{:S(2)}) collective-permute-start(bf16[256,256]{1,0:T(8,128)(2,1)S(1)} %get-tuple-element.76), channel_id=1, source_target_pairs={{0,0},{1,57},{8,8},{9,1},{16,16},{17,9},{24,24},{25,17},{32,32},{3... | collective-permute-start | bytes 393224 | tf_op jit(solution)/shard_map/key_sum/ppermute | solution.py:506
  70.2 1.4 %collective-permute-start.16 = (bf16[256,128]{1,0:T(8,128)(2,1)S(1)}, bf16[256,128]{1,0:T(8,128)(2,1)S(1)}, u32[]{:S(2)}, u32[]{:S(2)}) collective-permute-start(bf16[256,128]{1,0:T(8,128)(2,1)S(1)} %select_convert_fusion), channel_id=1, source_target_pairs={{0,1},{1,0},{2,3},{3,2},{4,5},{5,4},{6,7},{7,6},{8,9},{9,8},{10,11... | collective-permute-start | bytes 196616 | tf_op jit(solution)/shard_map/key_sum/ppermute | solution.py:429
  71.6 4.9 %collective-permute-start.17 = (bf16[256,128]{1,0:T(8,128)(2,1)S(1)}, bf16[256,128]{1,0:T(8,128)(2,1)S(1)}, u32[]{:S(2)}, u32[]{:S(2)}) collective-permute-start(bf16[256,128]{1,0:T(8,128)(2,1)S(1)} %add_convert_fusion.5.own_ref), channel_id=1, source_target_pairs={{0,2},{2,4},{4,6},{6,0},{1,3},{3,5},{5,7},{7,1},{8,10},{10,12},{12... | collective-permute-start | bytes 196616 | tf_op jit(solution)/shard_map/heads/ppermute | solution.py:401
  72.9 5.4 %collective-permute-start.18 = (bf16[256,128]{1,0:T(8,128)(2,1)S(1)}, bf16[256,128]{1,0:T(8,128)(2,1)S(1)}, u32[]{:S(2)}, u32[]{:S(2)}) collective-permute-start(bf16[256,128]{1,0:T(8,128)(2,1)S(1)} %add_convert_fusion.5.own_ref), channel_id=1, source_target_pairs={{0,4},{2,6},{4,0},{6,2},{1,5},{3,7},{5,1},{7,3},{8,12},{10,14},{12... | collective-permute-start | bytes 196616 | tf_op jit(solution)/shard_map/heads/ppermute | solution.py:401
  75.3 3.4 %collective-permute-start.19 = (bf16[256,128]{1,0:T(8,128)(2,1)S(1)}, bf16[256,128]{1,0:T(8,128)(2,1)S(1)}, u32[]{:S(2)}, u32[]{:S(2)}) collective-permute-start(bf16[256,128]{1,0:T(8,128)(2,1)S(1)} %add_convert_fusion.5.own_ref), channel_id=1, source_target_pairs={{0,6},{2,0},{4,2},{6,4},{1,7},{3,1},{5,3},{7,5},{8,14},{10,8},{12,... | collective-permute-start | bytes 196616 | tf_op jit(solution)/shard_map/heads/ppermute | solution.py:401
  78.8 3.0 %collective-permute-start.20 = (bf16[4,256,128]{2,1,0:T(8,128)(2,1)S(1)}, bf16[4,256,128]{2,1,0:T(8,128)(2,1)S(1)}, u32[]{:S(2)}, u32[]{:S(2)}) collective-permute-start(bf16[4,256,128]{2,1,0:T(8,128)(2,1)S(1)} %pad_maximum_fusion), channel_id=1, source_target_pairs={{0,1},{1,0},{2,3},{3,2},{4,5},{5,4},{6,7},{7,6},{8,9},{9,8},{10,11... | collective-permute-start | bytes 786440 | tf_op jit(solution)/shard_map/heads/ppermute | solution.py:429

commit v4 on v3

--- a/solution.py
+++ b/solution.py
@@ -20,7 +20,7 @@
 LOWEST = -1e30
 VMEM_BYTES = 32 * 1024 * 1024
 WHOLE_VMEM = 60 * 1024 * 1024
-STEPS = ((0, 7), (1, 3), (2, 4), (6, 5))
+STEPS = ((0, 1), (2, 6), (3, 5), (7, 4))
 F32 = jnp.float32
 BF16 = jnp.bfloat16
 
@@ -369,17 +369,24 @@
     copies[4].wait()
 
 
-def join_kernel(own_ref, p1, p2, p3, theirs_ref, key_ref, value_ref):
+def join_kernel(both_ref, near_ref, far_ref, theirs_ref, key_ref, value_ref):
     x_rank, core = lax.axis_index("x"), lax.axis_index("core")
-    for k, ref in enumerate((own_ref, p1, p2, p3)):
+
+    def place(out_ref, k, block):
         column = pl.multiple_of(lax.rem(x_rank + NX - k, NX) * DH, DH)
-        for owner in range(2):
-
-            @pl.when(core == owner)
-            def _(owner=owner, ref=ref, k=k, column=column):
-                outs = (key_ref, value_ref)
-                outs[owner][:, pl.ds(column, DH)] = ref[...]
-                outs[1 - owner][:, pl.ds(column, DH)] = theirs_ref[k]
+        out_ref[:, pl.ds(column, DH)] = block
+
+    for owner in range(2):
+
+        @pl.when(core == owner)
+        def _(owner=owner):
+            own_out, other_out = (key_ref, value_ref) if owner == 0 else (value_ref, key_ref)
+            near, opposite = (1, 3) if owner == 0 else (3, 1)
+            for k, ref in ((0, both_ref), (near, near_ref), (opposite, theirs_ref)):
+                place(key_ref, k, ref[:, :DH])
+                place(value_ref, k, ref[:, DH : 2 * DH])
+            place(own_out, 2, far_ref[...])
+            place(other_out, 2, theirs_ref[:, 2 * DH :])
 
 
 def call(kernel, n_scalars, n_arrays, out_shape, scratch=(), flops=0, far_in=0):
@@ -510,16 +517,23 @@
         ]
         parts, back = lax.optimization_barrier((parts, back))
         total = sum(parts[t].astype(F32) for t in range(len(STEPS)))
-        core = lax.axis_index("core")
-        kept = jnp.where(core == 0, total[:, :DH], total[:, DH:])
-        sent = jnp.where(core == 0, total[:, DH:], total[:, :DH]).astype(BF16)
-        own_sum = (kept + swap(sent).astype(F32)).astype(BF16)
+        rounded = lax.optimization_barrier(total.astype(BF16))
+        both = (rounded.astype(F32) + swap(rounded).astype(F32)).astype(BF16)
     with jax.named_scope("heads"):
-        heads = shifts(own_sum, "x", NX)
-        theirs_sum = swap(jnp.stack([own_sum, *heads]))
+        own_half = lax.dynamic_slice(both, (0, lax.axis_index("core") * DH), (ROWS, DH))
+        far = lax.ppermute(own_half, "x", [(i, (i + 2) % NX) for i in range(NX)])
+        near = lax.ppermute(
+            both, ("x", "core"),
+            [
+                (x * NCORE + c, (x + (1, -1)[c]) % NX * NCORE + c)
+                for x in range(NX)
+                for c in range(NCORE)
+            ],
+        )
+        theirs = swap(jnp.concatenate([near, far], axis=1))
         full = shape((ROWS, KVH * DH), BF16)
-        key_grad, value_grad = call(join_kernel, 0, 5, (full, full))(
-            own_sum, *heads, theirs_sum
+        key_grad, value_grad = call(join_kernel, 0, 4, (full, full))(
+            both, near, far, theirs
         )
     with jax.named_scope("query_sum"):
         query_grad = own_query

time: 83.3 us -> 82.5 us (level)
  starting transfers between devices: 46.4 us -> 39.9 us
  waiting for transfers between devices: 19 us -> 23.4 us
  Pallas kernels: 14 us -> 15.7 us
    ppermute x6 -> x3, starting transfers between devices: 9.99 us -> 4.54 us  [shifts(): lax.ppermute(array, axis, [(i, (i + k) % size) for i in range(size)])]
    ppermute x0 -> x2, waiting for transfers between devices: none -> 5.11 us  [the longest x1 5.11 us: shards(): far = lax.ppermute(own_half, 'x', [(i, (i + 2) % NX) for i in range(NX)])]
    ppermute x0 -> x2, starting transfers between devices: none -> 3.07 us  [the longest x1 2.54 us: shards(): lax.ppermute(both, ('x', 'core'), [(x * NCORE + c, (x + (1, -1)[c]) % NX...]
    ppermute x6 -> x3, waiting for transfers between devices: 2.24 us -> 0.01 us  [shifts(): lax.ppermute(array, axis, [(i, (i + k) % size) for i in range(size)])]
    ppermute x4, starting transfers between devices: 11.5 us -> 9.72 us  [shards(): parts[t] = lax.ppermute(pair, ('z', 'core'), key_pairs(STEPS[t]))]
    ppermute x4, starting transfers between devices: 4.1 us -> 2.57 us  [swap(): return lax.ppermute(array, 'core', [(0, 1), (1, 0)])]
    ppermute x4, waiting for transfers between devices: 7.02 us -> 8.17 us  [shards(): parts[t] = lax.ppermute(pair, ('z', 'core'), key_pairs(STEPS[t]))]
  transfers between devices with their start and end apart: 22 -> 21, of which waited for: 11 -> 11; matrix products, arithmetic and copies ran while one was open for 2% -> 2% of each run, Pallas kernels for 5% -> 5%
where the time goes in v4:
time: 82.5 us; the launch traced here: 82.4 us
  starting transfers between devices  39.9 us (48%)
  waiting for transfers between devices  23.4 us (28%)
  Pallas kernels  15.7 us (19%)
  between operations  1.46 us (2%)
  other arithmetic  0.95 us (1%)
  local copies, waits for them, and re-layouts  0.94 us (1%)
    ppermute x4, starting transfers between devices, shards(): parts[t] = lax.ppermute(pair, ('z', 'core'), key_pairs(STEPS[t]))  9.72 us
    all_to_all x1, starting transfers between devices, shards(): mine = lax.all_to_all(spread, 'z', 0, 0, tiled=True)  9.03 us
    ppermute x4, waiting for transfers between devices, shards(): parts[t] = lax.ppermute(pair, ('z', 'core'), key_pairs(STEPS[t]))  8.17 us
    ppermute x1, starting transfers between devices, shards(): relayed = lax.ppermute(down, ('y', 'core'), step_of_one_core(1, -1))  5.2 us
    ppermute x1, waiting for transfers between devices, shards(): far = lax.ppermute(own_half, 'x', [(i, (i + 2) % NX) for i in range(NX)])  5.11 us
    ppermute x3, starting transfers between devices, shifts(): lax.ppermute(array, axis, [(i, (i + k) % size) for i in range(size)])  4.54 us
    pallas_call x1, Pallas kernels, shards(): call(scores_kernel, 2, 12, (blocks, tall, tall, tiles, shape((8, DH, WIDE...  4.5 us
    pallas_call x1, Pallas kernels, shards(): call(probs_kernel, 2, 7, (blocks, sides, tall, tall, tiles, shape((24, WI...  4.13 us
  transfers between devices with their start and end apart: 21, of which 11 were waited for; matrix products, arithmetic and copies ran while one was open for 2% of the time, Pallas kernels for 5%

profile of v4, /device:TPU:1, one launch (start us, length us, event | category | flops | bytes accessed | tf_op | source)
XLA Modules:
  0.0 82.4 jit_solution(5135945442140028752)
XLA Ops:
  0.6 0.0 copy-start
  0.6 0.0 copy-start.1
  0.7 2.2 %gather.1 = (bf16[272,512]{1,0:T(8,128)(2,1)}, bf16[8,2,128,128]{3,2,1,0:T(8,128)(2,1)}, f32[8,256]{1,0:T(8,128)}) custom-call(bf16[256,256]{1,0:T(8,128)(2,1)} %queries_ref.1, bf16[256,256]{1,0:T(8,128)(2,1)} %saved_ref.1, bf16[256,256]{1,0:T(8,128)(2,1)} %g0.1, bf16[256,512]{1,0:T(8,128)(2,1)} %key_ref.1, bf16[256,512]{1,0:T(8,128)(2,1)} %value_ref.1), custom_call_target="tpu_custom_call" | custom-call | tf_op jit(solution)/shard_map/gather/pallas_call | solution.py:443
  2.8 0.0 copy-start.2
  2.8 9.0 %all-to-all-start = ((bf16[8,2,128,128]{3,2,1,0:T(8,128)(2,1)}), bf16[8,2,128,128]{3,2,1,0:T(8,128)(2,1)S(1)}, u32[]{:S(2)}, u32[]{:S(2)}) async-start(bf16[8,2,128,128]{3,2,1,0:T(8,128)(2,1)} %get-tuple-element.38), calls=%async_computation | async-start | bytes 1048576 | tf_op jit(solution)/shard_map/gather/all_to_all | solution.py:457
  11.9 2.7 %collective-permute-start.2 = (bf16[272,512]{1,0:T(8,128)(2,1)}, bf16[272,512]{1,0:T(8,128)(2,1)S(1)}, u32[]{:S(2)}, u32[]{:S(2)}) collective-permute-start(bf16[272,512]{1,0:T(8,128)(2,1)} %get-tuple-element.39), channel_id=1, source_target_pairs={{0,192},{64,0},{128,64},{192,128},{1,193},{65,1},{129,65},{193,129... | collective-permute-start | bytes 835592 | tf_op jit(solution)/shard_map/gather/ppermute | solution.py:452
  14.6 0.0 collective-permute-start
  14.6 1.6 %collective-permute-start.1 = (bf16[272,512]{1,0:T(8,128)(2,1)}, bf16[272,512]{1,0:T(8,128)(2,1)S(1)}, u32[]{:S(2)}, u32[]{:S(2)}) collective-permute-start(bf16[272,512]{1,0:T(8,128)(2,1)} %get-tuple-element.39), channel_id=1, source_target_pairs={{0,128},{1,1},{64,192},{65,65},{128,0},{129,129},{192,64},{193,193... | collective-permute-start | bytes 835592 | tf_op jit(solution)/shard_map/gather/ppermute | solution.py:454
  16.2 3.7 %collective-permute-done.2.q3.g3 = bf16[272,512]{1,0:T(8,128)(2,1)S(1)} collective-permute-done((bf16[272,512]{1,0:T(8,128)(2,1)}, bf16[272,512]{1,0:T(8,128)(2,1)S(1)}, u32[]{:S(2)}, u32[]{:S(2)}) %collective-permute-start.2) | collective-permute-done | bytes 278560 | tf_op jit(solution)/shard_map/gather/ppermute | solution.py:452
  19.9 5.2 %collective-permute-start.3 = (bf16[272,512]{1,0:T(8,128)(2,1)S(1)}, bf16[272,512]{1,0:T(8,128)(2,1)S(1)}, u32[]{:S(2)}, u32[]{:S(2)}) collective-permute-start(bf16[272,512]{1,0:T(8,128)(2,1)S(1)} %collective-permute-done.2.q3.g3), channel_id=1, source_target_pairs={{0,0},{1,193},{64,64},{65,1},{128,128},{129,65},{192,192},{193,129... | collective-permute-start | bytes 835592 | tf_op jit(solution)/shard_map/gather/ppermute | solution.py:455
  25.1 0.9 %slice.27.q0 = bf16[256,256]{1,0:T(8,128)(2,1)S(1)} slice(bf16[272,512]{1,0:T(8,128)(2,1)} %get-tuple-element.39), slice={[0:256], [0:256]} | slice | bytes 262144 | tf_op jit(solution)/shard_map/gather/slice | solution.py:458
  26.0 0.0 collective-permute-done.q1.g1
  26.1 0.0 collective-permute-done.1.q2.g2
  26.1 3.1 %collective-permute-done.3.q4.g4 = bf16[272,512]{1,0:T(8,128)(2,1)S(1)} collective-permute-done((bf16[272,512]{1,0:T(8,128)(2,1)S(1)}, bf16[272,512]{1,0:T(8,128)(2,1)S(1)}, u32[]{:S(2)}, u32[]{:S(2)}) %collective-permute-start.3) | collective-permute-done | bytes 278560 | tf_op jit(solution)/shard_map/gather/ppermute | solution.py:455
  29.1 0.7 all-to-all-done.mine_ref
  29.8 0.5 collective-permute-start.4
  31.0 0.9 %collective-permute-done.4.theirs_ref = bf16[8,2,128,128]{3,2,1,0:T(8,128)(2,1)S(1)} collective-permute-done((bf16[8,2,128,128]{3,2,1,0:T(8,128)(2,1)S(1)}, bf16[8,2,128,128]{3,2,1,0:T(8,128)(2,1)S(1)}, u32[]{:S(2)}, u32[]{:S(2)}) %collective-permute-start.4) | collective-permute-done | bytes 524320 | tf_op jit(solution)/shard_map/gather/ppermute | solution.py:436
  31.8 0.0 copy-done.1
  31.8 4.1 %probs.1 = (bf16[8,256,128]{2,1,0:T(8,128)(2,1)S(1)}, bf16[2,8,128,128]{3,2,1,0:T(8,128)(2,1)S(1)}, bf16[4,1024,256]{2,1,0:T(8,128)(2,1)S(1)}, bf16[4,1024,256]{...) custom-call(s32[2,32]{1,0:T(2,128)S(1)} %bitcast.9, s32[1]{0:T(128)S(6)} %copy.10.prompt_ref, ...), custom_call_target="tpu_custom_call" | custom-call | tf_op jit(solution)/shard_map/probs/pallas_call | solution.py:462
  36.0 0.9 %collective-permute-start.5 = (f32[24,256]{1,0:T(8,128)S(1)}, f32[24,256]{1,0:T(8,128)S(1)}, u32[]{:S(2)}, u32[]{:S(2)}) collective-permute-start(f32[24,256]{1,0:T(8,128)S(1)} %get-tuple-element.57.st0), channel_id=1, source_target_pairs={{0,64},{64,128},{128,192},{192,0},{1,65},{65,129},{129,193},{193,1... | collective-permute-start | bytes 73736 | tf_op jit(solution)/shard_map/probs/ppermute | solution.py:408
  36.8 2.6 %collective-permute-start.6 = (f32[24,256]{1,0:T(8,128)S(1)}, f32[24,256]{1,0:T(8,128)S(1)}, u32[]{:S(2)}, u32[]{:S(2)}) collective-permute-start(f32[24,256]{1,0:T(8,128)S(1)} %get-tuple-element.57.st0), channel_id=1, source_target_pairs={{0,128},{64,192},{128,0},{192,64},{1,129},{65,193},{129,1},{193,65... | collective-permute-start | bytes 73736 | tf_op jit(solution)/shard_map/probs/ppermute | solution.py:408
  39.5 1.1 %collective-permute-start.7 = (f32[24,256]{1,0:T(8,128)S(1)}, f32[24,256]{1,0:T(8,128)S(1)}, u32[]{:S(2)}, u32[]{:S(2)}) collective-permute-start(f32[24,256]{1,0:T(8,128)S(1)} %get-tuple-element.57.st0), channel_id=1, source_target_pairs={{0,192},{64,0},{128,64},{192,128},{1,193},{65,1},{129,65},{193,129... | collective-permute-start | bytes 73736 | tf_op jit(solution)/shard_map/probs/ppermute | solution.py:408
  40.5 0.0 copy-done
  40.5 0.0 copy-done.2
  40.5 4.5 %scores.1 = (bf16[8,256,128]{2,1,0:T(8,128)(2,1)S(1)}, bf16[4,1024,256]{2,1,0:T(8,128)(2,1)S(1)}, bf16[4,1024,256]{2,1,0:T(8,128)(2,1)S(1)}, bf16[4,8,128,256]{3,2,1,0:T(8,128)(2,1)S(1)}, f32[8,128,256]{2,1,0:T(8,128)S(1)}) custom-call(s32[2,32]{1,0:T(2,128)S(1)} %bitcast.10, s32[1]{0:T(128)S(6)} %copy.10.prompt_ref, ...), custom_call_target="tpu_custom_call" | custom-call | flops 4000000000 | tf_op jit(solution)/shard_map/scores/pallas_call | solution.py:474
  45.0 0.0 collective-permute-done.5.st1
  45.1 0.0 collective-permute-done.6.st2
  45.1 0.0 collective-permute-done.7.st3
  45.1 4.0 %grads.1 = (f32[256,256]{1,0:T(8,128)S(1)}, bf16[256,256]{1,0:T(8,128)(2,1)S(1)}, bf16[256,256]{1,0:T(8,128)(2,1)S(1)}, bf16[256,256]{1,0:T(8,128)(2,1)S(1)}, f3...) custom-call(s32[2,32]{1,0:T(2,128)S(1)} %bitcast.11, s32[1]{0:T(128)S(6)} %copy.10.prompt_ref, ...), custom_call_target="tpu_custom_call" | custom-call | tf_op jit(solution)/shard_map/grads/pallas_call | solution.py:490
  49.1 1.3 %collective-permute-start.8 = (bf16[4,256,256]{2,1,0:T(8,128)(2,1)S(1)}, bf16[4,256,256]{2,1,0:T(8,128)(2,1)S(1)}, u32[]{:S(2)}, u32[]{:S(2)}) collective-permute-start(bf16[4,256,256]{2,1,0:T(8,128)(2,1)S(1)} %get-tuple-element.60), channel_id=1, source_target_pairs={{0,1},{1,0},{2,3},{3,2},{4,5},{5,4},{6,7},{7,6},{8,9},{9,8},{10,11... | collective-permute-start | bytes 1572872 | tf_op jit(solution)/shard_map/key_sum/ppermute | solution.py:436
  50.4 0.0 collective-permute-start.13
  50.4 1.0 %collective-permute-start.14 = (bf16[256,256]{1,0:T(8,128)(2,1)S(1)}, bf16[256,256]{1,0:T(8,128)(2,1)S(1)}, u32[]{:S(2)}, u32[]{:S(2)}) collective-permute-start(bf16[256,256]{1,0:T(8,128)(2,1)S(1)} %get-tuple-element.62), channel_id=1, source_target_pairs={{0,128},{64,192},{128,0},{192,64},{1,129},{65,193},{129,1},{193,65... | collective-permute-start | bytes 393224 | tf_op jit(solution)/shard_map/key_sum/ppermute | solution.py:515
  51.4 0.4 collective-permute-start.15
  51.8 0.1 collective-permute-done.8
  51.9 0.1 fusion.3
  52.0 2.8 %collective-permute-start.10 = (bf16[256,256]{1,0:T(8,128)(2,1)S(1)}, bf16[256,256]{1,0:T(8,128)(2,1)S(1)}, u32[]{:S(2)}, u32[]{:S(2)}) collective-permute-start(bf16[256,256]{1,0:T(8,128)(2,1)S(1)} %get-tuple-element.75), channel_id=1, source_target_pairs={{0,16},{1,49},{8,24},{9,57},{16,32},{17,1},{24,40},{25,9},{32,48},... | collective-permute-start | bytes 393224 | tf_op jit(solution)/shard_map/key_sum/ppermute | solution.py:513
  54.9 2.1 %collective-permute-start.11 = (bf16[256,256]{1,0:T(8,128)(2,1)S(1)}, bf16[256,256]{1,0:T(8,128)(2,1)S(1)}, u32[]{:S(2)}, u32[]{:S(2)}) collective-permute-start(bf16[256,256]{1,0:T(8,128)(2,1)S(1)} %get-tuple-element.74), channel_id=1, source_target_pairs={{0,24},{1,41},{8,32},{9,49},{16,40},{17,57},{24,48},{25,1},{32,56}... | collective-permute-start | bytes 393224 | tf_op jit(solution)/shard_map/key_sum/ppermute | solution.py:513
  57.0 0.0 collective-permute-done.13
  57.0 2.9 %collective-permute-start.12 = (bf16[256,256]{1,0:T(8,128)(2,1)S(1)}, bf16[256,256]{1,0:T(8,128)(2,1)S(1)}, u32[]{:S(2)}, u32[]{:S(2)}) collective-permute-start(bf16[256,256]{1,0:T(8,128)(2,1)S(1)} %get-tuple-element.73), channel_id=1, source_target_pairs={{0,56},{1,33},{8,0},{9,41},{16,8},{17,49},{24,16},{25,57},{32,24},... | collective-permute-start | bytes 393224 | tf_op jit(solution)/shard_map/key_sum/ppermute | solution.py:513
  59.9 0.0 collective-permute-done.14
  59.9 1.9 %collective-permute-start.9 = (bf16[256,256]{1,0:T(8,128)(2,1)S(1)}, bf16[256,256]{1,0:T(8,128)(2,1)S(1)}, u32[]{:S(2)}, u32[]{:S(2)}) collective-permute-start(bf16[256,256]{1,0:T(8,128)(2,1)S(1)} %get-tuple-element.76), channel_id=1, source_target_pairs={{0,0},{1,9},{8,8},{9,17},{16,16},{17,25},{24,24},{25,33},{32,32},{... | collective-permute-start | bytes 393224 | tf_op jit(solution)/shard_map/key_sum/ppermute | solution.py:513
  61.8 0.0 collective-permute-done.15
  61.8 0.0 collective-permute-done.10
  61.8 5.1 %collective-permute-done.11 = bf16[256,256]{1,0:T(8,128)(2,1)S(1)} collective-permute-done((bf16[256,256]{1,0:T(8,128)(2,1)S(1)}, bf16[256,256]{1,0:T(8,128)(2,1)S(1)}, u32[]{:S(2)}, u32[]{:S(2)}) %collective-permute-start.11) | collective-permute-done | bytes 131104 | tf_op jit(solution)/shard_map/key_sum/ppermute | solution.py:513
  66.9 1.0 %collective-permute-done.12 = bf16[256,256]{1,0:T(8,128)(2,1)S(1)} collective-permute-done((bf16[256,256]{1,0:T(8,128)(2,1)S(1)}, bf16[256,256]{1,0:T(8,128)(2,1)S(1)}, u32[]{:S(2)}, u32[]{:S(2)}) %collective-permute-start.12) | collective-permute-done | bytes 131104 | tf_op jit(solution)/shard_map/key_sum/ppermute | solution.py:513
  67.9 2.1 %collective-permute-done.9 = bf16[256,256]{1,0:T(8,128)(2,1)S(1)} collective-permute-done((bf16[256,256]{1,0:T(8,128)(2,1)S(1)}, bf16[256,256]{1,0:T(8,128)(2,1)S(1)}, u32[]{:S(2)}, u32[]{:S(2)}) %collective-permute-start.9) | collective-permute-done | bytes 131104 | tf_op jit(solution)/shard_map/key_sum/ppermute | solution.py:513
  70.0 0.1 add_convert_fusion.1
  70.0 0.1 collective-permute-start.16
  70.1 1.3 %collective-permute-done.16 = bf16[256,256]{1,0:T(8,128)(2,1)S(1)} collective-permute-done((bf16[256,256]{1,0:T(8,128)(2,1)S(1)}, bf16[256,256]{1,0:T(8,128)(2,1)S(1)}, u32[]{:S(2)}, u32[]{:S(2)}) %collective-permute-start.16) | collective-permute-done | bytes 131104 | tf_op jit(solution)/shard_map/key_sum/ppermute | solution.py:436
  71.5 2.5 %collective-permute-start.17 = (bf16[256,256]{1,0:T(8,128)(2,1)S(1)}, bf16[256,256]{1,0:T(8,128)(2,1)S(1)}, u32[]{:S(2)}, u32[]{:S(2)}) collective-permute-start(bf16[256,256]{1,0:T(8,128)(2,1)S(1)} %add_convert_fusion.both_ref), channel_id=1, source_target_pairs={{0,2},{1,7},{2,4},{3,1},{4,6},{5,3},{6,0},{7,5},{8,10},{9,15},{10,... | collective-permute-start | bytes 393224 | tf_op jit(solution)/shard_map/heads/ppermute | solution.py:525
  74.1 0.5 collective-permute-start.18
  74.6 5.1 %collective-permute-done.18.far_ref = bf16[256,128]{1,0:T(8,128)(2,1)S(1)} collective-permute-done((bf16[256,128]{1,0:T(8,128)(2,1)S(1)}, bf16[256,128]{1,0:T(8,128)(2,1)S(1)}, u32[]{:S(2)}, u32[]{:S(2)}) %collective-permute-start.18) | collective-permute-done | bytes 65568 | tf_op jit(solution)/shard_map/heads/ppermute | solution.py:524
  79.7 0.0 collective-permute-done.17.near_ref
  79.7 0.7 collective-permute-start.19
  80.4 0.7 add_convert_fusion.2
  81.1 0.4 collective-permute-done.19.theirs_ref
  81.5 0.9 %heads.1 = (bf16[256,512]{1,0:T(8,128)(2,1)}, bf16[256,512]{1,0:T(8,128)(2,1)}) custom-call(bf16[256,256]{1,0:T(8,128)(2,1)S(1)} %add_convert_fusion.both_ref, bf16[256,256]{1,0:T(8,128)(2,1)S(1)} %collective-permute-done.17.near_ref, bf16[256,128]{1,0:T(8,128)(2,1)S(1)} %collective-permute-done.18.far_ref, ...), custom_call_target="tpu_custom_call" | custom-call | tf_op jit(solution)/shard_map/heads/pallas_call | solution.py:535
  (3 shorter events, 0.1 us)
Async XLA Ops:
  0.6 39.9 %copy-start = (bf16[256,256]{1,0:T(8,128)(2,1)S(1)}, bf16[256,256]{1,0:T(8,128)(2,1)}, u32[]{:S(2)}) copy-start(bf16[256,256]{1,0:T(8,128)(2,1)} %g0.1) | copy-start | bytes 393220
  0.6 31.2 %copy-start.1 = (s32[32,2]{0,1:T(2,128)S(1)}, s32[32,2]{0,1:T(2,128)}, u32[]{:S(2)}) copy-start(s32[32,2]{0,1:T(2,128)} %param.12) | copy-start | bytes 772
  2.8 37.7 %copy-start.2 = (f32[8,256]{1,0:T(8,128)S(1)}, f32[8,256]{1,0:T(8,128)}, u32[]{:S(2)}) copy-start(f32[8,256]{1,0:T(8,128)} %get-tuple-element.48.own_delta) | copy-start | bytes 24580
  2.8 27.0 %all-to-all-start = ((bf16[8,2,128,128]{3,2,1,0:T(8,128)(2,1)}), bf16[8,2,128,128]{3,2,1,0:T(8,128)(2,1)S(1)}, u32[]{:S(2)}, u32[]{:S(2)}) async-start(bf16[8,2,128,128]{3,2,1,0:T(8,128)(2,1)} %get-tuple-element.38), calls=%async_computation | async-start | bytes 1048576 | tf_op jit(solution)/shard_map/gather/all_to_all | solution.py:457
  11.9 8.1 %collective-permute-start.2 = (bf16[272,512]{1,0:T(8,128)(2,1)}, bf16[272,512]{1,0:T(8,128)(2,1)S(1)}, u32[]{:S(2)}, u32[]{:S(2)}) collective-permute-start(bf16[272,512]{1,0:T(8,128)(2,1)} %get-tuple-element.39), channel_id=1, source_target_pairs={{0,192},{64,0},{128,64},{192,128},{1,193},{65,1},{129,65},{193,129... | collective-permute-start | bytes 835592 | tf_op jit(solution)/shard_map/gather/ppermute | solution.py:452
  14.6 11.5 %collective-permute-start = (bf16[272,512]{1,0:T(8,128)(2,1)}, bf16[272,512]{1,0:T(8,128)(2,1)S(1)}, u32[]{:S(2)}, u32[]{:S(2)}) collective-permute-start(bf16[272,512]{1,0:T(8,128)(2,1)} %get-tuple-element.39), channel_id=1, source_target_pairs={{0,64},{64,128},{128,192},{192,0},{1,65},{65,129},{129,193},{193,1... | collective-permute-start | bytes 835592 | tf_op jit(solution)/shard_map/gather/ppermute | solution.py:453
  14.6 11.5 %collective-permute-start.1 = (bf16[272,512]{1,0:T(8,128)(2,1)}, bf16[272,512]{1,0:T(8,128)(2,1)S(1)}, u32[]{:S(2)}, u32[]{:S(2)}) collective-permute-start(bf16[272,512]{1,0:T(8,128)(2,1)} %get-tuple-element.39), channel_id=1, source_target_pairs={{0,128},{1,1},{64,192},{65,65},{128,0},{129,129},{192,64},{193,193... | collective-permute-start | bytes 835592 | tf_op jit(solution)/shard_map/gather/ppermute | solution.py:454
  19.9 9.2 %collective-permute-start.3 = (bf16[272,512]{1,0:T(8,128)(2,1)S(1)}, bf16[272,512]{1,0:T(8,128)(2,1)S(1)}, u32[]{:S(2)}, u32[]{:S(2)}) collective-permute-start(bf16[272,512]{1,0:T(8,128)(2,1)S(1)} %collective-permute-done.2.q3.g3), channel_id=1, source_target_pairs={{0,0},{1,193},{64,64},{65,1},{128,128},{129,65},{192,192},{193,129... | collective-permute-start | bytes 835592 | tf_op jit(solution)/shard_map/gather/ppermute | solution.py:455
  29.8 2.0 %collective-permute-start.4 = (bf16[8,2,128,128]{3,2,1,0:T(8,128)(2,1)S(1)}, bf16[8,2,128,128]{3,2,1,0:T(8,128)(2,1)S(1)}, u32[]{:S(2)}, u32[]{:S(2)}) collective-permute-start(bf16[8,2,128,128]{3,2,1,0:T(8,128)(2,1)S(1)} %all-to-all-done.mine_ref), channel_id=1, source_target_pairs={{0,1},{1,0},{2,3},{3,2},{4,5},{5,4},{6,7},{7,6},{8,9},{9,8},{10,11... | collective-permute-start | bytes 1572872 | tf_op jit(solution)/shard_map/gather/ppermute | solution.py:436
  36.0 9.1 %collective-permute-start.5 = (f32[24,256]{1,0:T(8,128)S(1)}, f32[24,256]{1,0:T(8,128)S(1)}, u32[]{:S(2)}, u32[]{:S(2)}) collective-permute-start(f32[24,256]{1,0:T(8,128)S(1)} %get-tuple-element.57.st0), channel_id=1, source_target_pairs={{0,64},{64,128},{128,192},{192,0},{1,65},{65,129},{129,193},{193,1... | collective-permute-start | bytes 73736 | tf_op jit(solution)/shard_map/probs/ppermute | solution.py:408
  36.8 8.2 %collective-permute-start.6 = (f32[24,256]{1,0:T(8,128)S(1)}, f32[24,256]{1,0:T(8,128)S(1)}, u32[]{:S(2)}, u32[]{:S(2)}) collective-permute-start(f32[24,256]{1,0:T(8,128)S(1)} %get-tuple-element.57.st0), channel_id=1, source_target_pairs={{0,128},{64,192},{128,0},{192,64},{1,129},{65,193},{129,1},{193,65... | collective-permute-start | bytes 73736 | tf_op jit(solution)/shard_map/probs/ppermute | solution.py:408
  39.5 5.6 %collective-permute-start.7 = (f32[24,256]{1,0:T(8,128)S(1)}, f32[24,256]{1,0:T(8,128)S(1)}, u32[]{:S(2)}, u32[]{:S(2)}) collective-permute-start(f32[24,256]{1,0:T(8,128)S(1)} %get-tuple-element.57.st0), channel_id=1, source_target_pairs={{0,192},{64,0},{128,64},{192,128},{1,193},{65,1},{129,65},{193,129... | collective-permute-start | bytes 73736 | tf_op jit(solution)/shard_map/probs/ppermute | solution.py:408
  49.1 2.8 %collective-permute-start.8 = (bf16[4,256,256]{2,1,0:T(8,128)(2,1)S(1)}, bf16[4,256,256]{2,1,0:T(8,128)(2,1)S(1)}, u32[]{:S(2)}, u32[]{:S(2)}) collective-permute-start(bf16[4,256,256]{2,1,0:T(8,128)(2,1)S(1)} %get-tuple-element.60), channel_id=1, source_target_pairs={{0,1},{1,0},{2,3},{3,2},{4,5},{5,4},{6,7},{7,6},{8,9},{9,8},{10,11... | collective-permute-start | bytes 1572872 | tf_op jit(solution)/shard_map/key_sum/ppermute | solution.py:436
  50.4 6.6 %collective-permute-start.13 = (bf16[256,256]{1,0:T(8,128)(2,1)S(1)}, bf16[256,256]{1,0:T(8,128)(2,1)S(1)}, u32[]{:S(2)}, u32[]{:S(2)}) collective-permute-start(bf16[256,256]{1,0:T(8,128)(2,1)S(1)} %get-tuple-element.61), channel_id=1, source_target_pairs={{0,192},{64,0},{128,64},{192,128},{1,193},{65,1},{129,65},{193,129... | collective-permute-start | bytes 393224 | tf_op jit(solution)/shard_map/key_sum/ppermute | solution.py:515
  50.4 9.5 %collective-permute-start.14 = (bf16[256,256]{1,0:T(8,128)(2,1)S(1)}, bf16[256,256]{1,0:T(8,128)(2,1)S(1)}, u32[]{:S(2)}, u32[]{:S(2)}) collective-permute-start(bf16[256,256]{1,0:T(8,128)(2,1)S(1)} %get-tuple-element.62), channel_id=1, source_target_pairs={{0,128},{64,192},{128,0},{192,64},{1,129},{65,193},{129,1},{193,65... | collective-permute-start | bytes 393224 | tf_op jit(solution)/shard_map/key_sum/ppermute | solution.py:515
  51.4 10.4 %collective-permute-start.15 = (bf16[256,256]{1,0:T(8,128)(2,1)S(1)}, bf16[256,256]{1,0:T(8,128)(2,1)S(1)}, u32[]{:S(2)}, u32[]{:S(2)}) collective-permute-start(bf16[256,256]{1,0:T(8,128)(2,1)S(1)} %get-tuple-element.63), channel_id=1, source_target_pairs={{0,64},{64,128},{128,192},{192,0},{1,65},{65,129},{129,193},{193,1... | collective-permute-start | bytes 393224 | tf_op jit(solution)/shard_map/key_sum/ppermute | solution.py:515
  52.0 9.7 %collective-permute-start.10 = (bf16[256,256]{1,0:T(8,128)(2,1)S(1)}, bf16[256,256]{1,0:T(8,128)(2,1)S(1)}, u32[]{:S(2)}, u32[]{:S(2)}) collective-permute-start(bf16[256,256]{1,0:T(8,128)(2,1)S(1)} %get-tuple-element.75), channel_id=1, source_target_pairs={{0,16},{1,49},{8,24},{9,57},{16,32},{17,1},{24,40},{25,9},{32,48},... | collective-permute-start | bytes 393224 | tf_op jit(solution)/shard_map/key_sum/ppermute | solution.py:513
  54.9 12.0 %collective-permute-start.11 = (bf16[256,256]{1,0:T(8,128)(2,1)S(1)}, bf16[256,256]{1,0:T(8,128)(2,1)S(1)}, u32[]{:S(2)}, u32[]{:S(2)}) collective-permute-start(bf16[256,256]{1,0:T(8,128)(2,1)S(1)} %get-tuple-element.74), channel_id=1, source_target_pairs={{0,24},{1,41},{8,32},{9,49},{16,40},{17,57},{24,48},{25,1},{32,56}... | collective-permute-start | bytes 393224 | tf_op jit(solution)/shard_map/key_sum/ppermute | solution.py:513
  57.0 10.9 %collective-permute-start.12 = (bf16[256,256]{1,0:T(8,128)(2,1)S(1)}, bf16[256,256]{1,0:T(8,128)(2,1)S(1)}, u32[]{:S(2)}, u32[]{:S(2)}) collective-permute-start(bf16[256,256]{1,0:T(8,128)(2,1)S(1)} %get-tuple-element.73), channel_id=1, source_target_pairs={{0,56},{1,33},{8,0},{9,41},{16,8},{17,49},{24,16},{25,57},{32,24},... | collective-permute-start | bytes 393224 | tf_op jit(solution)/shard_map/key_sum/ppermute | solution.py:513
  59.9 10.1 %collective-permute-start.9 = (bf16[256,256]{1,0:T(8,128)(2,1)S(1)}, bf16[256,256]{1,0:T(8,128)(2,1)S(1)}, u32[]{:S(2)}, u32[]{:S(2)}) collective-permute-start(bf16[256,256]{1,0:T(8,128)(2,1)S(1)} %get-tuple-element.76), channel_id=1, source_target_pairs={{0,0},{1,9},{8,8},{9,17},{16,16},{17,25},{24,24},{25,33},{32,32},{... | collective-permute-start | bytes 393224 | tf_op jit(solution)/shard_map/key_sum/ppermute | solution.py:513
  70.0 1.4 %collective-permute-start.16 = (bf16[256,256]{1,0:T(8,128)(2,1)S(1)}, bf16[256,256]{1,0:T(8,128)(2,1)S(1)}, u32[]{:S(2)}, u32[]{:S(2)}) collective-permute-start(bf16[256,256]{1,0:T(8,128)(2,1)S(1)} %add_convert_fusion.1), channel_id=1, source_target_pairs={{0,1},{1,0},{2,3},{3,2},{4,5},{5,4},{6,7},{7,6},{8,9},{9,8},{10,11... | collective-permute-start | bytes 393224 | tf_op jit(solution)/shard_map/key_sum/ppermute | solution.py:436
  71.5 8.2 %collective-permute-start.17 = (bf16[256,256]{1,0:T(8,128)(2,1)S(1)}, bf16[256,256]{1,0:T(8,128)(2,1)S(1)}, u32[]{:S(2)}, u32[]{:S(2)}) collective-permute-start(bf16[256,256]{1,0:T(8,128)(2,1)S(1)} %add_convert_fusion.both_ref), channel_id=1, source_target_pairs={{0,2},{1,7},{2,4},{3,1},{4,6},{5,3},{6,0},{7,5},{8,10},{9,15},{10,... | collective-permute-start | bytes 393224 | tf_op jit(solution)/shard_map/heads/ppermute | solution.py:525
  74.1 5.6 %collective-permute-start.18 = (bf16[256,128]{1,0:T(8,128)(2,1)S(1)}, bf16[256,128]{1,0:T(8,128)(2,1)S(1)}, u32[]{:S(2)}, u32[]{:S(2)}) collective-permute-start(bf16[256,128]{1,0:T(8,128)(2,1)S(1)} %constant_dynamic-slice_fusion), channel_id=1, source_target_pairs={{0,4},{2,6},{4,0},{6,2},{1,5},{3,7},{5,1},{7,3},{8,12},{10,14},{12... | collective-permute-start | bytes 196616 | tf_op jit(solution)/shard_map/heads/ppermute | solution.py:524
  79.7 1.8 %collective-permute-start.19 = (bf16[256,384]{1,0:T(8,128)(2,1)S(1)}, bf16[256,384]{1,0:T(8,128)(2,1)S(1)}, u32[]{:S(2)}, u32[]{:S(2)}) collective-permute-start(bf16[256,384]{1,0:T(8,128)(2,1)S(1)} %pad_maximum_fusion), channel_id=1, source_target_pairs={{0,1},{1,0},{2,3},{3,2},{4,5},{5,4},{6,7},{7,6},{8,9},{9,8},{10,11... | collective-permute-start | bytes 589832 | tf_op jit(solution)/shard_map/heads/ppermute | solution.py:436
